TPU v7x, 32 devices: a whole 2x2x4 slice. The times are simulated.
32 devices in a mesh: grid: 8 (over z, y), rep: 4 (over x, core).
Axes of the slice: x: 2, y: 2, z: 4, core: 2. Of those that a mesh axis runs over, the one named last changes fastest.
Arguments:
- integrals: bfloat16 [16384, 512], P(('grid', 'rep')), may hold values from -6 to 6
- green_occ: bfloat16 [512, 2048], P(None, 'grid'), may hold values from -0.25 to 0.25
- tile_panels: int32 [128, 2], P(('grid', 'rep')), may hold values from 0 to 7, all different within a row; in each aligned block of 4 rows (0 to 3, 4 to 7, ...) at most 2 rows name the same one
- virtual_blocks: bfloat16 [8, 16, 256, 256], P('grid', 'rep'), may hold values from -0.06591797 to 0.06591797
Outputs:
- response_blocks: float32 [8, 128, 256], P('grid', 'rep')
Inputs may be any that keep to these rules, and one draw needn't show every extreme that they name: `tile_panels`: each row lists 2 different panels. In each aligned block of 4 rows (the tiles of one device) no panel is listed by more than 2 rows, and some panel is listed by exactly 2 rows.
All inputs are finite; a program needn't handle non-finite values.
Results may differ from a plain program's by a relative error of at most 0.0029.
Values may be sent and summed in bfloat16 or wider, within the bound.
No kernel may reach another device: no remote copies, remote signals or barrier semaphores. Data moves between devices by JAX's collectives and lax.ppermute only.
A program may use at most 128 MiB of HBM per device.

v0:
```python
import jax
import jax.numpy as jnp
from jax import lax
from jax.sharding import PartitionSpec as P

CAP = 2


def shards(integrals, green_occ, tile_panels, virtual_blocks):
    grid_count = lax.axis_size("grid")
    tile_count = tile_panels.shape[0]
    tile_rows = integrals.shape[0] // tile_count
    panel_width = green_occ.shape[1]
    owners = jnp.arange(grid_count, dtype=jnp.int32)
    hit_count = jnp.sum(
        (tile_panels[:, :, None] == owners[None, None, :]).astype(jnp.int32), axis=1
    )
    before = jnp.cumsum(hit_count, axis=0) - hit_count
    slot_ids = jnp.arange(CAP, dtype=jnp.int32)
    placement = (hit_count[:, :, None] == 1) & (before[:, :, None] == slot_ids[None, None, :])
    place_weights = placement.astype(jnp.bfloat16)
    tile_ids = jnp.arange(tile_count, dtype=jnp.int32)
    labels = jnp.sum(placement.astype(jnp.int32) * tile_ids[:, None, None], axis=0)
    contracted = jnp.dot(
        integrals,
        lax.all_gather(green_occ, "grid", axis=1, tiled=True),
        preferred_element_type=jnp.float32,
    ).astype(jnp.bfloat16)
    tile_blocks = contracted.reshape(tile_count, tile_rows, grid_count, panel_width)
    outgoing = jnp.einsum(
        "ldc,ltdw->dctw", place_weights, tile_blocks, preferred_element_type=jnp.float32
    ).astype(jnp.bfloat16)
    arrived, got_labels = (
        lax.all_to_all(outgoing, "grid", split_axis=0, concat_axis=0, tiled=True),
        lax.all_to_all(labels, "grid", split_axis=0, concat_axis=0, tiled=True),
    )
    slot_owner = (got_labels[:, :, None] == tile_ids[None, None, :]).astype(jnp.bfloat16)
    summed = jnp.einsum("gcl,gctw->ltw", slot_owner, arrived, preferred_element_type=jnp.float32)
    owner_part = jnp.einsum(
        "ltw,lwc->tc",
        summed,
        virtual_blocks[0].astype(jnp.float32),
        precision=lax.Precision.HIGHEST,
    )
    return lax.psum_scatter(owner_part[None], "rep", scatter_dimension=1, tiled=True)


def solution(mesh):
    in_specs = (
        P(("grid", "rep"), None),
        P(None, "grid"),
        P(("grid", "rep"), None),
        P("grid", "rep", None, None),
    )
    out_specs = P("grid", "rep", None)
    return jax.shard_map(shards, mesh=mesh, in_specs=in_specs, out_specs=out_specs, check_vma=False)
```

profile of v0, /device:TPU:0, one launch (start us, length us, event | category | flops | bytes accessed | tf_op | source)
XLA Modules:
  0.0 127.2 jit_solution(5414995478979201522)
XLA Ops:
  6.5 0.0 copy-start
  6.5 0.0 all-gather.2.cloned.1.call-start
  6.5 0.7 all-gather.2.cloned.1.call-update
  7.3 0.8 convert_reduce_fusion
  8.1 0.7 copy.11
  8.8 7.3 %all-to-all-start = ((s32[8,1,2]{2,1,0:T(1,128)}), s32[8,1,2]{2,1,0:T(1,128)S(1)}, u32[]{:S(2)}, u32[]{:S(2)}) async-start(s32[8,1,2]{2,1,0:T(1,128)} %copy.11), calls=%async_computation | async-start | bytes 8192 | tf_op jit(solution)/shard_map/all_to_all | solution.py:35
  16.1 0.1 copy.17
  16.2 47.0 %all-gather.2.cloned.1.call-done = bf16[512,2048]{1,0:T(8,128)(2,1)} async-done(((bf16[512,256]{1,0:T(8,128)(2,1)}), bf16[512,2048]{1,0:T(8,128)(2,1)}) %all-gather.2.cloned.1.call-update) | async-done | bytes 2097168 | tf_op jit(solution)/shard_map/all_gather | solution.py:26
  63.2 0.0 copy-done
  63.2 2.8 %convolution_convert_fusion = bf16[512,2048]{1,0:T(8,128)(2,1)S(1)} fusion(bf16[512,512]{1,0:T(8,128)(2,1)S(1)} %copy-done, bf16[512,2048]{1,0:T(8,128)(2,1)} %all-gather.2.cloned.1.call-done), kind=kOutput, calls=%fused_computation | convolution fusion | flops 1074790400 | bytes 4718592 | tf_op jit(solution)/shard_map/dot_general | solution.py:24
  66.1 0.7 copy.21
  66.8 3.8 %fusion.2 = bf16[8,2,128,256]{3,1,2,0:T(2,128)(2,1)} fusion(pred[4,8,2,1]{0,2,3,1:T(4,128)(4,1)S(1)} %copy.17, bf16[4,128,8,256]{3,2,1,0:T(8,128)(2,1)S(1)} %bitcast.22), kind=kOutput, calls=%fused_computation.3 | convolution fusion | flops 4718592 | bytes 3145792 | tf_op jit(solution)/shard_map/ldc,ltdw->dctw/dot_general | solution.py:30
  70.5 0.0 copy-start.1
  70.5 0.0 all-to-all-done
  70.5 3.7 %all-to-all-start.1 = ((bf16[8,2,128,256]{3,1,2,0:T(2,128)(2,1)}), bf16[8,2,128,256]{3,1,2,0:T(2,128)(2,1)S(1)}, u32[]{:S(2)}, u32[]{:S(2)}) async-start(bf16[8,2,128,256]{3,1,2,0:T(2,128)(2,1)} %fusion.2), calls=%async_computation.1 | async-start | bytes 2097152 | tf_op jit(solution)/shard_map/all_to_all | solution.py:34
  74.2 0.0 reduce-scatter.2.cloned.1.call-start
  74.3 0.1 copy.12
  74.3 25.4 %all-to-all-done.1 = bf16[8,2,128,256]{3,1,2,0:T(2,128)(2,1)S(1)} async-done(((bf16[8,2,128,256]{3,1,2,0:T(2,128)(2,1)}), bf16[8,2,128,256]{3,1,2,0:T(2,128)(2,1)S(1)}, u32[]{:S(2)}, u32[]{:S(2)}) %all-to-all-start.1) | async-done | bytes 1048608 | tf_op jit(solution)/shard_map/all_to_all | solution.py:34
  99.7 0.7 convolution_bitcast_fusion
  100.5 0.0 copy-done.1
  100.5 1.1 convolution_bitcast_fusion.1
  101.6 0.0 reduce-scatter.2.cloned.1.call-update
  101.6 18.8 %reduce-scatter.2.cloned.1.call-done = f32[1,32,256]{2,1,0:T(8,128)} async-done(((f32[1,128,256]{2,1,0:T(8,128)}), f32[1,32,256]{2,1,0:T(8,128)}) %reduce-scatter.2.cloned.1.call-update) | async-done | bytes 32784 | tf_op jit(solution)/shard_map/reduce_scatter | solution.py:45
  (5 shorter events, 0.1 us)
Async XLA Ops:
  6.5 56.7 %copy-start = (bf16[512,512]{1,0:T(8,128)(2,1)S(1)}, bf16[512,512]{1,0:T(8,128)(2,1)}, u32[]{:S(2)}) copy-start(bf16[512,512]{1,0:T(8,128)(2,1)} %param.4) | copy-start | bytes 1572868
  6.5 56.7 %all-gather.2.cloned.1.call-start = ((), (), s32[]{:S(2)}) async-start(), calls=%async_computation.3 | async-start | bytes 2359296 | tf_op jit(solution)/shard_map/all_gather | solution.py:26
  8.8 61.7 %all-to-all-start = ((s32[8,1,2]{2,1,0:T(1,128)}), s32[8,1,2]{2,1,0:T(1,128)S(1)}, u32[]{:S(2)}, u32[]{:S(2)}) async-start(s32[8,1,2]{2,1,0:T(1,128)} %copy.11), calls=%async_computation | async-start | bytes 8192 | tf_op jit(solution)/shard_map/all_to_all | solution.py:35
  70.5 30.0 %copy-start.1 = (bf16[1,4,256,256]{3,2,1,0:T(8,128)(2,1)S(1)}, bf16[1,4,256,256]{3,2,1,0:T(8,128)(2,1)}, u32[]{:S(2)}) copy-start(bf16[1,4,256,256]{3,2,1,0:T(8,128)(2,1)} %param.7) | copy-start | bytes 1572868
  70.5 29.2 %all-to-all-start.1 = ((bf16[8,2,128,256]{3,1,2,0:T(2,128)(2,1)}), bf16[8,2,128,256]{3,1,2,0:T(2,128)(2,1)S(1)}, u32[]{:S(2)}, u32[]{:S(2)}) async-start(bf16[8,2,128,256]{3,1,2,0:T(2,128)(2,1)} %fusion.2), calls=%async_computation.1 | async-start | bytes 2097152 | tf_op jit(solution)/shard_map/all_to_all | solution.py:34
  74.2 46.2 %reduce-scatter.2.cloned.1.call-start = ((), (), s32[]{:S(2)}) async-start(), calls=%async_computation.4 | async-start | bytes 163840 | tf_op jit(solution)/shard_map/reduce_scatter | solution.py:45
Sparse Core Ops, SparseCore 0:
  9.4 53.7 all-gather.1
  101.7 18.6 reduce-scatter.1
where the time goes:
time: 127 us
  waiting for transfers between devices  91.9 us (72%)
  between operations  13.4 us (11%)
  starting transfers between devices  11 us (9%)
  matrix products  8.44 us (7%)
  local copies, waits for them, and re-layouts  1.55 us (1%)
    all_gather x1, waiting for transfers between devices, shards(): lax.all_gather(green_occ, 'grid', axis=1, tiled=True)  47 us
    all_to_all x1, waiting for transfers between devices, shards(): lax.all_to_all(outgoing, 'grid', split_axis=0, concat_axis=0, tiled=True)  25.4 us
    reduce_scatter x1, waiting for transfers between devices, shards(): lax.psum_scatter(owner_part[None], 'rep', scatter_dimension=1, tiled=True)  18.8 us
    all_to_all x1, starting transfers between devices, shards(): lax.all_to_all(labels, 'grid', split_axis=0, concat_axis=0, tiled=True)  7.28 us
    dot_general x1, matrix products, shards(): jnp.einsum('ldc,ltdw->dctw', place_weights, tile_blocks, preferred_elemen...  3.75 us
    all_to_all x1, starting transfers between devices, shards(): lax.all_to_all(outgoing, 'grid', split_axis=0, concat_axis=0, tiled=True)  3.69 us
    dot_general x1, matrix products, shards(): jnp.dot(integrals, lax.all_gather(green_occ, 'grid', axis=1, tiled=True),...  2.85 us
  transfers between devices with their start and end apart: 4, of which 3 were waited for; matrix products, arithmetic and copies ran while one was open for 7% of the time, Pallas kernels for 0%

commit v1 on v0

v1 whole, which is shorter than its diff:
```python
import functools

import jax
import jax.numpy as jnp
from jax import lax
from jax.experimental import pallas as pl
from jax.experimental.pallas import tpu as pltpu
from jax.sharding import PartitionSpec as P

AXES = ("grid", "rep")
CAP = 2
LABEL_ROWS = 16


def contract_kernel(panel, listed, own, sibling, green, message, chosen):
    tiles, rows, _ = own.shape
    hits = []
    for block, source in enumerate((own, sibling)):
        picks, count = [jnp.int32(0)] * CAP, jnp.int32(0)
        for tile in range(tiles):
            hit = functools.reduce(
                jnp.logical_or, [listed[block, tile, s] == panel[0] for s in range(listed.shape[2])]
            )
            picks = [jnp.where(hit & (count == n), tile, pick) for n, pick in enumerate(picks)]
            count = count + hit.astype(jnp.int32)
        for n, pick in enumerate(picks):
            slot = block * CAP + n
            chosen[slot * rows : (slot + 1) * rows, :] = source[pick]
            hits.append((n < count, block * tiles + pick))
    product = jnp.dot(chosen[...], green[...], preferred_element_type=jnp.float32)
    width = message.shape[1]
    line = lax.broadcasted_iota(jnp.int32, (LABEL_ROWS, width), 0)
    labels = jnp.zeros((LABEL_ROWS, width), jnp.float32)
    for slot, (used, label) in enumerate(hits):
        part = product[slot * rows : (slot + 1) * rows]
        part = jnp.where(used, part, jnp.zeros_like(part))
        message[slot * rows : (slot + 1) * rows, :] = part.astype(message.dtype)
        labels = jnp.where((line == slot) & used, label.astype(jnp.float32), labels)
    message[len(hits) * rows :, :] = labels.astype(message.dtype)


def contract(panel, listed, own, sibling, green):
    tiles, rows, depth = own.shape
    slots, width = 2 * CAP, green.shape[1]
    smem, vmem = pl.BlockSpec(memory_space=pltpu.SMEM), pl.BlockSpec(memory_space=pltpu.VMEM)
    return pl.pallas_call(
        contract_kernel,
        out_shape=jax.ShapeDtypeStruct((slots * rows + LABEL_ROWS, width), jnp.bfloat16),
        in_specs=[smem, smem, vmem, vmem, vmem],
        out_specs=vmem,
        scratch_shapes=[pltpu.VMEM((slots * rows, depth), jnp.bfloat16)],
        cost_estimate=pl.CostEstimate(
            flops=2 * slots * rows * depth * width,
            bytes_accessed=2 * (2 * tiles * rows * depth + depth * width + slots * rows * width),
            transcendentals=0,
        ),
        name="contract",
    )(panel, listed, own, sibling, green)


def virtual_kernel(message, own, sibling, before, total):
    tiles = own.shape[0]
    rows = total.shape[0]
    slots = (message.shape[0] - LABEL_ROWS) // rows
    labels = message[slots * rows :, :].astype(jnp.float32)
    line = lax.broadcasted_iota(jnp.int32, labels.shape, 0)
    result = before[...]
    for slot in range(slots):
        label = jnp.max(jnp.where(line == slot, labels, 0.0)).astype(jnp.int32)
        half, start = (own, 0) if slot < CAP else (sibling, tiles)
        place = jnp.clip(label - start, 0, tiles - 1)
        result = result + jnp.dot(
            message[slot * rows : (slot + 1) * rows, :], half[place], preferred_element_type=jnp.float32
        )
    total[...] = result


def virtual_product(message, own, sibling, before):
    vmem = pl.BlockSpec(memory_space=pltpu.VMEM)
    rows, columns = before.shape
    return pl.pallas_call(
        virtual_kernel,
        out_shape=jax.ShapeDtypeStruct(before.shape, jnp.float32),
        in_specs=[vmem] * 4,
        out_specs=vmem,
        cost_estimate=pl.CostEstimate(
            flops=2 * message.shape[0] * message.shape[1] * columns,
            bytes_accessed=2 * (message.size + own.size + sibling.size) + 8 * before.size,
            transcendentals=0,
        ),
        name="virtual_product",
    )(message, own, sibling, before)


def shards(integrals, green_occ, tile_panels, virtual_blocks):
    grid_count, rep_count = lax.axis_size("grid"), lax.axis_size("rep")
    pairs = rep_count // 2
    share = grid_count // rep_count
    tile_count = tile_panels.shape[0]
    rows = integrals.shape[0] // tile_count
    place, rep = lax.axis_index("grid"), lax.axis_index("rep")

    def offset(at, turn, k):
        return (at % 2) * (grid_count // 2) + ((at // 2) ^ turn) * share + k

    def send(array, target):
        order = []
        for g in range(grid_count):
            for r in range(rep_count):
                to_g, to_r = target(g, r)
                order.append((g * rep_count + r, to_g * rep_count + to_r))
        return lax.ppermute(array, AXES, order)

    def to_sibling(array):
        return send(array, lambda g, r: (g, r ^ 1))

    panels = {}
    for k in range(share):
        panels[0, k] = send(green_occ, lambda g, r, k=k: (g ^ offset(r, 0, k), r))
    own_tiles = integrals.reshape(tile_count, rows, -1)
    sibling_tiles = to_sibling(own_tiles)
    listed = jnp.stack([tile_panels, to_sibling(tile_panels)])
    own_virtual = virtual_blocks[0]
    sibling_virtual = to_sibling(own_virtual)
    for turn in range(1, pairs):
        for k in range(share):
            panels[turn, k] = send(panels[0, k], lambda g, r, t=turn: (g, r ^ (2 * t)))

    messages = []
    for turn in range(pairs):
        for k in range(share):
            panel = (place ^ offset(rep, turn, k)).astype(jnp.int32).reshape(1)
            message = contract(panel, listed, own_tiles, sibling_tiles, panels[turn, k])
            messages.append(send(message, lambda g, r, t=turn, k=k: (g ^ offset(r, t, k), r)))

    total = jnp.zeros((rows, virtual_blocks.shape[-1]), jnp.float32)
    for message in messages:
        total = virtual_product(message, own_virtual, sibling_virtual, total)

    step = rep_count // 2
    while step:
        half = total.shape[0] // 2
        low, high = total[:half], total[half:]
        upper = (rep // step) % 2 == 1
        kept, given = jnp.where(upper, high, low), jnp.where(upper, low, high)
        total = kept + send(given, lambda g, r, s=step: (g, r ^ s))
        step //= 2
    return total[None]


def solution(mesh):
    in_specs = (
        P(("grid", "rep"), None),
        P(None, "grid"),
        P(("grid", "rep"), None),
        P("grid", "rep", None, None),
    )
    out_specs = P("grid", "rep", None)
    return jax.shard_map(shards, mesh=mesh, in_specs=in_specs, out_specs=out_specs, check_vma=False)
```

time: 127 us -> 63.9 us (0.50)
  waiting for transfers between devices: 91.9 us -> 6.01 us
  starting transfers between devices: 11 us -> 31.2 us
  Pallas kernels: 0 us -> 18.4 us
  between operations: 13.4 us -> 0.08 us
  matrix products: 8.44 us -> 0 us
  local copies, waits for them, and re-layouts: 1.55 us -> 5.5 us
  other arithmetic: 0.84 us -> 2.16 us
    all_gather x1 -> x0, waiting for transfers between devices: 47 us -> none  [shards(): lax.all_gather(green_occ, 'grid', axis=1, tiled=True)]
    ppermute x0 -> x13, starting transfers between devices: none -> 31.2 us  [send(): return lax.ppermute(array, AXES, order)]
    all_to_all x2 -> x0, waiting for transfers between devices: 25.4 us -> none  [the longest x1 25.4 us: shards(): lax.all_to_all(outgoing, 'grid', split_axis=0, concat_axis=0, tiled=True)]
    reduce_scatter x1 -> x0, waiting for transfers between devices: 18.8 us -> none  [shards(): lax.psum_scatter(owner_part[None], 'rep', scatter_dimension=1, tiled=True)]
    pallas_call x0 -> x8, Pallas kernels: none -> 18.4 us  [the longest x4 9.31 us: virtual_product(): pl.pallas_call(virtual_kernel, out_shape=jax.ShapeDtypeStruct(before.shap...]
    all_to_all x2 -> x0, starting transfers between devices: 11 us -> none  [the longest x1 7.28 us: shards(): lax.all_to_all(labels, 'grid', split_axis=0, concat_axis=0, tiled=True)]
    dot_general x4 -> x0, matrix products: 8.44 us -> none  [the longest x1 3.75 us: shards(): jnp.einsum('ldc,ltdw->dctw', place_weights, tile_blocks, preferred_elemen...]
    ppermute x0 -> x13, waiting for transfers between devices: none -> 6.01 us  [send(): return lax.ppermute(array, AXES, order)]
  transfers between devices with their start and end apart: 4 -> 13, of which waited for: 3 -> 3; matrix products, arithmetic and copies ran while one was open for 7% -> 2% of each run, Pallas kernels for 0% -> 25%
where the time goes in v1:
time: 63.9 us; the launch traced here: 63.4 us
  starting transfers between devices  31.2 us (49%)
  Pallas kernels  18.4 us (29%)
  waiting for transfers between devices  6.01 us (9%)
  local copies, waits for them, and re-layouts  5.5 us (9%)
  other arithmetic  2.16 us (3%)
    ppermute x13, starting transfers between devices, send(): return lax.ppermute(array, AXES, order)  31.2 us
    pallas_call x4, Pallas kernels, virtual_product(): pl.pallas_call(virtual_kernel, out_shape=jax.ShapeDtypeStruct(before.shap...  9.31 us
    pallas_call x4, Pallas kernels, contract(): pl.pallas_call(contract_kernel, out_shape=jax.ShapeDtypeStruct((slots * r...  9.13 us
    ppermute x13, waiting for transfers between devices, send(): return lax.ppermute(array, AXES, order)  6.01 us
    unnamed x24, local copies, waits for them, and re-layouts  4.6 us
  transfers between devices with their start and end apart: 13, of which 3 were waited for; matrix products, arithmetic and copies ran while one was open for 2% of the time, Pallas kernels for 25%

profile of v1, /device:TPU:0, one launch (start us, length us, event | category | flops | bytes accessed | tf_op | source)
XLA Modules:
  0.0 63.4 jit_solution(17293015318247890494)
XLA Ops:
  0.0 0.5 collective-permute-start.1
  0.5 1.6 %collective-permute-start.6 = (bf16[512,256]{1,0:T(8,128)(2,1)}, bf16[512,256]{1,0:T(8,128)(2,1)S(1)}, u32[]{:S(2)}, u32[]{:S(2)}) collective-permute-start(bf16[512,256]{1,0:T(8,128)(2,1)} %param.5), channel_id=1, source_target_pairs={{0,0},{1,17},{2,10},{3,27},{4,4},{5,21},{6,14},{7,31},{8,8},{9,25}... | collective-permute-start | bytes 786440 | tf_op jit(solution)/shard_map/ppermute | solution.py:112
  2.1 2.7 %collective-permute-start.2 = (bf16[512,256]{1,0:T(8,128)(2,1)}, bf16[512,256]{1,0:T(8,128)(2,1)S(1)}, u32[]{:S(2)}, u32[]{:S(2)}) collective-permute-start(bf16[512,256]{1,0:T(8,128)(2,1)} %param.5), channel_id=1, source_target_pairs={{0,4},{1,21},{2,14},{3,31},{4,0},{5,17},{6,10},{7,27},{8,12},{9,29... | collective-permute-start | bytes 786440 | tf_op jit(solution)/shard_map/ppermute | solution.py:112
  4.7 0.0 collective-permute-done.6.green
  4.7 9.1 %collective-permute-start.7 = (bf16[512,256]{1,0:T(8,128)(2,1)S(1)}, bf16[512,256]{1,0:T(8,128)(2,1)S(1)}, u32[]{:S(2)}, u32[]{:S(2)}) collective-permute-start(bf16[512,256]{1,0:T(8,128)(2,1)S(1)} %collective-permute-done.6.green), channel_id=1, source_target_pairs={{0,2},{1,3},{2,0},{3,1},{4,6},{5,7},{6,4},{7,5},{8,10},{9,11},{10,... | collective-permute-start | bytes 786440 | tf_op jit(solution)/shard_map/ppermute | solution.py:112
  13.8 0.0 collective-permute-done.2.green
  13.8 6.6 %collective-permute-start.3 = (bf16[512,256]{1,0:T(8,128)(2,1)S(1)}, bf16[512,256]{1,0:T(8,128)(2,1)S(1)}, u32[]{:S(2)}, u32[]{:S(2)}) collective-permute-start(bf16[512,256]{1,0:T(8,128)(2,1)S(1)} %collective-permute-done.2.green), channel_id=1, source_target_pairs={{0,2},{1,3},{2,0},{3,1},{4,6},{5,7},{6,4},{7,5},{8,10},{9,11},{10,... | collective-permute-start | bytes 786440 | tf_op jit(solution)/shard_map/ppermute | solution.py:112
  20.4 0.6 collective-permute-start.5
  21.0 0.0 collective-permute-start
  21.0 0.1 copy.5
  21.1 1.3 %collective-permute-done = s32[4,2]{0,1:T(2,128)S(1)} collective-permute-done((s32[4,2]{0,1:T(2,128)S(1)}, s32[4,2]{0,1:T(2,128)S(1)}, u32[]{:S(2)}, u32[]{:S(2)}) %collective-permute-start) | collective-permute-done | bytes 64 | tf_op jit(solution)/shard_map/ppermute | solution.py:112
  22.4 0.1 copy.6
  22.5 0.6 pad_add_fusion.listed
  23.1 0.0 collective-permute-done.1.sibling
  23.1 0.8 %copy-done.1 = bf16[4,128,512]{2,1,0:T(8,128)(2,1)} copy-done((bf16[4,128,512]{2,1,0:T(8,128)(2,1)}, bf16[4,128,512]{2,1,0:T(8,128)(2,1)S(1)}, u32[]{:S(2)}) %copy-start.1) | copy-done | bytes 524312
  23.9 2.3 %contract.6 = bf16[528,256]{1,0:T(8,128)(2,1)} custom-call(s32[1]{0:T(128)} %bitcast.6.panel, s32[2,4,2]{2,1,0:T(4,128)} %pad_add_fusion.listed, bf16[4,128,512]{2,1,0:T(8,128)(2,1)} %bitcast.16, bf16[4,128,512]{2,1,0:T(8,128)(2,1)} %copy-done.1, bf16[512,256]{1,0:T(8,128)(2,1)} %copy-done.7), custom_call_target="tpu_custom_call" | custom-call | flops 134217728 | bytes 1572864 | tf_op jit(solution)/shard_map/contract/pallas_call | solution.py:46
  26.2 0.5 collective-permute-start.9
  26.7 2.3 %contract.7 = bf16[528,256]{1,0:T(8,128)(2,1)} custom-call(s32[1]{0:T(128)} %bitcast.7.panel, s32[2,4,2]{2,1,0:T(4,128)} %pad_add_fusion.listed, bf16[4,128,512]{2,1,0:T(8,128)(2,1)} %bitcast.17, bf16[4,128,512]{2,1,0:T(8,128)(2,1)} %copy-done.1, bf16[512,256]{1,0:T(8,128)(2,1)} %copy-done.8), custom_call_target="tpu_custom_call" | custom-call | flops 134217728 | bytes 1572864 | tf_op jit(solution)/shard_map/contract/pallas_call | solution.py:46
  29.0 1.6 %collective-permute-start.10 = (bf16[528,256]{1,0:T(8,128)(2,1)}, bf16[528,256]{1,0:T(8,128)(2,1)S(1)}, u32[]{:S(2)}, u32[]{:S(2)}) collective-permute-start(bf16[528,256]{1,0:T(8,128)(2,1)} %contract.7), channel_id=1, source_target_pairs={{0,0},{1,17},{2,10},{3,27},{4,4},{5,21},{6,14},{7,31},{8,8},{9,25}... | collective-permute-start | bytes 811016 | tf_op jit(solution)/shard_map/ppermute | solution.py:112
  30.6 0.0 collective-permute-done.7.green
  30.6 0.7 %copy-done.10 = bf16[512,256]{1,0:T(8,128)(2,1)} copy-done((bf16[512,256]{1,0:T(8,128)(2,1)}, bf16[512,256]{1,0:T(8,128)(2,1)S(1)}, u32[]{:S(2)}) %copy-start.10) | copy-done | bytes 262168
  31.3 2.3 %contract.5 = bf16[528,256]{1,0:T(8,128)(2,1)} custom-call(s32[1]{0:T(128)} %bitcast.5.panel, s32[2,4,2]{2,1,0:T(4,128)} %pad_add_fusion.listed, bf16[4,128,512]{2,1,0:T(8,128)(2,1)} %bitcast.18, bf16[4,128,512]{2,1,0:T(8,128)(2,1)} %copy-done.1, bf16[512,256]{1,0:T(8,128)(2,1)} %copy-done.10), custom_call_target="tpu_custom_call" | custom-call | flops 134217728 | bytes 1572864 | tf_op jit(solution)/shard_map/contract/pallas_call | solution.py:46
  33.6 2.4 %collective-permute-start.8 = (bf16[528,256]{1,0:T(8,128)(2,1)}, bf16[528,256]{1,0:T(8,128)(2,1)S(1)}, u32[]{:S(2)}, u32[]{:S(2)}) collective-permute-start(bf16[528,256]{1,0:T(8,128)(2,1)} %contract.5), channel_id=1, source_target_pairs={{0,8},{1,25},{2,2},{3,19},{4,12},{5,29},{6,6},{7,23},{8,0},{9,17},... | collective-permute-start | bytes 811016 | tf_op jit(solution)/shard_map/ppermute | solution.py:112
  36.0 0.0 collective-permute-done.3.green
  36.0 0.7 %copy-done.9 = bf16[512,256]{1,0:T(8,128)(2,1)} copy-done((bf16[512,256]{1,0:T(8,128)(2,1)}, bf16[512,256]{1,0:T(8,128)(2,1)S(1)}, u32[]{:S(2)}) %copy-start.9) | copy-done | bytes 262168
  36.7 2.3 %contract.4 = bf16[528,256]{1,0:T(8,128)(2,1)} custom-call(s32[1]{0:T(128)} %bitcast.panel, s32[2,4,2]{2,1,0:T(4,128)} %pad_add_fusion.listed, bf16[4,128,512]{2,1,0:T(8,128)(2,1)} %bitcast.19, bf16[4,128,512]{2,1,0:T(8,128)(2,1)} %copy-done.1, bf16[512,256]{1,0:T(8,128)(2,1)} %copy-done.9), custom_call_target="tpu_custom_call" | custom-call | flops 134217728 | bytes 1572864 | tf_op jit(solution)/shard_map/contract/pallas_call | solution.py:46
  39.0 2.5 %collective-permute-start.4 = (bf16[528,256]{1,0:T(8,128)(2,1)}, bf16[528,256]{1,0:T(8,128)(2,1)S(1)}, u32[]{:S(2)}, u32[]{:S(2)}) collective-permute-start(bf16[528,256]{1,0:T(8,128)(2,1)} %contract.4), channel_id=1, source_target_pairs={{0,12},{1,29},{2,6},{3,23},{4,8},{5,25},{6,2},{7,19},{8,4},{9,21},... | collective-permute-start | bytes 811016 | tf_op jit(solution)/shard_map/ppermute | solution.py:112
  41.5 0.0 collective-permute-done.5.sibling
  41.5 0.0 collective-permute-done.10.message
  41.5 0.7 %broadcast_in_dim.6.before = f32[128,256]{1,0:T(8,128)} broadcast(f32[]{:T(128)} %constant.67.clone.1), dimensions={} | broadcast | bytes 131076 | tf_op jit(solution)/shard_map/broadcast_in_dim | solution.py:136
  42.2 0.1 copy-done
  42.4 0.1 copy-done.5
  42.5 2.3 %virtual_product.4.before = f32[128,256]{1,0:T(8,128)} custom-call(bf16[528,256]{1,0:T(8,128)(2,1)} %copy-done.5, bf16[4,256,256]{2,1,0:T(8,128)(2,1)} %bitcast.11, bf16[4,256,256]{2,1,0:T(8,128)(2,1)} %copy-done, f32[128,256]{1,0:T(8,128)} %broadcast_in_dim.6.before), custom_call_target="tpu_custom_call" | custom-call | flops 69206016 | bytes 1581056 | tf_op jit(solution)/shard_map/virtual_product/pallas_call | solution.py:81
  44.8 0.0 collective-permute-done.9.message
  44.8 0.7 %copy-done.3 = bf16[528,256]{1,0:T(8,128)(2,1)} copy-done((bf16[528,256]{1,0:T(8,128)(2,1)}, bf16[528,256]{1,0:T(8,128)(2,1)S(1)}, u32[]{:S(2)}) %copy-start.3) | copy-done | bytes 270360
  45.5 2.3 %virtual_product.5.before = f32[128,256]{1,0:T(8,128)} custom-call(bf16[528,256]{1,0:T(8,128)(2,1)} %copy-done.3, bf16[4,256,256]{2,1,0:T(8,128)(2,1)} %bitcast.12, bf16[4,256,256]{2,1,0:T(8,128)(2,1)} %copy-done, f32[128,256]{1,0:T(8,128)} %virtual_product.4.before), custom_call_target="tpu_custom_call" | custom-call | flops 69206016 | bytes 1581056 | tf_op jit(solution)/shard_map/virtual_product/pallas_call | solution.py:81
  47.8 0.0 collective-permute-done.8.message
  47.8 0.7 %copy-done.4 = bf16[528,256]{1,0:T(8,128)(2,1)} copy-done((bf16[528,256]{1,0:T(8,128)(2,1)}, bf16[528,256]{1,0:T(8,128)(2,1)S(1)}, u32[]{:S(2)}) %copy-start.4) | copy-done | bytes 270360
  48.5 2.3 %virtual_product.6.before = f32[128,256]{1,0:T(8,128)} custom-call(bf16[528,256]{1,0:T(8,128)(2,1)} %copy-done.4, bf16[4,256,256]{2,1,0:T(8,128)(2,1)} %bitcast.13, bf16[4,256,256]{2,1,0:T(8,128)(2,1)} %copy-done, f32[128,256]{1,0:T(8,128)} %virtual_product.5.before), custom_call_target="tpu_custom_call" | custom-call | flops 69206016 | bytes 1581056 | tf_op jit(solution)/shard_map/virtual_product/pallas_call | solution.py:81
  50.9 0.0 collective-permute-done.4.message
  50.9 0.7 %copy-done.6 = bf16[528,256]{1,0:T(8,128)(2,1)} copy-done((bf16[528,256]{1,0:T(8,128)(2,1)}, bf16[528,256]{1,0:T(8,128)(2,1)S(1)}, u32[]{:S(2)}) %copy-start.6) | copy-done | bytes 270360
  51.6 2.3 %virtual_product.7 = f32[128,256]{1,0:T(8,128)} custom-call(bf16[528,256]{1,0:T(8,128)(2,1)} %copy-done.6, bf16[4,256,256]{2,1,0:T(8,128)(2,1)} %bitcast.14, bf16[4,256,256]{2,1,0:T(8,128)(2,1)} %copy-done, f32[128,256]{1,0:T(8,128)} %virtual_product.6.before), custom_call_target="tpu_custom_call" | custom-call | flops 69206016 | bytes 1581056 | tf_op jit(solution)/shard_map/virtual_product/pallas_call | solution.py:81
  53.9 0.9 %slice_select_fusion = f32[64,256]{1,0:T(8,128)S(1)} fusion(f32[128,256]{1,0:T(8,128)} %virtual_product.7, pred[]{:T(512)S(6)} %eq.14), kind=kLoop, calls=%fused_computation.1 | loop fusion | flops 16384 | bytes 196609 | tf_op jit(solution)/shard_map/jit(_where)/select_n | solution.py:145
  54.8 0.5 collective-permute-start.11
  55.3 3.8 %collective-permute-done.11 = f32[64,256]{1,0:T(8,128)S(1)} collective-permute-done((f32[64,256]{1,0:T(8,128)S(1)}, f32[64,256]{1,0:T(8,128)S(1)}, u32[]{:S(2)}, u32[]{:S(2)}) %collective-permute-start.11) | collective-permute-done | bytes 65568 | tf_op jit(solution)/shard_map/ppermute | solution.py:112
  59.2 2.8 %collective-permute-start.12 = (f32[32,256]{1,0:T(8,128)S(1)}, f32[32,256]{1,0:T(8,128)S(1)}, u32[]{:S(2)}, u32[]{:S(2)}) collective-permute-start(f32[32,256]{1,0:T(8,128)S(1)} %slice_select_fusion.1), channel_id=1, source_target_pairs={{0,1},{1,0},{2,3},{3,2},{4,5},{5,4},{6,7},{7,6},{8,9},{9,8},{10,11... | collective-permute-start | bytes 98312 | tf_op jit(solution)/shard_map/ppermute | solution.py:112
  61.9 0.9 %collective-permute-done.12 = f32[32,256]{1,0:T(8,128)S(1)} collective-permute-done((f32[32,256]{1,0:T(8,128)S(1)}, f32[32,256]{1,0:T(8,128)S(1)}, u32[]{:S(2)}, u32[]{:S(2)}) %collective-permute-start.12) | collective-permute-done | bytes 32800 | tf_op jit(solution)/shard_map/ppermute | solution.py:112
  62.8 0.6 add_bitcast_fusion
  (18 shorter events, 0.0 us)
Async XLA Ops:
  0.0 21.0 %copy-start.11 = (s32[4,2]{0,1:T(2,128)S(1)}, s32[4,2]{0,1:T(2,128)}, u32[]{:S(2)}) copy-start(s32[4,2]{0,1:T(2,128)} %param.6) | copy-start | bytes 100
  0.0 23.1 %collective-permute-start.1 = (bf16[4,128,512]{2,1,0:T(8,128)(2,1)}, bf16[4,128,512]{2,1,0:T(8,128)(2,1)S(1)}, u32[]{:S(2)}, u32[]{:S(2)}) collective-permute-start(bf16[4,128,512]{2,1,0:T(8,128)(2,1)} %bitcast.15), channel_id=1, source_target_pairs={{0,1},{1,0},{2,3},{3,2},{4,5},{5,4},{6,7},{7,6},{8,9},{9,8},{10,11... | collective-permute-start | bytes 1572872 | tf_op jit(solution)/shard_map/ppermute | solution.py:112
  0.5 4.3 %collective-permute-start.6 = (bf16[512,256]{1,0:T(8,128)(2,1)}, bf16[512,256]{1,0:T(8,128)(2,1)S(1)}, u32[]{:S(2)}, u32[]{:S(2)}) collective-permute-start(bf16[512,256]{1,0:T(8,128)(2,1)} %param.5), channel_id=1, source_target_pairs={{0,0},{1,17},{2,10},{3,27},{4,4},{5,21},{6,14},{7,31},{8,8},{9,25}... | collective-permute-start | bytes 786440 | tf_op jit(solution)/shard_map/ppermute | solution.py:112
  2.1 11.8 %collective-permute-start.2 = (bf16[512,256]{1,0:T(8,128)(2,1)}, bf16[512,256]{1,0:T(8,128)(2,1)S(1)}, u32[]{:S(2)}, u32[]{:S(2)}) collective-permute-start(bf16[512,256]{1,0:T(8,128)(2,1)} %param.5), channel_id=1, source_target_pairs={{0,4},{1,21},{2,14},{3,31},{4,0},{5,17},{6,10},{7,27},{8,12},{9,29... | collective-permute-start | bytes 786440 | tf_op jit(solution)/shard_map/ppermute | solution.py:112
  4.7 21.5 %copy-start.8 = (bf16[512,256]{1,0:T(8,128)(2,1)}, bf16[512,256]{1,0:T(8,128)(2,1)S(1)}, u32[]{:S(2)}) copy-start(bf16[512,256]{1,0:T(8,128)(2,1)S(1)} %collective-permute-done.6.green) | copy-start | bytes 786436
  4.7 25.9 %collective-permute-start.7 = (bf16[512,256]{1,0:T(8,128)(2,1)S(1)}, bf16[512,256]{1,0:T(8,128)(2,1)S(1)}, u32[]{:S(2)}, u32[]{:S(2)}) collective-permute-start(bf16[512,256]{1,0:T(8,128)(2,1)S(1)} %collective-permute-done.6.green), channel_id=1, source_target_pairs={{0,2},{1,3},{2,0},{3,1},{4,6},{5,7},{6,4},{7,5},{8,10},{9,11},{10,... | collective-permute-start | bytes 786440 | tf_op jit(solution)/shard_map/ppermute | solution.py:112
  13.8 9.3 %copy-start.7 = (bf16[512,256]{1,0:T(8,128)(2,1)}, bf16[512,256]{1,0:T(8,128)(2,1)S(1)}, u32[]{:S(2)}) copy-start(bf16[512,256]{1,0:T(8,128)(2,1)S(1)} %collective-permute-done.2.green) | copy-start | bytes 786436
  13.8 22.2 %collective-permute-start.3 = (bf16[512,256]{1,0:T(8,128)(2,1)S(1)}, bf16[512,256]{1,0:T(8,128)(2,1)S(1)}, u32[]{:S(2)}, u32[]{:S(2)}) collective-permute-start(bf16[512,256]{1,0:T(8,128)(2,1)S(1)} %collective-permute-done.2.green), channel_id=1, source_target_pairs={{0,2},{1,3},{2,0},{3,1},{4,6},{5,7},{6,4},{7,5},{8,10},{9,11},{10,... | collective-permute-start | bytes 786440 | tf_op jit(solution)/shard_map/ppermute | solution.py:112
  20.4 21.1 %collective-permute-start.5 = (bf16[4,256,256]{2,1,0:T(8,128)(2,1)}, bf16[4,256,256]{2,1,0:T(8,128)(2,1)S(1)}, u32[]{:S(2)}, u32[]{:S(2)}) collective-permute-start(bf16[4,256,256]{2,1,0:T(8,128)(2,1)} %bitcast.10), channel_id=1, source_target_pairs={{0,1},{1,0},{2,3},{3,2},{4,5},{5,4},{6,7},{7,6},{8,9},{9,8},{10,11... | collective-permute-start | bytes 1572872 | tf_op jit(solution)/shard_map/ppermute | solution.py:112
  21.0 1.4 %collective-permute-start = (s32[4,2]{0,1:T(2,128)S(1)}, s32[4,2]{0,1:T(2,128)S(1)}, u32[]{:S(2)}, u32[]{:S(2)}) collective-permute-start(s32[4,2]{0,1:T(2,128)S(1)} %copy-done.11), channel_id=1, source_target_pairs={{0,1},{1,0},{2,3},{3,2},{4,5},{5,4},{6,7},{7,6},{8,9},{9,8},{10,11... | collective-permute-start | bytes 104 | tf_op jit(solution)/shard_map/ppermute | solution.py:112
  23.1 0.8 %copy-start.1 = (bf16[4,128,512]{2,1,0:T(8,128)(2,1)}, bf16[4,128,512]{2,1,0:T(8,128)(2,1)S(1)}, u32[]{:S(2)}) copy-start(bf16[4,128,512]{2,1,0:T(8,128)(2,1)S(1)} %collective-permute-done.1.sibling) | copy-start | bytes 1572868
  26.2 18.6 %collective-permute-start.9 = (bf16[528,256]{1,0:T(8,128)(2,1)}, bf16[528,256]{1,0:T(8,128)(2,1)S(1)}, u32[]{:S(2)}, u32[]{:S(2)}) collective-permute-start(bf16[528,256]{1,0:T(8,128)(2,1)} %contract.6), channel_id=1, source_target_pairs={{0,4},{1,21},{2,14},{3,31},{4,0},{5,17},{6,10},{7,27},{8,12},{9,29... | collective-permute-start | bytes 811016 | tf_op jit(solution)/shard_map/ppermute | solution.py:112
  29.0 12.5 %collective-permute-start.10 = (bf16[528,256]{1,0:T(8,128)(2,1)}, bf16[528,256]{1,0:T(8,128)(2,1)S(1)}, u32[]{:S(2)}, u32[]{:S(2)}) collective-permute-start(bf16[528,256]{1,0:T(8,128)(2,1)} %contract.7), channel_id=1, source_target_pairs={{0,0},{1,17},{2,10},{3,27},{4,4},{5,21},{6,14},{7,31},{8,8},{9,25}... | collective-permute-start | bytes 811016 | tf_op jit(solution)/shard_map/ppermute | solution.py:112
  30.6 0.7 %copy-start.10 = (bf16[512,256]{1,0:T(8,128)(2,1)}, bf16[512,256]{1,0:T(8,128)(2,1)S(1)}, u32[]{:S(2)}) copy-start(bf16[512,256]{1,0:T(8,128)(2,1)S(1)} %collective-permute-done.7.green) | copy-start | bytes 786436
  33.6 14.3 %collective-permute-start.8 = (bf16[528,256]{1,0:T(8,128)(2,1)}, bf16[528,256]{1,0:T(8,128)(2,1)S(1)}, u32[]{:S(2)}, u32[]{:S(2)}) collective-permute-start(bf16[528,256]{1,0:T(8,128)(2,1)} %contract.5), channel_id=1, source_target_pairs={{0,8},{1,25},{2,2},{3,19},{4,12},{5,29},{6,6},{7,23},{8,0},{9,17},... | collective-permute-start | bytes 811016 | tf_op jit(solution)/shard_map/ppermute | solution.py:112
  36.0 0.7 %copy-start.9 = (bf16[512,256]{1,0:T(8,128)(2,1)}, bf16[512,256]{1,0:T(8,128)(2,1)S(1)}, u32[]{:S(2)}) copy-start(bf16[512,256]{1,0:T(8,128)(2,1)S(1)} %collective-permute-done.3.green) | copy-start | bytes 786436
  39.0 11.8 %collective-permute-start.4 = (bf16[528,256]{1,0:T(8,128)(2,1)}, bf16[528,256]{1,0:T(8,128)(2,1)S(1)}, u32[]{:S(2)}, u32[]{:S(2)}) collective-permute-start(bf16[528,256]{1,0:T(8,128)(2,1)} %contract.4), channel_id=1, source_target_pairs={{0,12},{1,29},{2,6},{3,23},{4,8},{5,25},{6,2},{7,19},{8,4},{9,21},... | collective-permute-start | bytes 811016 | tf_op jit(solution)/shard_map/ppermute | solution.py:112
  41.5 0.9 %copy-start = (bf16[4,256,256]{2,1,0:T(8,128)(2,1)}, bf16[4,256,256]{2,1,0:T(8,128)(2,1)S(1)}, u32[]{:S(2)}) copy-start(bf16[4,256,256]{2,1,0:T(8,128)(2,1)S(1)} %collective-permute-done.5.sibling) | copy-start | bytes 1572868
  41.5 1.0 %copy-start.5 = (bf16[528,256]{1,0:T(8,128)(2,1)}, bf16[528,256]{1,0:T(8,128)(2,1)S(1)}, u32[]{:S(2)}) copy-start(bf16[528,256]{1,0:T(8,128)(2,1)S(1)} %collective-permute-done.10.message) | copy-start | bytes 811012
  44.8 0.7 %copy-start.3 = (bf16[528,256]{1,0:T(8,128)(2,1)}, bf16[528,256]{1,0:T(8,128)(2,1)S(1)}, u32[]{:S(2)}) copy-start(bf16[528,256]{1,0:T(8,128)(2,1)S(1)} %collective-permute-done.9.message) | copy-start | bytes 811012
  47.8 0.7 %copy-start.4 = (bf16[528,256]{1,0:T(8,128)(2,1)}, bf16[528,256]{1,0:T(8,128)(2,1)S(1)}, u32[]{:S(2)}) copy-start(bf16[528,256]{1,0:T(8,128)(2,1)S(1)} %collective-permute-done.8.message) | copy-start | bytes 811012
  50.9 0.7 %copy-start.6 = (bf16[528,256]{1,0:T(8,128)(2,1)}, bf16[528,256]{1,0:T(8,128)(2,1)S(1)}, u32[]{:S(2)}) copy-start(bf16[528,256]{1,0:T(8,128)(2,1)S(1)} %collective-permute-done.4.message) | copy-start | bytes 811012
  53.9 5.3 %copy-start.2 = (f32[128,256]{1,0:T(8,128)S(1)}, f32[128,256]{1,0:T(8,128)}, u32[]{:S(2)}) copy-start(f32[128,256]{1,0:T(8,128)} %virtual_product.7) | copy-start | bytes 393220
  54.8 4.3 %collective-permute-start.11 = (f32[64,256]{1,0:T(8,128)S(1)}, f32[64,256]{1,0:T(8,128)S(1)}, u32[]{:S(2)}, u32[]{:S(2)}) collective-permute-start(f32[64,256]{1,0:T(8,128)S(1)} %slice_select_fusion), channel_id=1, source_target_pairs={{0,2},{1,3},{2,0},{3,1},{4,6},{5,7},{6,4},{7,5},{8,10},{9,11},{10,... | collective-permute-start | bytes 196616 | tf_op jit(solution)/shard_map/ppermute | solution.py:112
  59.2 3.6 %collective-permute-start.12 = (f32[32,256]{1,0:T(8,128)S(1)}, f32[32,256]{1,0:T(8,128)S(1)}, u32[]{:S(2)}, u32[]{:S(2)}) collective-permute-start(f32[32,256]{1,0:T(8,128)S(1)} %slice_select_fusion.1), channel_id=1, source_target_pairs={{0,1},{1,0},{2,3},{3,2},{4,5},{5,4},{6,7},{7,6},{8,9},{9,8},{10,11... | collective-permute-start | bytes 98312 | tf_op jit(solution)/shard_map/ppermute | solution.py:112

commit v2 on v1

--- a/solution.py
+++ b/solution.py
@@ -9,6 +9,7 @@
 
 AXES = ("grid", "rep")
 CAP = 2
+KERNEL_VMEM = 16 << 20
 LABEL_ROWS = 16
 
 
@@ -54,6 +55,7 @@
             bytes_accessed=2 * (2 * tiles * rows * depth + depth * width + slots * rows * width),
             transcendentals=0,
         ),
+        compiler_params=pltpu.CompilerParams(vmem_limit_bytes=KERNEL_VMEM),
         name="contract",
     )(panel, listed, own, sibling, green)
 
@@ -88,6 +90,7 @@
             bytes_accessed=2 * (message.size + own.size + sibling.size) + 8 * before.size,
             transcendentals=0,
         ),
+        compiler_params=pltpu.CompilerParams(vmem_limit_bytes=KERNEL_VMEM),
         name="virtual_product",
     )(message, own, sibling, before)
 

time: 63.9 us -> 56.1 us (0.88)
  Pallas kernels: 18.4 us -> 5.05 us
  waiting for transfers between devices: 6.01 us -> 16.2 us
  local copies, waits for them, and re-layouts: 5.5 us -> 2.89 us
  other arithmetic: 2.16 us -> 0.66 us
  starting transfers between devices: 31.2 us -> 30.4 us
    ppermute x13, waiting for transfers between devices: 6.01 us -> 16.2 us  [send(): return lax.ppermute(array, AXES, order)]
    pallas_call x4, Pallas kernels: 9.31 us -> 1.47 us  [virtual_product(): pl.pallas_call(virtual_kernel, out_shape=jax.ShapeDtypeStruct(before.shap...]
    pallas_call x4, Pallas kernels: 9.13 us -> 3.58 us  [contract(): pl.pallas_call(contract_kernel, out_shape=jax.ShapeDtypeStruct((slots * r...]
    unnamed x24 -> x12, local copies, waits for them, and re-layouts: 4.6 us -> 2.7 us
    select_n x2, other arithmetic: 0.93 us -> 0.02 us  [shards(): kept, given = (jnp.where(upper, high, low), jnp.where(upper, low, high))]
    ppermute x13, starting transfers between devices: 31.2 us -> 30.4 us  [send(): return lax.ppermute(array, AXES, order)]
    broadcast_in_dim x1, local copies, waits for them, and re-layouts: 0.72 us -> 0.01 us  [shards(): total = jnp.zeros((rows, virtual_blocks.shape[-1]), jnp.float32)]
  transfers between devices with their start and end apart: 13 -> 13, of which waited for: 3 -> 5; matrix products, arithmetic and copies ran while one was open for 2% -> 0% of each run, Pallas kernels for 25% -> 8%
where the time goes in v2:
time: 56.1 us; the launch traced here: 55.4 us
  starting transfers between devices  30.4 us (54%)
  waiting for transfers between devices  16.2 us (29%)
  Pallas kernels  5.05 us (9%)
  local copies, waits for them, and re-layouts  2.89 us (5%)
  other arithmetic  0.66 us (1%)
    ppermute x13, starting transfers between devices, send(): return lax.ppermute(array, AXES, order)  30.4 us
    ppermute x13, waiting for transfers between devices, send(): return lax.ppermute(array, AXES, order)  16.2 us
    pallas_call x4, Pallas kernels, contract(): pl.pallas_call(contract_kernel, out_shape=jax.ShapeDtypeStruct((slots * r...  3.58 us
    unnamed x12, local copies, waits for them, and re-layouts  2.7 us
    pallas_call x4, Pallas kernels, virtual_product(): pl.pallas_call(virtual_kernel, out_shape=jax.ShapeDtypeStruct(before.shap...  1.47 us
  transfers between devices with their start and end apart: 13, of which 5 were waited for; matrix products, arithmetic and copies ran while one was open for 0% of the time, Pallas kernels for 8%

profile of v2, /device:TPU:0, one launch (start us, length us, event | category | flops | bytes accessed | tf_op | source)
XLA Modules:
  0.0 55.4 jit_solution(16341292802797683879)
XLA Ops:
  0.0 0.0 copy-start.5
  0.0 0.5 collective-permute-start.1
  0.5 1.6 %collective-permute-start.6 = (bf16[512,256]{1,0:T(8,128)(2,1)}, bf16[512,256]{1,0:T(8,128)(2,1)S(1)}, u32[]{:S(2)}, u32[]{:S(2)}) collective-permute-start(bf16[512,256]{1,0:T(8,128)(2,1)} %param.5), channel_id=1, source_target_pairs={{0,0},{1,17},{2,10},{3,27},{4,4},{5,21},{6,14},{7,31},{8,8},{9,25}... | collective-permute-start | bytes 786440 | tf_op jit(solution)/shard_map/ppermute | solution.py:115
  2.1 2.7 %collective-permute-start.2 = (bf16[512,256]{1,0:T(8,128)(2,1)}, bf16[512,256]{1,0:T(8,128)(2,1)S(1)}, u32[]{:S(2)}, u32[]{:S(2)}) collective-permute-start(bf16[512,256]{1,0:T(8,128)(2,1)} %param.5), channel_id=1, source_target_pairs={{0,4},{1,21},{2,14},{3,31},{4,0},{5,17},{6,10},{7,27},{8,12},{9,29... | collective-permute-start | bytes 786440 | tf_op jit(solution)/shard_map/ppermute | solution.py:115
  4.7 0.0 collective-permute-done.6.green
  4.7 9.1 %collective-permute-start.7 = (bf16[512,256]{1,0:T(8,128)(2,1)S(1)}, bf16[512,256]{1,0:T(8,128)(2,1)S(1)}, u32[]{:S(2)}, u32[]{:S(2)}) collective-permute-start(bf16[512,256]{1,0:T(8,128)(2,1)S(1)} %collective-permute-done.6.green), channel_id=1, source_target_pairs={{0,2},{1,3},{2,0},{3,1},{4,6},{5,7},{6,4},{7,5},{8,10},{9,11},{10,... | collective-permute-start | bytes 786440 | tf_op jit(solution)/shard_map/ppermute | solution.py:115
  13.8 0.0 collective-permute-done.2.green
  13.8 6.6 %collective-permute-start.3 = (bf16[512,256]{1,0:T(8,128)(2,1)S(1)}, bf16[512,256]{1,0:T(8,128)(2,1)S(1)}, u32[]{:S(2)}, u32[]{:S(2)}) collective-permute-start(bf16[512,256]{1,0:T(8,128)(2,1)S(1)} %collective-permute-done.2.green), channel_id=1, source_target_pairs={{0,2},{1,3},{2,0},{3,1},{4,6},{5,7},{6,4},{7,5},{8,10},{9,11},{10,... | collective-permute-start | bytes 786440 | tf_op jit(solution)/shard_map/ppermute | solution.py:115
  20.4 0.6 %collective-permute-start.5 = (bf16[4,256,256]{2,1,0:T(8,128)(2,1)}, bf16[4,256,256]{2,1,0:T(8,128)(2,1)S(1)}, u32[]{:S(2)}, u32[]{:S(2)}) collective-permute-start(bf16[4,256,256]{2,1,0:T(8,128)(2,1)} %bitcast.10), channel_id=1, source_target_pairs={{0,1},{1,0},{2,3},{3,2},{4,5},{5,4},{6,7},{7,6},{8,9},{9,8},{10,11... | collective-permute-start | bytes 1572872 | tf_op jit(solution)/shard_map/ppermute | solution.py:115
  21.0 0.0 copy-done.5
  21.0 0.0 collective-permute-start
  21.0 0.1 copy.5
  21.1 1.3 %collective-permute-done = s32[4,2]{0,1:T(2,128)S(1)} collective-permute-done((s32[4,2]{0,1:T(2,128)S(1)}, s32[4,2]{0,1:T(2,128)S(1)}, u32[]{:S(2)}, u32[]{:S(2)}) %collective-permute-start) | collective-permute-done | bytes 64 | tf_op jit(solution)/shard_map/ppermute | solution.py:115
  22.4 0.1 copy.6
  22.5 0.0 collective-permute-done.1.sibling
  22.5 0.0 copy-start.1
  22.5 1.0 %copy-done.1 = bf16[512,512]{1,0:T(8,128)(2,1)S(1)} copy-done((bf16[512,512]{1,0:T(8,128)(2,1)S(1)}, bf16[512,512]{1,0:T(8,128)(2,1)}, u32[]{:S(2)}) %copy-start.1) | copy-done | bytes 524312
  23.5 0.9 %contract.6 = bf16[528,256]{1,0:T(8,128)(2,1)S(1)} custom-call(s32[1]{0:T(128)} %bitcast.6.panel, s32[2,4,2]{2,1,0:T(4,128)S(1)} %pad_add_fusion.listed, bf16[4,128,512]{2,1,0:T(8,128)(2,1)S(1)} %bitcast.16, bf16[4,128,512]{2,1,0:T(8,128)(2,1)S(1)} %collective-permute-done.1.sibling, bf16[512,256]{1,0:T(8,128)(2,1)S(1)} %collective-permute-done.2.green), custom_call_target="tpu_custom_call" | custom-call | flops 134217728 | bytes 1572864 | tf_op jit(solution)/shard_map/contract/pallas_call | solution.py:47
  24.4 0.6 %collective-permute-start.9 = (bf16[528,256]{1,0:T(8,128)(2,1)S(1)}, bf16[528,256]{1,0:T(8,128)(2,1)S(1)}, u32[]{:S(2)}, u32[]{:S(2)}) collective-permute-start(bf16[528,256]{1,0:T(8,128)(2,1)S(1)} %contract.6), channel_id=1, source_target_pairs={{0,4},{1,21},{2,14},{3,31},{4,0},{5,17},{6,10},{7,27},{8,12},{9,29... | collective-permute-start | bytes 811016 | tf_op jit(solution)/shard_map/ppermute | solution.py:115
  25.0 0.9 %contract.7 = bf16[528,256]{1,0:T(8,128)(2,1)S(1)} custom-call(s32[1]{0:T(128)} %bitcast.7.panel, s32[2,4,2]{2,1,0:T(4,128)S(1)} %pad_add_fusion.listed, bf16[4,128,512]{2,1,0:T(8,128)(2,1)S(1)} %bitcast.17, bf16[4,128,512]{2,1,0:T(8,128)(2,1)S(1)} %collective-permute-done.1.sibling, bf16[512,256]{1,0:T(8,128)(2,1)S(1)} %collective-permute-done.6.green), custom_call_target="tpu_custom_call" | custom-call | flops 134217728 | bytes 1572864 | tf_op jit(solution)/shard_map/contract/pallas_call | solution.py:47
  25.9 0.7 %collective-permute-start.10 = (bf16[528,256]{1,0:T(8,128)(2,1)S(1)}, bf16[528,256]{1,0:T(8,128)(2,1)S(1)}, u32[]{:S(2)}, u32[]{:S(2)}) collective-permute-start(bf16[528,256]{1,0:T(8,128)(2,1)S(1)} %contract.7), channel_id=1, source_target_pairs={{0,0},{1,17},{2,10},{3,27},{4,4},{5,21},{6,14},{7,31},{8,8},{9,25}... | collective-permute-start | bytes 811016 | tf_op jit(solution)/shard_map/ppermute | solution.py:115
  26.6 0.0 collective-permute-done.7.green
  26.6 0.0 copy-start.2
  26.6 0.9 %contract.5 = bf16[528,256]{1,0:T(8,128)(2,1)S(1)} custom-call(s32[1]{0:T(128)} %bitcast.5.panel, s32[2,4,2]{2,1,0:T(4,128)S(1)} %pad_add_fusion.listed, bf16[4,128,512]{2,1,0:T(8,128)(2,1)S(1)} %bitcast.18, bf16[4,128,512]{2,1,0:T(8,128)(2,1)S(1)} %collective-permute-done.1.sibling, bf16[512,256]{1,0:T(8,128)(2,1)S(1)} %collective-permute-done.7.green), custom_call_target="tpu_custom_call" | custom-call | flops 134217728 | bytes 1572864 | tf_op jit(solution)/shard_map/contract/pallas_call | solution.py:47
  27.5 2.4 %collective-permute-start.8 = (bf16[528,256]{1,0:T(8,128)(2,1)S(1)}, bf16[528,256]{1,0:T(8,128)(2,1)S(1)}, u32[]{:S(2)}, u32[]{:S(2)}) collective-permute-start(bf16[528,256]{1,0:T(8,128)(2,1)S(1)} %contract.5), channel_id=1, source_target_pairs={{0,8},{1,25},{2,2},{3,19},{4,12},{5,29},{6,6},{7,23},{8,0},{9,17},... | collective-permute-start | bytes 811016 | tf_op jit(solution)/shard_map/ppermute | solution.py:115
  30.0 0.0 collective-permute-done.3.green
  30.0 0.0 copy-start.3
  30.0 0.7 %copy-done.3 = bf16[512,256]{1,0:T(8,128)(2,1)} copy-done((bf16[512,256]{1,0:T(8,128)(2,1)}, bf16[512,256]{1,0:T(8,128)(2,1)S(1)}, u32[]{:S(2)}) %copy-start.3) | copy-done | bytes 262168
  30.7 0.0 copy-done.2
  30.7 0.0 copy-start.4
  30.7 0.9 %copy-done.4 = bf16[512,256]{1,0:T(8,128)(2,1)S(1)} copy-done((bf16[512,256]{1,0:T(8,128)(2,1)S(1)}, bf16[512,256]{1,0:T(8,128)(2,1)}, u32[]{:S(2)}) %copy-start.4) | copy-done | bytes 262168
  31.6 0.9 %contract.4 = bf16[528,256]{1,0:T(8,128)(2,1)S(1)} custom-call(s32[1]{0:T(128)} %bitcast.panel, s32[2,4,2]{2,1,0:T(4,128)S(1)} %pad_add_fusion.listed, bf16[4,128,512]{2,1,0:T(8,128)(2,1)S(1)} %bitcast.19, bf16[4,128,512]{2,1,0:T(8,128)(2,1)S(1)} %collective-permute-done.1.sibling, bf16[512,256]{1,0:T(8,128)(2,1)S(1)} %copy-done.4), custom_call_target="tpu_custom_call" | custom-call | flops 134217728 | bytes 1572864 | tf_op jit(solution)/shard_map/contract/pallas_call | solution.py:47
  32.5 2.5 %collective-permute-start.4 = (bf16[528,256]{1,0:T(8,128)(2,1)S(1)}, bf16[528,256]{1,0:T(8,128)(2,1)S(1)}, u32[]{:S(2)}, u32[]{:S(2)}) collective-permute-start(bf16[528,256]{1,0:T(8,128)(2,1)S(1)} %contract.4), channel_id=1, source_target_pairs={{0,12},{1,29},{2,6},{3,23},{4,8},{5,25},{6,2},{7,19},{8,4},{9,21},... | collective-permute-start | bytes 811016 | tf_op jit(solution)/shard_map/ppermute | solution.py:115
  35.1 0.0 collective-permute-done.5.sibling
  35.1 0.0 collective-permute-done.10.message
  35.1 0.0 copy-done
  35.1 0.4 virtual_product.4.before
  35.5 0.0 collective-permute-done.9.message
  35.5 0.4 virtual_product.5.before
  35.9 3.8 %collective-permute-done.8.message = bf16[528,256]{1,0:T(8,128)(2,1)S(1)} collective-permute-done((bf16[528,256]{1,0:T(8,128)(2,1)S(1)}, bf16[528,256]{1,0:T(8,128)(2,1)S(1)}, u32[]{:S(2)}, u32[]{:S(2)}) %collective-permute-start.8) | collective-permute-done | bytes 270368 | tf_op jit(solution)/shard_map/ppermute | solution.py:115
  39.7 0.4 virtual_product.6.before
  40.1 6.0 %collective-permute-done.4.message = bf16[528,256]{1,0:T(8,128)(2,1)S(1)} collective-permute-done((bf16[528,256]{1,0:T(8,128)(2,1)S(1)}, bf16[528,256]{1,0:T(8,128)(2,1)S(1)}, u32[]{:S(2)}, u32[]{:S(2)}) %collective-permute-start.4) | collective-permute-done | bytes 270368 | tf_op jit(solution)/shard_map/ppermute | solution.py:115
  46.0 0.4 virtual_product.7
  46.4 0.1 collective-permute-start.11
  46.5 4.2 %collective-permute-done.11 = f32[64,256]{1,0:T(8,128)S(1)} collective-permute-done((f32[64,256]{1,0:T(8,128)S(1)}, f32[64,256]{1,0:T(8,128)S(1)}, u32[]{:S(2)}, u32[]{:S(2)}) %collective-permute-start.11) | collective-permute-done | bytes 65568 | tf_op jit(solution)/shard_map/ppermute | solution.py:115
  50.8 3.1 %collective-permute-start.12 = (f32[32,256]{1,0:T(8,128)S(1)}, f32[32,256]{1,0:T(8,128)S(1)}, u32[]{:S(2)}, u32[]{:S(2)}) collective-permute-start(f32[32,256]{1,0:T(8,128)S(1)} %slice_select_fusion.1), channel_id=1, source_target_pairs={{0,1},{1,0},{2,3},{3,2},{4,5},{5,4},{6,7},{7,6},{8,9},{9,8},{10,11... | collective-permute-start | bytes 98312 | tf_op jit(solution)/shard_map/ppermute | solution.py:115
  53.9 0.9 %collective-permute-done.12 = f32[32,256]{1,0:T(8,128)S(1)} collective-permute-done((f32[32,256]{1,0:T(8,128)S(1)}, f32[32,256]{1,0:T(8,128)S(1)}, u32[]{:S(2)}, u32[]{:S(2)}) %collective-permute-start.12) | collective-permute-done | bytes 32800 | tf_op jit(solution)/shard_map/ppermute | solution.py:115
  54.8 0.6 %add_bitcast_fusion = f32[1,32,256]{2,1,0:T(8,128)} fusion(f32[32,256]{1,0:T(8,128)S(1)} %collective-permute-done.12, f32[64,256]{1,0:T(8,128)S(1)} %select_add_fusion, pred[]{:T(512)S(6)} %eq.13), kind=kLoop, calls=%fused_computation.2 | loop fusion | flops 16384 | bytes 131073 | tf_op jit(solution)/shard_map/broadcast_in_dim | solution.py:151
  (6 shorter events, 0.0 us)
Async XLA Ops:
  0.0 21.0 %copy-start.5 = (s32[4,2]{0,1:T(2,128)S(1)}, s32[4,2]{0,1:T(2,128)}, u32[]{:S(2)}) copy-start(s32[4,2]{0,1:T(2,128)} %param.6) | copy-start | bytes 100
  0.0 22.5 %collective-permute-start.1 = (bf16[4,128,512]{2,1,0:T(8,128)(2,1)}, bf16[4,128,512]{2,1,0:T(8,128)(2,1)S(1)}, u32[]{:S(2)}, u32[]{:S(2)}) collective-permute-start(bf16[4,128,512]{2,1,0:T(8,128)(2,1)} %bitcast.15), channel_id=1, source_target_pairs={{0,1},{1,0},{2,3},{3,2},{4,5},{5,4},{6,7},{7,6},{8,9},{9,8},{10,11... | collective-permute-start | bytes 1572872 | tf_op jit(solution)/shard_map/ppermute | solution.py:115
  0.5 4.3 %collective-permute-start.6 = (bf16[512,256]{1,0:T(8,128)(2,1)}, bf16[512,256]{1,0:T(8,128)(2,1)S(1)}, u32[]{:S(2)}, u32[]{:S(2)}) collective-permute-start(bf16[512,256]{1,0:T(8,128)(2,1)} %param.5), channel_id=1, source_target_pairs={{0,0},{1,17},{2,10},{3,27},{4,4},{5,21},{6,14},{7,31},{8,8},{9,25}... | collective-permute-start | bytes 786440 | tf_op jit(solution)/shard_map/ppermute | solution.py:115
  2.1 11.8 %collective-permute-start.2 = (bf16[512,256]{1,0:T(8,128)(2,1)}, bf16[512,256]{1,0:T(8,128)(2,1)S(1)}, u32[]{:S(2)}, u32[]{:S(2)}) collective-permute-start(bf16[512,256]{1,0:T(8,128)(2,1)} %param.5), channel_id=1, source_target_pairs={{0,4},{1,21},{2,14},{3,31},{4,0},{5,17},{6,10},{7,27},{8,12},{9,29... | collective-permute-start | bytes 786440 | tf_op jit(solution)/shard_map/ppermute | solution.py:115
  4.7 21.9 %collective-permute-start.7 = (bf16[512,256]{1,0:T(8,128)(2,1)S(1)}, bf16[512,256]{1,0:T(8,128)(2,1)S(1)}, u32[]{:S(2)}, u32[]{:S(2)}) collective-permute-start(bf16[512,256]{1,0:T(8,128)(2,1)S(1)} %collective-permute-done.6.green), channel_id=1, source_target_pairs={{0,2},{1,3},{2,0},{3,1},{4,6},{5,7},{6,4},{7,5},{8,10},{9,11},{10,... | collective-permute-start | bytes 786440 | tf_op jit(solution)/shard_map/ppermute | solution.py:115
  13.8 16.2 %collective-permute-start.3 = (bf16[512,256]{1,0:T(8,128)(2,1)S(1)}, bf16[512,256]{1,0:T(8,128)(2,1)S(1)}, u32[]{:S(2)}, u32[]{:S(2)}) collective-permute-start(bf16[512,256]{1,0:T(8,128)(2,1)S(1)} %collective-permute-done.2.green), channel_id=1, source_target_pairs={{0,2},{1,3},{2,0},{3,1},{4,6},{5,7},{6,4},{7,5},{8,10},{9,11},{10,... | collective-permute-start | bytes 786440 | tf_op jit(solution)/shard_map/ppermute | solution.py:115
  20.4 14.7 %collective-permute-start.5 = (bf16[4,256,256]{2,1,0:T(8,128)(2,1)}, bf16[4,256,256]{2,1,0:T(8,128)(2,1)S(1)}, u32[]{:S(2)}, u32[]{:S(2)}) collective-permute-start(bf16[4,256,256]{2,1,0:T(8,128)(2,1)} %bitcast.10), channel_id=1, source_target_pairs={{0,1},{1,0},{2,3},{3,2},{4,5},{5,4},{6,7},{7,6},{8,9},{9,8},{10,11... | collective-permute-start | bytes 1572872 | tf_op jit(solution)/shard_map/ppermute | solution.py:115
  21.0 1.4 %collective-permute-start = (s32[4,2]{0,1:T(2,128)S(1)}, s32[4,2]{0,1:T(2,128)S(1)}, u32[]{:S(2)}, u32[]{:S(2)}) collective-permute-start(s32[4,2]{0,1:T(2,128)S(1)} %copy-done.5), channel_id=1, source_target_pairs={{0,1},{1,0},{2,3},{3,2},{4,5},{5,4},{6,7},{7,6},{8,9},{9,8},{10,11... | collective-permute-start | bytes 104 | tf_op jit(solution)/shard_map/ppermute | solution.py:115
  22.5 1.0 %copy-start.1 = (bf16[512,512]{1,0:T(8,128)(2,1)S(1)}, bf16[512,512]{1,0:T(8,128)(2,1)}, u32[]{:S(2)}) copy-start(bf16[512,512]{1,0:T(8,128)(2,1)} %param.4) | copy-start | bytes 1572868
  24.4 11.0 %collective-permute-start.9 = (bf16[528,256]{1,0:T(8,128)(2,1)S(1)}, bf16[528,256]{1,0:T(8,128)(2,1)S(1)}, u32[]{:S(2)}, u32[]{:S(2)}) collective-permute-start(bf16[528,256]{1,0:T(8,128)(2,1)S(1)} %contract.6), channel_id=1, source_target_pairs={{0,4},{1,21},{2,14},{3,31},{4,0},{5,17},{6,10},{7,27},{8,12},{9,29... | collective-permute-start | bytes 811016 | tf_op jit(solution)/shard_map/ppermute | solution.py:115
  25.9 9.2 %collective-permute-start.10 = (bf16[528,256]{1,0:T(8,128)(2,1)S(1)}, bf16[528,256]{1,0:T(8,128)(2,1)S(1)}, u32[]{:S(2)}, u32[]{:S(2)}) collective-permute-start(bf16[528,256]{1,0:T(8,128)(2,1)S(1)} %contract.7), channel_id=1, source_target_pairs={{0,0},{1,17},{2,10},{3,27},{4,4},{5,21},{6,14},{7,31},{8,8},{9,25}... | collective-permute-start | bytes 811016 | tf_op jit(solution)/shard_map/ppermute | solution.py:115
  26.6 4.1 %copy-start.2 = (bf16[512,512]{1,0:T(8,128)(2,1)S(1)}, bf16[512,512]{1,0:T(8,128)(2,1)}, u32[]{:S(2)}) copy-start(bf16[512,512]{1,0:T(8,128)(2,1)} %param.4) | copy-start | bytes 1572868
  27.5 12.2 %collective-permute-start.8 = (bf16[528,256]{1,0:T(8,128)(2,1)S(1)}, bf16[528,256]{1,0:T(8,128)(2,1)S(1)}, u32[]{:S(2)}, u32[]{:S(2)}) collective-permute-start(bf16[528,256]{1,0:T(8,128)(2,1)S(1)} %contract.5), channel_id=1, source_target_pairs={{0,8},{1,25},{2,2},{3,19},{4,12},{5,29},{6,6},{7,23},{8,0},{9,17},... | collective-permute-start | bytes 811016 | tf_op jit(solution)/shard_map/ppermute | solution.py:115
  30.0 0.7 %copy-start.3 = (bf16[512,256]{1,0:T(8,128)(2,1)}, bf16[512,256]{1,0:T(8,128)(2,1)S(1)}, u32[]{:S(2)}) copy-start(bf16[512,256]{1,0:T(8,128)(2,1)S(1)} %collective-permute-done.3.green) | copy-start | bytes 786436
  30.7 1.0 %copy-start.4 = (bf16[512,256]{1,0:T(8,128)(2,1)S(1)}, bf16[512,256]{1,0:T(8,128)(2,1)}, u32[]{:S(2)}) copy-start(bf16[512,256]{1,0:T(8,128)(2,1)} %copy-done.3) | copy-start | bytes 786436
  31.6 3.4 %copy-start = (bf16[1,4,256,256]{3,2,1,0:T(8,128)(2,1)S(1)}, bf16[1,4,256,256]{3,2,1,0:T(8,128)(2,1)}, u32[]{:S(2)}) copy-start(bf16[1,4,256,256]{3,2,1,0:T(8,128)(2,1)} %param.7) | copy-start | bytes 1572868
  32.5 13.5 %collective-permute-start.4 = (bf16[528,256]{1,0:T(8,128)(2,1)S(1)}, bf16[528,256]{1,0:T(8,128)(2,1)S(1)}, u32[]{:S(2)}, u32[]{:S(2)}) collective-permute-start(bf16[528,256]{1,0:T(8,128)(2,1)S(1)} %contract.4), channel_id=1, source_target_pairs={{0,12},{1,29},{2,6},{3,23},{4,8},{5,25},{6,2},{7,19},{8,4},{9,21},... | collective-permute-start | bytes 811016 | tf_op jit(solution)/shard_map/ppermute | solution.py:115
  46.4 4.3 %collective-permute-start.11 = (f32[64,256]{1,0:T(8,128)S(1)}, f32[64,256]{1,0:T(8,128)S(1)}, u32[]{:S(2)}, u32[]{:S(2)}) collective-permute-start(f32[64,256]{1,0:T(8,128)S(1)} %slice_select_fusion), channel_id=1, source_target_pairs={{0,2},{1,3},{2,0},{3,1},{4,6},{5,7},{6,4},{7,5},{8,10},{9,11},{10,... | collective-permute-start | bytes 196616 | tf_op jit(solution)/shard_map/ppermute | solution.py:115
  50.8 4.0 %collective-permute-start.12 = (f32[32,256]{1,0:T(8,128)S(1)}, f32[32,256]{1,0:T(8,128)S(1)}, u32[]{:S(2)}, u32[]{:S(2)}) collective-permute-start(f32[32,256]{1,0:T(8,128)S(1)} %slice_select_fusion.1), channel_id=1, source_target_pairs={{0,1},{1,0},{2,3},{3,2},{4,5},{5,4},{6,7},{7,6},{8,9},{9,8},{10,11... | collective-permute-start | bytes 98312 | tf_op jit(solution)/shard_map/ppermute | solution.py:115

commit v3 on v0

v3 whole, which is shorter than its diff:
```python
import jax
import jax.numpy as jnp
from jax import lax
from jax.experimental import pallas as pl
from jax.experimental.pallas import tpu as pltpu
from jax.sharding import PartitionSpec as P

AXES = ("grid", "rep")
KERNEL_VMEM = 16 << 20
SQUARE = 4
CHUNK = 2
VMEM = pl.BlockSpec(memory_space=pltpu.VMEM)
SMEM = pl.BlockSpec(memory_space=pltpu.SMEM)


def sources_of(own, first, second, corner_head, corner_tail, rows):
    labels = own.shape[0] - CHUNK * rows
    places = []
    for array in (own, first, second):
        tiles = [array[labels + n * rows : labels + (n + 1) * rows, :] for n in range(CHUNK)]
        places.append((array[:labels, :], tiles))
    places.append((corner_head[:labels, :], [corner_head[labels:, :], corner_tail[...]]))
    return places


def masked_products(panel, places, green, picks):
    width = green.shape[1]
    wanted = panel.astype(jnp.float32)
    products = []
    for labels, tiles in places:
        named = (labels[:, :width].astype(jnp.float32) == wanted).astype(jnp.float32)
        line = []
        for n, tile in enumerate(tiles):
            hit = jnp.max(named[n * picks : (n + 1) * picks], axis=0, keepdims=True)
            product = jnp.dot(tile, green, preferred_element_type=jnp.float32)
            line.append((product * hit).astype(jnp.bfloat16))
        products.append(line)
    return products


def far_kernel(picks, panel, part, own, first, second, corner_head, corner_tail, kept, swapped, message, green):
    rows, half = message.shape[0] // CHUNK, kept.shape[0]
    green[pl.ds(part[0] * half, half), :] = kept[...]
    green[pl.ds((1 - part[0]) * half, half), :] = swapped[...]
    places = sources_of(own, first, second, corner_head, corner_tail, rows)
    products = masked_products(panel[0], places, green[...], picks)
    for n in range(CHUNK):
        total = sum(line[n].astype(jnp.float32) for line in products)
        message[n * rows : (n + 1) * rows, :] = total.astype(message.dtype)


def near_kernel(picks, panel, own, first, second, corner_head, corner_tail, green, virtual, before, total):
    rows = before.shape[0]
    places = sources_of(own, first, second, corner_head, corner_tail, rows)
    products = masked_products(panel[0], places, green[...], picks)
    result = before[...]
    for n in range(CHUNK):
        for line in products:
            result = result + jnp.dot(line[n], virtual[n], preferred_element_type=jnp.float32)
    total[...] = result


def virtual_kernel(message, virtual, before, total):
    rows = before.shape[0]
    result = before[...]
    for n in range(CHUNK):
        result = result + jnp.dot(
            message[n * rows : (n + 1) * rows, :], virtual[n], preferred_element_type=jnp.float32
        )
    total[...] = result


def call(kernel, name, out, specs, flops, scratch=()):
    def run(*operands):
        moved = sum(operand.size * operand.dtype.itemsize for operand in operands)
        return pl.pallas_call(
            kernel,
            out_shape=out,
            in_specs=specs,
            out_specs=VMEM,
            scratch_shapes=scratch,
            cost_estimate=pl.CostEstimate(flops=flops, bytes_accessed=moved, transcendentals=0),
            compiler_params=pltpu.CompilerParams(vmem_limit_bytes=KERNEL_VMEM),
            name=name,
        )(*operands)

    return run


def shards(integrals, green_occ, tile_panels, virtual_blocks):
    grid_count, rep_count = lax.axis_size("grid"), lax.axis_size("rep")
    tile_count, picks = tile_panels.shape
    rows, depth = integrals.shape[0] // tile_count, integrals.shape[1]
    width, columns = virtual_blocks.shape[-2:]
    place, rep = lax.axis_index("grid"), lax.axis_index("rep")

    def send(array, grid_bits, rep_bits=0):
        order = []
        for g in range(grid_count):
            for r in range(rep_count):
                order.append((g * rep_count + r, (g ^ grid_bits) * rep_count + (r ^ rep_bits)))
        return lax.ppermute(array, AXES, order)

    def scalar(value):
        return value.astype(jnp.int32).reshape(1)

    label_rows = -(-CHUNK * picks // 16) * 16
    chunks = range(tile_count // CHUNK)
    own, first, second = [], [], []
    part = rep % 2
    half = green_occ.shape[0] // 2
    mine = lax.dynamic_slice_in_dim(green_occ, part * half, half, 0)
    kept = {}
    for n in chunks:
        named = tile_panels[n * CHUNK : (n + 1) * CHUNK].reshape(CHUNK * picks, 1).astype(jnp.bfloat16)
        named = jnp.pad(named, ((0, label_rows - CHUNK * picks), (0, 0)), constant_values=-1)
        tiles = integrals[n * CHUNK * rows : (n + 1) * CHUNK * rows]
        own.append(jnp.concatenate([jnp.broadcast_to(named, (label_rows, depth)), tiles], axis=0))
        first.append(send(own[n], 1))
        second.append(send(own[n], 2))
        if n == 0:
            for far in range(SQUARE, grid_count, SQUARE):
                kept[far] = send(mine, far)
    swapped = {far: send(array, 0, 1) for far, array in kept.items()}

    cut = label_rows + rows
    heads = [send(first[n][:cut], 2) for n in chunks]
    tails = [send(second[n][cut:], 1) for n in chunks]
    square = [(own[n], first[n], second[n], heads[n], tails[n]) for n in chunks]

    tile_flops = 2 * rows * depth * width
    messages = []
    for n in chunks:
        for far in kept:
            contract = call(
                lambda *refs: far_kernel(picks, *refs),
                "far_panel",
                jax.ShapeDtypeStruct((CHUNK * rows, width), jnp.bfloat16),
                [SMEM, SMEM] + [VMEM] * 7,
                SQUARE * CHUNK * tile_flops,
                [pltpu.VMEM((depth, width), jnp.bfloat16)],
            )
            message = contract(scalar(place ^ far), scalar(part), *square[n], kept[far], swapped[far])
            messages.append((n, send(message, far)))

    sums = jax.ShapeDtypeStruct((rows, columns), jnp.float32)
    total = jnp.zeros(sums.shape, sums.dtype)
    blocks = [virtual_blocks[0, n * CHUNK : (n + 1) * CHUNK] for n in chunks]
    for n in chunks:
        near = call(
            lambda *refs: near_kernel(picks, *refs),
            "own_panel",
            sums,
            [SMEM] + [VMEM] * 8,
            SQUARE * CHUNK * (tile_flops + 2 * rows * width * columns),
        )
        total = near(scalar(place), *square[n], green_occ, blocks[n], total)
    for n, message in messages:
        product = call(virtual_kernel, "virtual_product", sums, [VMEM] * 3, 2 * CHUNK * rows * width * columns)
        total = product(message, blocks[n], total)

    step = rep_count // 2
    while step:
        middle = total.shape[0] // 2
        low, high = total[:middle], total[middle:]
        upper = (rep // step) % 2 == 1
        stays, leaves = jnp.where(upper, high, low), jnp.where(upper, low, high)
        total = stays + send(leaves, 0, step)
        step //= 2
    return total[None]


def solution(mesh):
    in_specs = (
        P(("grid", "rep"), None),
        P(None, "grid"),
        P(("grid", "rep"), None),
        P("grid", "rep", None, None),
    )
    out_specs = P("grid", "rep", None)
    return jax.shard_map(shards, mesh=mesh, in_specs=in_specs, out_specs=out_specs, check_vma=False)
```

time: 127 us -> 50.4 us (0.40)
  waiting for transfers between devices: 91.9 us -> 21.2 us
  between operations: 13.4 us -> 0.2 us
  starting transfers between devices: 11 us -> 23.3 us
  matrix products: 8.44 us -> 0 us
  Pallas kernels: 0 us -> 2.74 us
    all_gather x1 -> x0, waiting for transfers between devices: 47 us -> none  [shards(): lax.all_gather(green_occ, 'grid', axis=1, tiled=True)]
    all_to_all x2 -> x0, waiting for transfers between devices: 25.4 us -> none  [the longest x1 25.4 us: shards(): lax.all_to_all(outgoing, 'grid', split_axis=0, concat_axis=0, tiled=True)]
    ppermute x0 -> x14, starting transfers between devices: none -> 23.3 us  [send(): return lax.ppermute(array, AXES, order)]
    ppermute x0 -> x14, waiting for transfers between devices: none -> 21.2 us  [send(): return lax.ppermute(array, AXES, order)]
    reduce_scatter x1 -> x0, waiting for transfers between devices: 18.8 us -> none  [shards(): lax.psum_scatter(owner_part[None], 'rep', scatter_dimension=1, tiled=True)]
    all_to_all x2 -> x0, starting transfers between devices: 11 us -> none  [the longest x1 7.28 us: shards(): lax.all_to_all(labels, 'grid', split_axis=0, concat_axis=0, tiled=True)]
    dot_general x4 -> x0, matrix products: 8.44 us -> none  [the longest x1 3.75 us: shards(): jnp.einsum('ldc,ltdw->dctw', place_weights, tile_blocks, preferred_elemen...]
    pallas_call x0 -> x6, Pallas kernels: none -> 2.74 us  [run(): pl.pallas_call(kernel, out_shape=out, in_specs=specs, out_specs=VMEM, scr...]
  transfers between devices with their start and end apart: 4 -> 14, of which waited for: 3 -> 7; matrix products, arithmetic and copies ran while one was open for 7% -> 1% of each run, Pallas kernels for 0% -> 5%
where the time goes in v3:
time: 50.4 us; the launch traced here: 50.2 us
  starting transfers between devices  23.3 us (46%)
  waiting for transfers between devices  21.2 us (42%)
  Pallas kernels  2.74 us (5%)
  local copies, waits for them, and re-layouts  1.91 us (4%)
  other arithmetic  0.88 us (2%)
    ppermute x14, starting transfers between devices, send(): return lax.ppermute(array, AXES, order)  23.3 us
    ppermute x14, waiting for transfers between devices, send(): return lax.ppermute(array, AXES, order)  21.2 us
    pallas_call x6, Pallas kernels, run(): pl.pallas_call(kernel, out_shape=out, in_specs=specs, out_specs=VMEM, scr...  2.74 us
    slice x1, local copies, waits for them, and re-layouts, shards(): tiles = integrals[n * CHUNK * rows:(n + 1) * CHUNK * rows]  1.08 us
  transfers between devices with their start and end apart: 14, of which 7 were waited for; matrix products, arithmetic and copies ran while one was open for 1% of the time, Pallas kernels for 5%

profile of v3, /device:TPU:0, one launch (start us, length us, event | category | flops | bytes accessed | tf_op | source)
XLA Modules:
  0.0 50.2 jit_solution(15993133712013632865)
XLA Ops:
  0.0 0.0 copy-start.2
  0.0 1.1 %fusion = (bf16[256,512]{1,0:T(8,128)(2,1)S(1)}, bf16[256,512]{1,0:T(8,128)(2,1)S(1)}) fusion(bf16[512,512]{1,0:T(8,128)(2,1)} %param.4), kind=kLoop, calls=%fused_computation.11 | loop fusion | bytes 1048576 | tf_op jit(solution)/shard_map/slice | solution.py:117
  1.1 0.0 copy-done.2
  1.1 0.1 fusion.1
  1.2 0.1 copy.6
  1.3 0.1 convert_element_type.28
  1.4 0.1 pad_maximum_fusion.1.refs_2_.refs_1_
  1.5 3.0 %collective-permute-start.7 = (bf16[272,512]{1,0:T(8,128)(2,1)S(1)}, bf16[272,512]{1,0:T(8,128)(2,1)S(1)}, u32[]{:S(2)}, u32[]{:S(2)}) collective-permute-start(bf16[272,512]{1,0:T(8,128)(2,1)S(1)} %pad_maximum_fusion.1.refs_2_.refs_1_), channel_id=1, source_target_pairs={{0,4},{1,5},{2,6},{3,7},{4,0},{5,1},{6,2},{7,3},{8,12},{9,13},{10,... | collective-permute-start | bytes 835592 | tf_op jit(solution)/shard_map/ppermute | solution.py:102
  4.5 1.6 %collective-permute-start.8 = (bf16[272,512]{1,0:T(8,128)(2,1)S(1)}, bf16[272,512]{1,0:T(8,128)(2,1)S(1)}, u32[]{:S(2)}, u32[]{:S(2)}) collective-permute-start(bf16[272,512]{1,0:T(8,128)(2,1)S(1)} %pad_maximum_fusion.1.refs_2_.refs_1_), channel_id=1, source_target_pairs={{0,8},{1,9},{2,10},{3,11},{4,12},{5,13},{6,14},{7,15},{8,0},{9,1},... | collective-permute-start | bytes 835592 | tf_op jit(solution)/shard_map/ppermute | solution.py:102
  6.1 0.1 copy.5
  6.2 0.1 convert_element_type.27
  6.3 0.1 pad_maximum_fusion.refs_2_.refs_1_
  6.5 0.6 %collective-permute-start = (bf16[272,512]{1,0:T(8,128)(2,1)S(1)}, bf16[272,512]{1,0:T(8,128)(2,1)S(1)}, u32[]{:S(2)}, u32[]{:S(2)}) collective-permute-start(bf16[272,512]{1,0:T(8,128)(2,1)S(1)} %pad_maximum_fusion.refs_2_.refs_1_), channel_id=1, source_target_pairs={{0,4},{1,5},{2,6},{3,7},{4,0},{5,1},{6,2},{7,3},{8,12},{9,13},{10,... | collective-permute-start | bytes 835592 | tf_op jit(solution)/shard_map/ppermute | solution.py:102
  7.0 0.0 collective-permute-start.1
  7.0 0.2 copy-done
  7.3 2.9 %collective-permute-start.4 = (bf16[256,256]{1,0:T(8,128)(2,1)S(1)}, bf16[256,256]{1,0:T(8,128)(2,1)S(1)}, u32[]{:S(2)}, u32[]{:S(2)}) collective-permute-start(bf16[256,256]{1,0:T(8,128)(2,1)S(1)} %constant_dynamic-slice_fusion), channel_id=1, source_target_pairs={{0,16},{1,17},{2,18},{3,19},{4,20},{5,21},{6,22},{7,23},{8,24},{9,... | collective-permute-start | bytes 393224 | tf_op jit(solution)/shard_map/ppermute | solution.py:102
  10.1 1.9 %collective-permute-done.7.refs_3_.refs_2_ = bf16[272,512]{1,0:T(8,128)(2,1)S(1)} collective-permute-done((bf16[272,512]{1,0:T(8,128)(2,1)S(1)}, bf16[272,512]{1,0:T(8,128)(2,1)S(1)}, u32[]{:S(2)}, u32[]{:S(2)}) %collective-permute-start.7) | collective-permute-done | bytes 278560 | tf_op jit(solution)/shard_map/ppermute | solution.py:102
  12.0 2.2 %collective-permute-start.9 = (bf16[144,512]{1,0:T(8,128)(2,1)S(1)}, bf16[144,512]{1,0:T(8,128)(2,1)S(1)}, u32[]{:S(2)}, u32[]{:S(2)}) collective-permute-start(bf16[144,512]{1,0:T(8,128)(2,1)S(1)} %slice.60), channel_id=1, source_target_pairs={{0,8},{1,9},{2,10},{3,11},{4,12},{5,13},{6,14},{7,15},{8,0},{9,1},... | collective-permute-start | bytes 442376 | tf_op jit(solution)/shard_map/ppermute | solution.py:102
  14.2 7.8 %collective-permute-done.4.refs_7_ = bf16[256,256]{1,0:T(8,128)(2,1)S(1)} collective-permute-done((bf16[256,256]{1,0:T(8,128)(2,1)S(1)}, bf16[256,256]{1,0:T(8,128)(2,1)S(1)}, u32[]{:S(2)}, u32[]{:S(2)}) %collective-permute-start.4) | collective-permute-done | bytes 131104 | tf_op jit(solution)/shard_map/ppermute | solution.py:102
  22.0 0.0 collective-permute-start.5
  22.0 0.0 collective-permute-done.8.refs_4_.refs_3_
  22.0 0.6 %collective-permute-start.10 = (bf16[128,512]{1,0:T(8,128)(2,1)S(1)}, bf16[128,512]{1,0:T(8,128)(2,1)S(1)}, u32[]{:S(2)}, u32[]{:S(2)}) collective-permute-start(bf16[128,512]{1,0:T(8,128)(2,1)S(1)} %slice.61), channel_id=1, source_target_pairs={{0,4},{1,5},{2,6},{3,7},{4,0},{5,1},{6,2},{7,3},{8,12},{9,13},{10,... | collective-permute-start | bytes 393224 | tf_op jit(solution)/shard_map/ppermute | solution.py:102
  22.6 0.0 collective-permute-done.refs_3_.refs_2_
  22.6 3.6 %collective-permute-start.2 = (bf16[144,512]{1,0:T(8,128)(2,1)S(1)}, bf16[144,512]{1,0:T(8,128)(2,1)S(1)}, u32[]{:S(2)}, u32[]{:S(2)}) collective-permute-start(bf16[144,512]{1,0:T(8,128)(2,1)S(1)} %slice.58), channel_id=1, source_target_pairs={{0,8},{1,9},{2,10},{3,11},{4,12},{5,13},{6,14},{7,15},{8,0},{9,1},... | collective-permute-start | bytes 442376 | tf_op jit(solution)/shard_map/ppermute | solution.py:102
  26.2 0.0 collective-permute-done.1.refs_4_.refs_3_
  26.2 1.6 %collective-permute-start.3 = (bf16[128,512]{1,0:T(8,128)(2,1)S(1)}, bf16[128,512]{1,0:T(8,128)(2,1)S(1)}, u32[]{:S(2)}, u32[]{:S(2)}) collective-permute-start(bf16[128,512]{1,0:T(8,128)(2,1)S(1)} %slice.59), channel_id=1, source_target_pairs={{0,4},{1,5},{2,6},{3,7},{4,0},{5,1},{6,2},{7,3},{8,12},{9,13},{10,... | collective-permute-start | bytes 393224 | tf_op jit(solution)/shard_map/ppermute | solution.py:102
  27.8 0.0 collective-permute-done.5.refs_8_
  27.8 0.2 collective-permute-done.10.refs_6_.refs_5_
  28.0 0.0 collective-permute-done.9.refs_5_.refs_4_
  28.0 0.5 far_panel.3
  28.5 0.0 copy-start.1
  28.5 3.8 %collective-permute-start.11 = (bf16[256,256]{1,0:T(8,128)(2,1)S(1)}, bf16[256,256]{1,0:T(8,128)(2,1)S(1)}, u32[]{:S(2)}, u32[]{:S(2)}) collective-permute-start(bf16[256,256]{1,0:T(8,128)(2,1)S(1)} %far_panel.3), channel_id=1, source_target_pairs={{0,16},{1,17},{2,18},{3,19},{4,20},{5,21},{6,22},{7,23},{8,24},{9,... | collective-permute-start | bytes 393224 | tf_op jit(solution)/shard_map/ppermute | solution.py:102
  32.3 0.0 collective-permute-done.3.refs_6_.refs_5_
  32.3 0.0 collective-permute-done.2.refs_5_.refs_4_
  32.3 0.5 far_panel.2
  32.8 1.9 %collective-permute-start.6 = (bf16[256,256]{1,0:T(8,128)(2,1)S(1)}, bf16[256,256]{1,0:T(8,128)(2,1)S(1)}, u32[]{:S(2)}, u32[]{:S(2)}) collective-permute-start(bf16[256,256]{1,0:T(8,128)(2,1)S(1)} %far_panel.2), channel_id=1, source_target_pairs={{0,16},{1,17},{2,18},{3,19},{4,20},{5,21},{6,22},{7,23},{8,24},{9,... | collective-permute-start | bytes 393224 | tf_op jit(solution)/shard_map/ppermute | solution.py:102
  34.7 0.0 copy-done.1
  34.8 0.7 %own_panel.2.refs_8_ = f32[128,256]{1,0:T(8,128)S(1)} custom-call(s32[1]{0:T(128)} %bitcast.6.refs_0_, bf16[272,512]{1,0:T(8,128)(2,1)S(1)} %pad_maximum_fusion.1.refs_2_.refs_1_, bf16[272,512]{1,0:T(8,128)(2,1)S(1)} %collective-permute-done.7.refs_3_.refs_2_, bf16[272,512]{1,0:T(8,128)(2,1)S(1)} %collective-permute-done.8.refs_4_.refs_3_, ...), custom_call_target="tpu_custom_call" | custom-call | flops 402653184 | bytes 1769476 | tf_op jit(solution)/shard_map/own_panel/pallas_call | solution.py:76
  35.5 0.7 %own_panel.3.before = f32[128,256]{1,0:T(8,128)S(1)} custom-call(s32[1]{0:T(128)} %bitcast.6.refs_0_, bf16[272,512]{1,0:T(8,128)(2,1)S(1)} %pad_maximum_fusion.refs_2_.refs_1_, bf16[272,512]{1,0:T(8,128)(2,1)S(1)} %collective-permute-done.refs_3_.refs_2_, bf16[272,512]{1,0:T(8,128)(2,1)S(1)} %collective-permute-done.1.refs_4_.refs_3_, ...), custom_call_target="tpu_custom_call" | custom-call | flops 402653184 | bytes 1769476 | tf_op jit(solution)/shard_map/own_panel/pallas_call | solution.py:76
  36.2 5.1 %collective-permute-done.11.message = bf16[256,256]{1,0:T(8,128)(2,1)S(1)} collective-permute-done((bf16[256,256]{1,0:T(8,128)(2,1)S(1)}, bf16[256,256]{1,0:T(8,128)(2,1)S(1)}, u32[]{:S(2)}, u32[]{:S(2)}) %collective-permute-start.11) | collective-permute-done | bytes 131104 | tf_op jit(solution)/shard_map/ppermute | solution.py:102
  41.4 0.2 virtual_product.2.before
  41.6 2.2 %collective-permute-done.6.message = bf16[256,256]{1,0:T(8,128)(2,1)S(1)} collective-permute-done((bf16[256,256]{1,0:T(8,128)(2,1)S(1)}, bf16[256,256]{1,0:T(8,128)(2,1)S(1)}, u32[]{:S(2)}, u32[]{:S(2)}) %collective-permute-start.6) | collective-permute-done | bytes 131104 | tf_op jit(solution)/shard_map/ppermute | solution.py:102
  43.7 0.2 virtual_product.3
  44.0 1.6 %collective-permute-start.12 = (f32[64,256]{1,0:T(8,128)S(1)}, f32[64,256]{1,0:T(8,128)S(1)}, u32[]{:S(2)}, u32[]{:S(2)}) collective-permute-start(f32[64,256]{1,0:T(8,128)S(1)} %slice_select_fusion), channel_id=1, source_target_pairs={{0,2},{1,3},{2,0},{3,1},{4,6},{5,7},{6,4},{7,5},{8,10},{9,11},{10,... | collective-permute-start | bytes 196616 | tf_op jit(solution)/shard_map/ppermute | solution.py:102
  45.5 2.8 %collective-permute-done.12 = f32[64,256]{1,0:T(8,128)S(1)} collective-permute-done((f32[64,256]{1,0:T(8,128)S(1)}, f32[64,256]{1,0:T(8,128)S(1)}, u32[]{:S(2)}, u32[]{:S(2)}) %collective-permute-start.12) | collective-permute-done | bytes 65568 | tf_op jit(solution)/shard_map/ppermute | solution.py:102
  48.3 0.1 collective-permute-start.13
  48.4 1.2 %collective-permute-done.13 = f32[32,256]{1,0:T(8,128)S(1)} collective-permute-done((f32[32,256]{1,0:T(8,128)S(1)}, f32[32,256]{1,0:T(8,128)S(1)}, u32[]{:S(2)}, u32[]{:S(2)}) %collective-permute-start.13) | collective-permute-done | bytes 32800 | tf_op jit(solution)/shard_map/ppermute | solution.py:102
  49.6 0.6 %add_bitcast_fusion = f32[1,32,256]{2,1,0:T(8,128)} fusion(f32[32,256]{1,0:T(8,128)S(1)} %collective-permute-done.13, f32[64,256]{1,0:T(8,128)S(1)} %select_add_fusion, pred[]{:T(512)S(6)} %eq.10), kind=kLoop, calls=%fused_computation.6 | loop fusion | flops 16384 | bytes 131073 | tf_op jit(solution)/shard_map/broadcast_in_dim | solution.py:170
  (16 shorter events, 0.2 us)
Async XLA Ops:
  0.0 1.1 %copy-start.2 = (s32[4,2]{0,1:T(2,128)S(1)}, s32[4,2]{0,1:T(2,128)}, u32[]{:S(2)}) copy-start(s32[4,2]{0,1:T(2,128)} %param.6) | copy-start | bytes 100
  1.5 10.5 %collective-permute-start.7 = (bf16[272,512]{1,0:T(8,128)(2,1)S(1)}, bf16[272,512]{1,0:T(8,128)(2,1)S(1)}, u32[]{:S(2)}, u32[]{:S(2)}) collective-permute-start(bf16[272,512]{1,0:T(8,128)(2,1)S(1)} %pad_maximum_fusion.1.refs_2_.refs_1_), channel_id=1, source_target_pairs={{0,4},{1,5},{2,6},{3,7},{4,0},{5,1},{6,2},{7,3},{8,12},{9,13},{10,... | collective-permute-start | bytes 835592 | tf_op jit(solution)/shard_map/ppermute | solution.py:102
  4.5 17.5 %collective-permute-start.8 = (bf16[272,512]{1,0:T(8,128)(2,1)S(1)}, bf16[272,512]{1,0:T(8,128)(2,1)S(1)}, u32[]{:S(2)}, u32[]{:S(2)}) collective-permute-start(bf16[272,512]{1,0:T(8,128)(2,1)S(1)} %pad_maximum_fusion.1.refs_2_.refs_1_), channel_id=1, source_target_pairs={{0,8},{1,9},{2,10},{3,11},{4,12},{5,13},{6,14},{7,15},{8,0},{9,1},... | collective-permute-start | bytes 835592 | tf_op jit(solution)/shard_map/ppermute | solution.py:102
  6.3 0.9 %copy-start = (bf16[512,256]{1,0:T(8,128)(2,1)S(1)}, bf16[512,256]{1,0:T(8,128)(2,1)}, u32[]{:S(2)}) copy-start(bf16[512,256]{1,0:T(8,128)(2,1)} %refs_6_.3) | copy-start | bytes 786436
  6.5 16.1 %collective-permute-start = (bf16[272,512]{1,0:T(8,128)(2,1)S(1)}, bf16[272,512]{1,0:T(8,128)(2,1)S(1)}, u32[]{:S(2)}, u32[]{:S(2)}) collective-permute-start(bf16[272,512]{1,0:T(8,128)(2,1)S(1)} %pad_maximum_fusion.refs_2_.refs_1_), channel_id=1, source_target_pairs={{0,4},{1,5},{2,6},{3,7},{4,0},{5,1},{6,2},{7,3},{8,12},{9,13},{10,... | collective-permute-start | bytes 835592 | tf_op jit(solution)/shard_map/ppermute | solution.py:102
  7.0 19.1 %collective-permute-start.1 = (bf16[272,512]{1,0:T(8,128)(2,1)S(1)}, bf16[272,512]{1,0:T(8,128)(2,1)S(1)}, u32[]{:S(2)}, u32[]{:S(2)}) collective-permute-start(bf16[272,512]{1,0:T(8,128)(2,1)S(1)} %pad_maximum_fusion.refs_2_.refs_1_), channel_id=1, source_target_pairs={{0,8},{1,9},{2,10},{3,11},{4,12},{5,13},{6,14},{7,15},{8,0},{9,1},... | collective-permute-start | bytes 835592 | tf_op jit(solution)/shard_map/ppermute | solution.py:102
  7.3 14.7 %collective-permute-start.4 = (bf16[256,256]{1,0:T(8,128)(2,1)S(1)}, bf16[256,256]{1,0:T(8,128)(2,1)S(1)}, u32[]{:S(2)}, u32[]{:S(2)}) collective-permute-start(bf16[256,256]{1,0:T(8,128)(2,1)S(1)} %constant_dynamic-slice_fusion), channel_id=1, source_target_pairs={{0,16},{1,17},{2,18},{3,19},{4,20},{5,21},{6,22},{7,23},{8,24},{9,... | collective-permute-start | bytes 393224 | tf_op jit(solution)/shard_map/ppermute | solution.py:102
  12.0 16.0 %collective-permute-start.9 = (bf16[144,512]{1,0:T(8,128)(2,1)S(1)}, bf16[144,512]{1,0:T(8,128)(2,1)S(1)}, u32[]{:S(2)}, u32[]{:S(2)}) collective-permute-start(bf16[144,512]{1,0:T(8,128)(2,1)S(1)} %slice.60), channel_id=1, source_target_pairs={{0,8},{1,9},{2,10},{3,11},{4,12},{5,13},{6,14},{7,15},{8,0},{9,1},... | collective-permute-start | bytes 442376 | tf_op jit(solution)/shard_map/ppermute | solution.py:102
  22.0 5.8 %collective-permute-start.5 = (bf16[256,256]{1,0:T(8,128)(2,1)S(1)}, bf16[256,256]{1,0:T(8,128)(2,1)S(1)}, u32[]{:S(2)}, u32[]{:S(2)}) collective-permute-start(bf16[256,256]{1,0:T(8,128)(2,1)S(1)} %collective-permute-done.4.refs_7_), channel_id=1, source_target_pairs={{0,1},{1,0},{2,3},{3,2},{4,5},{5,4},{6,7},{7,6},{8,9},{9,8},{10,11... | collective-permute-start | bytes 393224 | tf_op jit(solution)/shard_map/ppermute | solution.py:102
  22.0 6.0 %collective-permute-start.10 = (bf16[128,512]{1,0:T(8,128)(2,1)S(1)}, bf16[128,512]{1,0:T(8,128)(2,1)S(1)}, u32[]{:S(2)}, u32[]{:S(2)}) collective-permute-start(bf16[128,512]{1,0:T(8,128)(2,1)S(1)} %slice.61), channel_id=1, source_target_pairs={{0,4},{1,5},{2,6},{3,7},{4,0},{5,1},{6,2},{7,3},{8,12},{9,13},{10,... | collective-permute-start | bytes 393224 | tf_op jit(solution)/shard_map/ppermute | solution.py:102
  22.6 9.7 %collective-permute-start.2 = (bf16[144,512]{1,0:T(8,128)(2,1)S(1)}, bf16[144,512]{1,0:T(8,128)(2,1)S(1)}, u32[]{:S(2)}, u32[]{:S(2)}) collective-permute-start(bf16[144,512]{1,0:T(8,128)(2,1)S(1)} %slice.58), channel_id=1, source_target_pairs={{0,8},{1,9},{2,10},{3,11},{4,12},{5,13},{6,14},{7,15},{8,0},{9,1},... | collective-permute-start | bytes 442376 | tf_op jit(solution)/shard_map/ppermute | solution.py:102
  26.2 6.1 %collective-permute-start.3 = (bf16[128,512]{1,0:T(8,128)(2,1)S(1)}, bf16[128,512]{1,0:T(8,128)(2,1)S(1)}, u32[]{:S(2)}, u32[]{:S(2)}) collective-permute-start(bf16[128,512]{1,0:T(8,128)(2,1)S(1)} %slice.59), channel_id=1, source_target_pairs={{0,4},{1,5},{2,6},{3,7},{4,0},{5,1},{6,2},{7,3},{8,12},{9,13},{10,... | collective-permute-start | bytes 393224 | tf_op jit(solution)/shard_map/ppermute | solution.py:102
  28.5 6.3 %copy-start.1 = (bf16[1,4,256,256]{3,2,1,0:T(8,128)(2,1)S(1)}, bf16[1,4,256,256]{3,2,1,0:T(8,128)(2,1)}, u32[]{:S(2)}) copy-start(bf16[1,4,256,256]{3,2,1,0:T(8,128)(2,1)} %param.7) | copy-start | bytes 1572868
  28.5 12.9 %collective-permute-start.11 = (bf16[256,256]{1,0:T(8,128)(2,1)S(1)}, bf16[256,256]{1,0:T(8,128)(2,1)S(1)}, u32[]{:S(2)}, u32[]{:S(2)}) collective-permute-start(bf16[256,256]{1,0:T(8,128)(2,1)S(1)} %far_panel.3), channel_id=1, source_target_pairs={{0,16},{1,17},{2,18},{3,19},{4,20},{5,21},{6,22},{7,23},{8,24},{9,... | collective-permute-start | bytes 393224 | tf_op jit(solution)/shard_map/ppermute | solution.py:102
  32.8 10.9 %collective-permute-start.6 = (bf16[256,256]{1,0:T(8,128)(2,1)S(1)}, bf16[256,256]{1,0:T(8,128)(2,1)S(1)}, u32[]{:S(2)}, u32[]{:S(2)}) collective-permute-start(bf16[256,256]{1,0:T(8,128)(2,1)S(1)} %far_panel.2), channel_id=1, source_target_pairs={{0,16},{1,17},{2,18},{3,19},{4,20},{5,21},{6,22},{7,23},{8,24},{9,... | collective-permute-start | bytes 393224 | tf_op jit(solution)/shard_map/ppermute | solution.py:102
  44.0 4.3 %collective-permute-start.12 = (f32[64,256]{1,0:T(8,128)S(1)}, f32[64,256]{1,0:T(8,128)S(1)}, u32[]{:S(2)}, u32[]{:S(2)}) collective-permute-start(f32[64,256]{1,0:T(8,128)S(1)} %slice_select_fusion), channel_id=1, source_target_pairs={{0,2},{1,3},{2,0},{3,1},{4,6},{5,7},{6,4},{7,5},{8,10},{9,11},{10,... | collective-permute-start | bytes 196616 | tf_op jit(solution)/shard_map/ppermute | solution.py:102
  48.3 1.3 %collective-permute-start.13 = (f32[32,256]{1,0:T(8,128)S(1)}, f32[32,256]{1,0:T(8,128)S(1)}, u32[]{:S(2)}, u32[]{:S(2)}) collective-permute-start(f32[32,256]{1,0:T(8,128)S(1)} %slice_select_fusion.1), channel_id=1, source_target_pairs={{0,1},{1,0},{2,3},{3,2},{4,5},{5,4},{6,7},{7,6},{8,9},{9,8},{10,11... | collective-permute-start | bytes 98312 | tf_op jit(solution)/shard_map/ppermute | solution.py:102

commit v4 on v0

v4 whole, which is shorter than its diff:
```python
import jax
import jax.numpy as jnp
from jax import lax
from jax.experimental import pallas as pl
from jax.experimental.pallas import tpu as pltpu
from jax.sharding import PartitionSpec as P

AXES = ("grid", "rep")
KERNEL_VMEM = 16 << 20
PACK_VMEM = 56 << 20
SQUARE = 4
CHUNK = 2
VMEM = pl.BlockSpec(memory_space=pltpu.VMEM)
ANY = pl.BlockSpec(memory_space=pl.ANY)
HBM = pl.BlockSpec(memory_space=pltpu.HBM)


def position():
    rep = lax.axis_index("rep")
    return lax.axis_index("grid"), rep // 2, rep % 2


def pack_kernel(picks, listed, integrals, green, half_green, *rest):
    *messages, names, done = rest
    half = half_green.shape[0]
    tile_rows = integrals.shape[0] // len(messages)
    label_rows = messages[0].shape[0] - tile_rows
    start = pl.multiple_of(position()[2] * half, half)
    copies = [
        pltpu.make_async_copy(listed, names, done.at[0]),
        pltpu.make_async_copy(green.at[pl.ds(start, half), :], half_green, done.at[1]),
    ]
    for m, message in enumerate(messages):
        copies.append(
            pltpu.make_async_copy(
                integrals.at[m * tile_rows : (m + 1) * tile_rows, :],
                message.at[label_rows:, :],
                done.at[m + 2],
            )
        )
    for copy in copies:
        copy.start()
    copies[0].wait()
    line = lax.broadcasted_iota(jnp.int32, (label_rows, messages[0].shape[1]), 0)
    for m, message in enumerate(messages):
        value = jnp.full(line.shape, -1, jnp.int32)
        for n in range(CHUNK):
            for s in range(picks):
                tile = m * CHUNK + n
                value = jnp.where(line == n * picks + s, names[s : s + 1, tile : tile + 1], value)
        message[:label_rows, :] = value.astype(jnp.float32).astype(message.dtype)
    for copy in copies[1:]:
        copy.wait()


def join_kernel(own, *rest):
    *halves, panels = rest
    half = halves[0].shape[0]
    core = position()[2]
    panels[0] = own[...]
    for n in range(len(halves) // 2):
        for h, array in enumerate(halves[2 * n : 2 * n + 2]):
            start = pl.multiple_of((core ^ h) * half, half)
            panels[1 + n, pl.ds(start, half), :] = array[...]


def sums_kernel(picks, fars, own, first, second, corner, panels, after, *rest):
    *messages, total = rest
    pairs = len(messages) // len(fars)
    share = messages[0].shape[0] // CHUNK
    rows, width = share * pairs, panels.shape[2]
    labels = own.shape[0] - CHUNK * rows
    place, x, _ = position()
    sources = [own, first, second, corner]
    names = [source[:labels, :width].astype(jnp.float32) for source in sources]
    for p, far in enumerate(fars):
        wanted = (place ^ far).astype(jnp.float32)
        green = panels[p]
        for n in range(CHUNK):
            sums = jnp.zeros((rows, width), jnp.float32)
            for source, name in zip(sources, names):
                named = (name[n * picks : (n + 1) * picks] == wanted).astype(jnp.float32)
                hit = jnp.max(named, axis=0, keepdims=True)
                tile = source[labels + n * rows : labels + (n + 1) * rows, :]
                product = jnp.dot(tile, green, preferred_element_type=jnp.float32) * hit
                sums = sums + product.astype(jnp.bfloat16).astype(jnp.float32)
            total[n] = sums
        for t in range(pairs):
            start = pl.multiple_of((x ^ t) * share, share)
            for n in range(CHUNK):
                block = total[n, pl.ds(start, share), :]
                message = messages[p * pairs + t]
                message[n * share : (n + 1) * share, :] = block.astype(message.dtype)


def virtual_sum(rows, operands):
    result = None
    for message, virtual in zip(operands[::2], operands[1::2]):
        for n in range(CHUNK):
            tile = message[n * rows : (n + 1) * rows, :]
            product = jnp.dot(tile, virtual[n], preferred_element_type=jnp.float32)
            result = product if result is None else result + product
    return result


def first_kernel(*refs):
    *operands, total = refs
    total[...] = virtual_sum(total.shape[0], operands)


def last_kernel(before, *refs):
    *operands, stays, leaves, total = refs
    middle = stays.shape[0]
    total[...] = before[...] + virtual_sum(total.shape[0], operands)
    core = position()[2]
    stays[...] = total[pl.ds(pl.multiple_of(core * middle, middle), middle), :]
    leaves[...] = total[pl.ds(pl.multiple_of((1 - core) * middle, middle), middle), :]


def call(kernel, name, out, specs, flops, scratch=(), vmem=KERNEL_VMEM):
    def run(*operands):
        return pl.pallas_call(
            kernel,
            out_shape=out,
            in_specs=specs,
            out_specs=jax.tree.map(lambda _: VMEM, out),
            scratch_shapes=scratch,
            cost_estimate=pl.CostEstimate(flops=flops, bytes_accessed=0, transcendentals=0),
            compiler_params=pltpu.CompilerParams(vmem_limit_bytes=vmem),
            name=name,
        )(*operands)

    return run


def shards(integrals, green_occ, tile_panels, virtual_blocks):
    grid_count, rep_count = lax.axis_size("grid"), lax.axis_size("rep")
    pairs = rep_count // 2
    tile_count, picks = tile_panels.shape
    rows, depth = integrals.shape[0] // tile_count, integrals.shape[1]
    width, columns = virtual_blocks.shape[-2:]
    share = rows // pairs

    def send(array, grid_bits, rep_bits=0):
        order = []
        for g in range(grid_count):
            for r in range(rep_count):
                order.append((g * rep_count + r, (g ^ grid_bits) * rep_count + (r ^ rep_bits)))
        return lax.ppermute(array, AXES, order)

    def like(shape, dtype):
        return jax.ShapeDtypeStruct(shape, dtype)

    label_rows = -(-CHUNK * picks // 16) * 16
    chunks = range(tile_count // CHUNK)
    half = green_occ.shape[0] // 2
    outs = [like((half, green_occ.shape[1]), green_occ.dtype)]
    outs += [like((label_rows + CHUNK * rows, depth), integrals.dtype) for _ in chunks]
    scratch = [
        pltpu.VMEM((picks, tile_count), jnp.int32),
        pltpu.SemaphoreType.DMA((2 + len(chunks),)),
    ]
    pack = call(lambda *refs: pack_kernel(picks, *refs), "pack", outs, [HBM] * 3, 0, scratch, PACK_VMEM)
    mine, *own = pack(tile_panels.T, integrals, green_occ)

    near = [n % 2 == 1 for n in chunks]
    first, second, corner = {}, {}, {}
    for wanted in (True, False):
        for n in chunks:
            if near[n] == wanted:
                second[n] = send(own[n], 2)
            else:
                first[n] = send(own[n], 1)
        if wanted:
            fars = list(range(SQUARE, grid_count, SQUARE))
            kept = [send(mine, far) for far in fars]
    for n in chunks:
        corner[n] = send(second[n], 1) if near[n] else send(first[n], 2)
    halves = [array for one in kept for array in (one, send(one, 0, 1))]
    fars = [0] + fars
    join = call(
        join_kernel,
        "join",
        like((len(fars),) + green_occ.shape, green_occ.dtype),
        [VMEM] * (1 + len(halves)),
        5 * 10**9,
    )
    panels = join(green_occ, *halves)

    virtual = [virtual_blocks[0]]
    virtual += [send(virtual[0], 0, 2 * t) for t in range(1, pairs)]

    after, operands = mine, {}
    ordered = sorted(chunks, key=lambda n: not near[n])
    for n in ordered:
        outs = [like((CHUNK * share, width), jnp.bfloat16)] * (len(fars) * pairs)
        sums = call(
            lambda *refs: sums_kernel(picks, fars, *refs),
            "sums",
            outs,
            [VMEM] * 5 + [ANY],
            2 * 10**9,
            [pltpu.VMEM((CHUNK, rows, width), jnp.float32)],
        )
        parts = sums(own[n], first[n], second[n], corner[n], panels, after)
        after = parts[0]
        operands[n] = []
        for p, far in enumerate(fars):
            for t in range(pairs):
                part = parts[p * pairs + t]
                message = send(part, far, 2 * t) if far or t else part
                operands[n] += [message, virtual[t][n * CHUNK : (n + 1) * CHUNK]]

    *early, late = ordered
    operands_of = [array for n in early for array in operands[n]]
    part = call(
        first_kernel, "virtual_first", like((share, columns), jnp.float32), [VMEM] * len(operands_of), 10**10
    )(*operands_of)
    last = call(
        last_kernel,
        "virtual_last",
        [like((share // 2, columns), jnp.float32)] * 2,
        [VMEM] * (1 + len(operands[late])),
        0,
        [pltpu.VMEM((share, columns), jnp.float32)],
    )
    stays, leaves = last(part, *operands[late])
    return (stays + send(leaves, 0, 1))[None]


def solution(mesh):
    in_specs = (
        P(("grid", "rep"), None),
        P(None, "grid"),
        P(("grid", "rep"), None),
        P("grid", "rep", None, None),
    )
    out_specs = P("grid", "rep", None)
    return jax.shard_map(shards, mesh=mesh, in_specs=in_specs, out_specs=out_specs, check_vma=False)
```

time: 127 us -> 45.1 us (0.36)
  waiting for transfers between devices: 91.9 us -> 19 us
  between operations: 13.4 us -> 0.11 us
  starting transfers between devices: 11 us -> 21 us
  matrix products: 8.44 us -> 0 us
  Pallas kernels: 0 us -> 4.17 us
  local copies, waits for them, and re-layouts: 1.55 us -> 0.09 us
    all_gather x1 -> x0, waiting for transfers between devices: 47 us -> none  [shards(): lax.all_gather(green_occ, 'grid', axis=1, tiled=True)]
    all_to_all x2 -> x0, waiting for transfers between devices: 25.4 us -> none  [the longest x1 25.4 us: shards(): lax.all_to_all(outgoing, 'grid', split_axis=0, concat_axis=0, tiled=True)]
    ppermute x0 -> x16, starting transfers between devices: none -> 21 us  [send(): return lax.ppermute(array, AXES, order)]
    ppermute x0 -> x16, waiting for transfers between devices: none -> 19 us  [send(): return lax.ppermute(array, AXES, order)]
    reduce_scatter x1 -> x0, waiting for transfers between devices: 18.8 us -> none  [shards(): lax.psum_scatter(owner_part[None], 'rep', scatter_dimension=1, tiled=True)]
    all_to_all x2 -> x0, starting transfers between devices: 11 us -> none  [the longest x1 7.28 us: shards(): lax.all_to_all(labels, 'grid', split_axis=0, concat_axis=0, tiled=True)]
    dot_general x4 -> x0, matrix products: 8.44 us -> none  [the longest x1 3.75 us: shards(): jnp.einsum('ldc,ltdw->dctw', place_weights, tile_blocks, preferred_elemen...]
    pallas_call x0 -> x6, Pallas kernels: none -> 4.17 us  [run(): pl.pallas_call(kernel, out_shape=out, in_specs=specs, out_specs=jax.tree....]
  transfers between devices with their start and end apart: 4 -> 16, of which waited for: 3 -> 9; matrix products, arithmetic and copies ran while one was open for 7% -> 0% of each run, Pallas kernels for 0% -> 4%
where the time goes in v4:
time: 45.1 us; the launch traced here: 45 us
  starting transfers between devices  21 us (47%)
  waiting for transfers between devices  19 us (42%)
  Pallas kernels  4.17 us (9%)
  other arithmetic  0.62 us (1%)
    ppermute x16, starting transfers between devices, send(): return lax.ppermute(array, AXES, order)  21 us
    ppermute x16, waiting for transfers between devices, send(): return lax.ppermute(array, AXES, order)  19 us
    pallas_call x6, Pallas kernels, run(): pl.pallas_call(kernel, out_shape=out, in_specs=specs, out_specs=jax.tree....  4.17 us
  transfers between devices with their start and end apart: 16, of which 9 were waited for; matrix products, arithmetic and copies ran while one was open for 0% of the time, Pallas kernels for 4%

profile of v4, /device:TPU:0, one launch (start us, length us, event | category | flops | bytes accessed | tf_op | source)
XLA Modules:
  0.0 45.0 jit_solution(5005542818616953231)
XLA Ops:
  0.0 0.0 copy-start.4
  0.0 2.1 %pack.1 = (bf16[256,256]{1,0:T(8,128)(2,1)}, bf16[272,512]{1,0:T(8,128)(2,1)}, bf16[272,512]{1,0:T(8,128)(2,1)}) custom-call(s32[2,4]{1,0:T(2,128)} %bitcast.9, bf16[512,512]{1,0:T(8,128)(2,1)} %refs_1_.1, bf16[512,256]{1,0:T(8,128)(2,1)} %own.1), custom_call_target="tpu_custom_call" | custom-call | tf_op jit(solution)/shard_map/pack/pallas_call | solution.py:122
  2.1 4.1 %collective-permute-start.3 = (bf16[256,256]{1,0:T(8,128)(2,1)}, bf16[256,256]{1,0:T(8,128)(2,1)S(1)}, u32[]{:S(2)}, u32[]{:S(2)}) collective-permute-start(bf16[256,256]{1,0:T(8,128)(2,1)} %get-tuple-element.19.refs_5_), channel_id=1, source_target_pairs={{0,16},{1,17},{2,18},{3,19},{4,20},{5,21},{6,22},{7,23},{8,24},{9,... | collective-permute-start | bytes 393224 | tf_op jit(solution)/shard_map/ppermute | solution.py:149
  6.2 1.6 %collective-permute-start.1 = (bf16[272,512]{1,0:T(8,128)(2,1)}, bf16[272,512]{1,0:T(8,128)(2,1)S(1)}, u32[]{:S(2)}, u32[]{:S(2)}) collective-permute-start(bf16[272,512]{1,0:T(8,128)(2,1)} %get-tuple-element.18.refs_0_), channel_id=1, source_target_pairs={{0,8},{1,9},{2,10},{3,11},{4,12},{5,13},{6,14},{7,15},{8,0},{9,1},... | collective-permute-start | bytes 835592 | tf_op jit(solution)/shard_map/ppermute | solution.py:149
  7.7 1.5 %collective-permute-start = (bf16[272,512]{1,0:T(8,128)(2,1)}, bf16[272,512]{1,0:T(8,128)(2,1)S(1)}, u32[]{:S(2)}, u32[]{:S(2)}) collective-permute-start(bf16[272,512]{1,0:T(8,128)(2,1)} %get-tuple-element.18.refs_0_), channel_id=1, source_target_pairs={{0,4},{1,5},{2,6},{3,7},{4,0},{5,1},{6,2},{7,3},{8,12},{9,13},{10,... | collective-permute-start | bytes 835592 | tf_op jit(solution)/shard_map/ppermute | solution.py:149
  9.3 0.5 %collective-permute-start.9 = (bf16[272,512]{1,0:T(8,128)(2,1)}, bf16[272,512]{1,0:T(8,128)(2,1)S(1)}, u32[]{:S(2)}, u32[]{:S(2)}) collective-permute-start(bf16[272,512]{1,0:T(8,128)(2,1)} %get-tuple-element.24.refs_0_), channel_id=1, source_target_pairs={{0,4},{1,5},{2,6},{3,7},{4,0},{5,1},{6,2},{7,3},{8,12},{9,13},{10,... | collective-permute-start | bytes 835592 | tf_op jit(solution)/shard_map/ppermute | solution.py:149
  9.8 0.0 copy-done.4
  9.8 0.0 copy-start.1
  9.8 0.0 copy-start
  9.8 1.5 %collective-permute-start.6 = (bf16[4,256,256]{2,1,0:T(8,128)(2,1)S(1)}, bf16[4,256,256]{2,1,0:T(8,128)(2,1)S(1)}, u32[]{:S(2)}, u32[]{:S(2)}) collective-permute-start(bf16[4,256,256]{2,1,0:T(8,128)(2,1)S(1)} %bitcast.8), channel_id=1, source_target_pairs={{0,2},{1,3},{2,0},{3,1},{4,6},{5,7},{6,4},{7,5},{8,10},{9,11},{10,... | collective-permute-start | bytes 1572872 | tf_op jit(solution)/shard_map/ppermute | solution.py:149
  11.3 1.5 %collective-permute-done.3.rest_0_ = bf16[256,256]{1,0:T(8,128)(2,1)S(1)} collective-permute-done((bf16[256,256]{1,0:T(8,128)(2,1)}, bf16[256,256]{1,0:T(8,128)(2,1)S(1)}, u32[]{:S(2)}, u32[]{:S(2)}) %collective-permute-start.3) | collective-permute-done | bytes 131104 | tf_op jit(solution)/shard_map/ppermute | solution.py:149
  12.8 0.0 collective-permute-start.4
  12.8 1.3 %collective-permute-done.4.rest_1_ = bf16[256,256]{1,0:T(8,128)(2,1)S(1)} collective-permute-done((bf16[256,256]{1,0:T(8,128)(2,1)S(1)}, bf16[256,256]{1,0:T(8,128)(2,1)S(1)}, u32[]{:S(2)}, u32[]{:S(2)}) %collective-permute-start.4) | collective-permute-done | bytes 131104 | tf_op jit(solution)/shard_map/ppermute | solution.py:149
  14.1 0.0 copy-done.1
  14.1 0.8 %collective-permute-start.10 = (bf16[272,512]{1,0:T(8,128)(2,1)S(1)}, bf16[272,512]{1,0:T(8,128)(2,1)S(1)}, u32[]{:S(2)}, u32[]{:S(2)}) collective-permute-start(bf16[272,512]{1,0:T(8,128)(2,1)S(1)} %copy-done.1), channel_id=1, source_target_pairs={{0,8},{1,9},{2,10},{3,11},{4,12},{5,13},{6,14},{7,15},{8,0},{9,1},... | collective-permute-start | bytes 835592 | tf_op jit(solution)/shard_map/ppermute | solution.py:149
  14.9 1.2 %collective-permute-done.1.refs_2_ = bf16[272,512]{1,0:T(8,128)(2,1)S(1)} collective-permute-done((bf16[272,512]{1,0:T(8,128)(2,1)}, bf16[272,512]{1,0:T(8,128)(2,1)S(1)}, u32[]{:S(2)}, u32[]{:S(2)}) %collective-permute-start.1) | collective-permute-done | bytes 278560 | tf_op jit(solution)/shard_map/ppermute | solution.py:149
  16.1 1.6 %collective-permute-start.2 = (bf16[272,512]{1,0:T(8,128)(2,1)S(1)}, bf16[272,512]{1,0:T(8,128)(2,1)S(1)}, u32[]{:S(2)}, u32[]{:S(2)}) collective-permute-start(bf16[272,512]{1,0:T(8,128)(2,1)S(1)} %collective-permute-done.1.refs_2_), channel_id=1, source_target_pairs={{0,4},{1,5},{2,6},{3,7},{4,0},{5,1},{6,2},{7,3},{8,12},{9,13},{10,... | collective-permute-start | bytes 835592 | tf_op jit(solution)/shard_map/ppermute | solution.py:149
  17.7 0.0 copy-done
  17.8 0.0 copy-start.2
  17.8 0.0 copy-start.3
  17.8 5.7 %collective-permute-done.9.refs_1_ = bf16[272,512]{1,0:T(8,128)(2,1)S(1)} collective-permute-done((bf16[272,512]{1,0:T(8,128)(2,1)}, bf16[272,512]{1,0:T(8,128)(2,1)S(1)}, u32[]{:S(2)}, u32[]{:S(2)}) %collective-permute-start.9) | collective-permute-done | bytes 278560 | tf_op jit(solution)/shard_map/ppermute | solution.py:149
  23.5 0.4 collective-permute-start.11
  24.0 0.0 collective-permute-done.6
  24.0 0.0 collective-permute-done.refs_1_
  24.0 3.7 %collective-permute-done.2.refs_3_ = bf16[272,512]{1,0:T(8,128)(2,1)S(1)} collective-permute-done((bf16[272,512]{1,0:T(8,128)(2,1)S(1)}, bf16[272,512]{1,0:T(8,128)(2,1)S(1)}, u32[]{:S(2)}, u32[]{:S(2)}) %collective-permute-start.2) | collective-permute-done | bytes 278560 | tf_op jit(solution)/shard_map/ppermute | solution.py:149
  27.7 0.0 copy-done.2
  27.7 0.0 copy-done.3
  27.7 0.7 %sums.2 = (bf16[128,256]{1,0:T(8,128)(2,1)S(1)}, bf16[128,256]{1,0:T(8,128)(2,1)S(1)}, bf16[128,256]{1,0:T(8,128)(2,1)S(1)}, bf16[128,256]{1,0:T(8,128)(2,1)S(1)}) custom-call(bf16[272,512]{1,0:T(8,128)(2,1)S(1)} %copy-done.2, bf16[272,512]{1,0:T(8,128)(2,1)S(1)} %collective-permute-done.refs_1_, bf16[272,512]{1,0:T(8,128)(2,1)S(1)} %collective-permute-done.1.refs_2_, ...), custom_call_target="tpu_custom_call" | custom-call | flops 2000000000 | tf_op jit(solution)/shard_map/sums/pallas_call | solution.py:122
  28.5 1.6 %collective-permute-start.5 = (bf16[128,256]{1,0:T(8,128)(2,1)S(1)}, bf16[128,256]{1,0:T(8,128)(2,1)S(1)}, u32[]{:S(2)}, u32[]{:S(2)}) collective-permute-start(bf16[128,256]{1,0:T(8,128)(2,1)S(1)} %get-tuple-element.21), channel_id=1, source_target_pairs={{0,2},{1,3},{2,0},{3,1},{4,6},{5,7},{6,4},{7,5},{8,10},{9,11},{10,... | collective-permute-start | bytes 196616 | tf_op jit(solution)/shard_map/ppermute | solution.py:149
  30.0 0.4 collective-permute-start.7
  30.4 2.5 %collective-permute-start.8 = (bf16[128,256]{1,0:T(8,128)(2,1)S(1)}, bf16[128,256]{1,0:T(8,128)(2,1)S(1)}, u32[]{:S(2)}, u32[]{:S(2)}) collective-permute-start(bf16[128,256]{1,0:T(8,128)(2,1)S(1)} %get-tuple-element.23), channel_id=1, source_target_pairs={{0,18},{1,19},{2,16},{3,17},{4,22},{5,23},{6,20},{7,21},{8,26},{9,... | collective-permute-start | bytes 196616 | tf_op jit(solution)/shard_map/ppermute | solution.py:149
  32.9 0.0 collective-permute-done.10.refs_2_
  32.9 0.0 collective-permute-done.11.refs_3_
  32.9 0.7 %sums.3 = (bf16[128,256]{1,0:T(8,128)(2,1)S(1)}, bf16[128,256]{1,0:T(8,128)(2,1)S(1)}, bf16[128,256]{1,0:T(8,128)(2,1)S(1)}, bf16[128,256]{1,0:T(8,128)(2,1)S(1)}) custom-call(bf16[272,512]{1,0:T(8,128)(2,1)S(1)} %copy-done.1, bf16[272,512]{1,0:T(8,128)(2,1)S(1)} %collective-permute-done.9.refs_1_, bf16[272,512]{1,0:T(8,128)(2,1)S(1)} %collective-permute-done.10.refs_2_, ...), custom_call_target="tpu_custom_call" | custom-call | flops 2000000000 | tf_op jit(solution)/shard_map/sums/pallas_call | solution.py:122
  33.7 1.5 %collective-permute-start.12 = (bf16[128,256]{1,0:T(8,128)(2,1)S(1)}, bf16[128,256]{1,0:T(8,128)(2,1)S(1)}, u32[]{:S(2)}, u32[]{:S(2)}) collective-permute-start(bf16[128,256]{1,0:T(8,128)(2,1)S(1)} %get-tuple-element.26), channel_id=1, source_target_pairs={{0,2},{1,3},{2,0},{3,1},{4,6},{5,7},{6,4},{7,5},{8,10},{9,11},{10,... | collective-permute-start | bytes 196616 | tf_op jit(solution)/shard_map/ppermute | solution.py:149
  35.2 0.4 collective-permute-start.13
  35.6 0.0 collective-permute-done.5.refs_2_
  35.6 2.5 %collective-permute-start.14 = (bf16[128,256]{1,0:T(8,128)(2,1)S(1)}, bf16[128,256]{1,0:T(8,128)(2,1)S(1)}, u32[]{:S(2)}, u32[]{:S(2)}) collective-permute-start(bf16[128,256]{1,0:T(8,128)(2,1)S(1)} %get-tuple-element.28), channel_id=1, source_target_pairs={{0,18},{1,19},{2,16},{3,17},{4,22},{5,23},{6,20},{7,21},{8,26},{9,... | collective-permute-start | bytes 196616 | tf_op jit(solution)/shard_map/ppermute | solution.py:149
  38.1 0.3 collective-permute-done.7.refs_4_
  38.5 0.0 collective-permute-done.8.refs_6_
  38.5 0.3 virtual_first.1.before
  38.8 0.0 collective-permute-done.12.refs_2_
  38.9 3.3 %collective-permute-done.13.refs_4_ = bf16[128,256]{1,0:T(8,128)(2,1)S(1)} collective-permute-done((bf16[128,256]{1,0:T(8,128)(2,1)S(1)}, bf16[128,256]{1,0:T(8,128)(2,1)S(1)}, u32[]{:S(2)}, u32[]{:S(2)}) %collective-permute-start.13) | collective-permute-done | bytes 65568 | tf_op jit(solution)/shard_map/ppermute | solution.py:149
  42.1 0.7 %collective-permute-done.14.refs_6_ = bf16[128,256]{1,0:T(8,128)(2,1)S(1)} collective-permute-done((bf16[128,256]{1,0:T(8,128)(2,1)S(1)}, bf16[128,256]{1,0:T(8,128)(2,1)S(1)}, u32[]{:S(2)}, u32[]{:S(2)}) %collective-permute-start.14) | collective-permute-done | bytes 65568 | tf_op jit(solution)/shard_map/ppermute | solution.py:149
  42.8 0.3 virtual_last.1
  43.1 0.1 collective-permute-start.15
  43.2 1.2 %collective-permute-done.15 = f32[32,256]{1,0:T(8,128)S(1)} collective-permute-done((f32[32,256]{1,0:T(8,128)S(1)}, f32[32,256]{1,0:T(8,128)S(1)}, u32[]{:S(2)}, u32[]{:S(2)}) %collective-permute-start.15) | collective-permute-done | bytes 32800 | tf_op jit(solution)/shard_map/ppermute | solution.py:149
  44.4 0.6 %add_bitcast_fusion = f32[1,32,256]{2,1,0:T(8,128)} fusion(f32[32,256]{1,0:T(8,128)S(1)} %get-tuple-element.29, f32[32,256]{1,0:T(8,128)S(1)} %collective-permute-done.15), kind=kLoop, calls=%fused_computation.2 | loop fusion | flops 8192 | bytes 98304 | tf_op jit(solution)/shard_map/broadcast_in_dim | solution.py:228
  (3 shorter events, 0.1 us)
Async XLA Ops:
  0.0 9.8 %copy-start.4 = (bf16[1,4,256,256]{3,2,1,0:T(8,128)(2,1)S(1)}, bf16[1,4,256,256]{3,2,1,0:T(8,128)(2,1)}, u32[]{:S(2)}) copy-start(bf16[1,4,256,256]{3,2,1,0:T(8,128)(2,1)} %param.7) | copy-start | bytes 1572868
  2.1 10.7 %collective-permute-start.3 = (bf16[256,256]{1,0:T(8,128)(2,1)}, bf16[256,256]{1,0:T(8,128)(2,1)S(1)}, u32[]{:S(2)}, u32[]{:S(2)}) collective-permute-start(bf16[256,256]{1,0:T(8,128)(2,1)} %get-tuple-element.19.refs_5_), channel_id=1, source_target_pairs={{0,16},{1,17},{2,18},{3,19},{4,20},{5,21},{6,22},{7,23},{8,24},{9,... | collective-permute-start | bytes 393224 | tf_op jit(solution)/shard_map/ppermute | solution.py:149
  6.2 10.0 %collective-permute-start.1 = (bf16[272,512]{1,0:T(8,128)(2,1)}, bf16[272,512]{1,0:T(8,128)(2,1)S(1)}, u32[]{:S(2)}, u32[]{:S(2)}) collective-permute-start(bf16[272,512]{1,0:T(8,128)(2,1)} %get-tuple-element.18.refs_0_), channel_id=1, source_target_pairs={{0,8},{1,9},{2,10},{3,11},{4,12},{5,13},{6,14},{7,15},{8,0},{9,1},... | collective-permute-start | bytes 835592 | tf_op jit(solution)/shard_map/ppermute | solution.py:149
  7.7 16.3 %collective-permute-start = (bf16[272,512]{1,0:T(8,128)(2,1)}, bf16[272,512]{1,0:T(8,128)(2,1)S(1)}, u32[]{:S(2)}, u32[]{:S(2)}) collective-permute-start(bf16[272,512]{1,0:T(8,128)(2,1)} %get-tuple-element.18.refs_0_), channel_id=1, source_target_pairs={{0,4},{1,5},{2,6},{3,7},{4,0},{5,1},{6,2},{7,3},{8,12},{9,13},{10,... | collective-permute-start | bytes 835592 | tf_op jit(solution)/shard_map/ppermute | solution.py:149
  9.3 14.3 %collective-permute-start.9 = (bf16[272,512]{1,0:T(8,128)(2,1)}, bf16[272,512]{1,0:T(8,128)(2,1)S(1)}, u32[]{:S(2)}, u32[]{:S(2)}) collective-permute-start(bf16[272,512]{1,0:T(8,128)(2,1)} %get-tuple-element.24.refs_0_), channel_id=1, source_target_pairs={{0,4},{1,5},{2,6},{3,7},{4,0},{5,1},{6,2},{7,3},{8,12},{9,13},{10,... | collective-permute-start | bytes 835592 | tf_op jit(solution)/shard_map/ppermute | solution.py:149
  9.8 4.4 %copy-start.1 = (bf16[272,512]{1,0:T(8,128)(2,1)S(1)}, bf16[272,512]{1,0:T(8,128)(2,1)}, u32[]{:S(2)}) copy-start(bf16[272,512]{1,0:T(8,128)(2,1)} %get-tuple-element.24.refs_0_) | copy-start | bytes 835588
  9.8 7.9 %copy-start = (bf16[512,256]{1,0:T(8,128)(2,1)S(1)}, bf16[512,256]{1,0:T(8,128)(2,1)}, u32[]{:S(2)}) copy-start(bf16[512,256]{1,0:T(8,128)(2,1)} %own.1) | copy-start | bytes 786436
  9.8 14.2 %collective-permute-start.6 = (bf16[4,256,256]{2,1,0:T(8,128)(2,1)S(1)}, bf16[4,256,256]{2,1,0:T(8,128)(2,1)S(1)}, u32[]{:S(2)}, u32[]{:S(2)}) collective-permute-start(bf16[4,256,256]{2,1,0:T(8,128)(2,1)S(1)} %bitcast.8), channel_id=1, source_target_pairs={{0,2},{1,3},{2,0},{3,1},{4,6},{5,7},{6,4},{7,5},{8,10},{9,11},{10,... | collective-permute-start | bytes 1572872 | tf_op jit(solution)/shard_map/ppermute | solution.py:149
  12.8 1.3 %collective-permute-start.4 = (bf16[256,256]{1,0:T(8,128)(2,1)S(1)}, bf16[256,256]{1,0:T(8,128)(2,1)S(1)}, u32[]{:S(2)}, u32[]{:S(2)}) collective-permute-start(bf16[256,256]{1,0:T(8,128)(2,1)S(1)} %collective-permute-done.3.rest_0_), channel_id=1, source_target_pairs={{0,1},{1,0},{2,3},{3,2},{4,5},{5,4},{6,7},{7,6},{8,9},{9,8},{10,11... | collective-permute-start | bytes 393224 | tf_op jit(solution)/shard_map/ppermute | solution.py:149
  14.1 18.8 %collective-permute-start.10 = (bf16[272,512]{1,0:T(8,128)(2,1)S(1)}, bf16[272,512]{1,0:T(8,128)(2,1)S(1)}, u32[]{:S(2)}, u32[]{:S(2)}) collective-permute-start(bf16[272,512]{1,0:T(8,128)(2,1)S(1)} %copy-done.1), channel_id=1, source_target_pairs={{0,8},{1,9},{2,10},{3,11},{4,12},{5,13},{6,14},{7,15},{8,0},{9,1},... | collective-permute-start | bytes 835592 | tf_op jit(solution)/shard_map/ppermute | solution.py:149
  16.1 11.6 %collective-permute-start.2 = (bf16[272,512]{1,0:T(8,128)(2,1)S(1)}, bf16[272,512]{1,0:T(8,128)(2,1)S(1)}, u32[]{:S(2)}, u32[]{:S(2)}) collective-permute-start(bf16[272,512]{1,0:T(8,128)(2,1)S(1)} %collective-permute-done.1.refs_2_), channel_id=1, source_target_pairs={{0,4},{1,5},{2,6},{3,7},{4,0},{5,1},{6,2},{7,3},{8,12},{9,13},{10,... | collective-permute-start | bytes 835592 | tf_op jit(solution)/shard_map/ppermute | solution.py:149
  17.8 10.0 %copy-start.2 = (bf16[272,512]{1,0:T(8,128)(2,1)S(1)}, bf16[272,512]{1,0:T(8,128)(2,1)}, u32[]{:S(2)}) copy-start(bf16[272,512]{1,0:T(8,128)(2,1)} %get-tuple-element.18.refs_0_) | copy-start | bytes 835588
  17.8 10.0 %copy-start.3 = (bf16[256,256]{1,0:T(8,128)(2,1)S(1)}, bf16[256,256]{1,0:T(8,128)(2,1)}, u32[]{:S(2)}) copy-start(bf16[256,256]{1,0:T(8,128)(2,1)} %get-tuple-element.19.refs_5_) | copy-start | bytes 393220
  23.5 9.4 %collective-permute-start.11 = (bf16[272,512]{1,0:T(8,128)(2,1)S(1)}, bf16[272,512]{1,0:T(8,128)(2,1)S(1)}, u32[]{:S(2)}, u32[]{:S(2)}) collective-permute-start(bf16[272,512]{1,0:T(8,128)(2,1)S(1)} %collective-permute-done.9.refs_1_), channel_id=1, source_target_pairs={{0,8},{1,9},{2,10},{3,11},{4,12},{5,13},{6,14},{7,15},{8,0},{9,1},... | collective-permute-start | bytes 835592 | tf_op jit(solution)/shard_map/ppermute | solution.py:149
  28.5 7.1 %collective-permute-start.5 = (bf16[128,256]{1,0:T(8,128)(2,1)S(1)}, bf16[128,256]{1,0:T(8,128)(2,1)S(1)}, u32[]{:S(2)}, u32[]{:S(2)}) collective-permute-start(bf16[128,256]{1,0:T(8,128)(2,1)S(1)} %get-tuple-element.21), channel_id=1, source_target_pairs={{0,2},{1,3},{2,0},{3,1},{4,6},{5,7},{6,4},{7,5},{8,10},{9,11},{10,... | collective-permute-start | bytes 196616 | tf_op jit(solution)/shard_map/ppermute | solution.py:149
  30.0 8.5 %collective-permute-start.7 = (bf16[128,256]{1,0:T(8,128)(2,1)S(1)}, bf16[128,256]{1,0:T(8,128)(2,1)S(1)}, u32[]{:S(2)}, u32[]{:S(2)}) collective-permute-start(bf16[128,256]{1,0:T(8,128)(2,1)S(1)} %get-tuple-element.22), channel_id=1, source_target_pairs={{0,16},{1,17},{2,18},{3,19},{4,20},{5,21},{6,22},{7,23},{8,24},{9,... | collective-permute-start | bytes 196616 | tf_op jit(solution)/shard_map/ppermute | solution.py:149
  30.4 8.1 %collective-permute-start.8 = (bf16[128,256]{1,0:T(8,128)(2,1)S(1)}, bf16[128,256]{1,0:T(8,128)(2,1)S(1)}, u32[]{:S(2)}, u32[]{:S(2)}) collective-permute-start(bf16[128,256]{1,0:T(8,128)(2,1)S(1)} %get-tuple-element.23), channel_id=1, source_target_pairs={{0,18},{1,19},{2,16},{3,17},{4,22},{5,23},{6,20},{7,21},{8,26},{9,... | collective-permute-start | bytes 196616 | tf_op jit(solution)/shard_map/ppermute | solution.py:149
  33.7 5.2 %collective-permute-start.12 = (bf16[128,256]{1,0:T(8,128)(2,1)S(1)}, bf16[128,256]{1,0:T(8,128)(2,1)S(1)}, u32[]{:S(2)}, u32[]{:S(2)}) collective-permute-start(bf16[128,256]{1,0:T(8,128)(2,1)S(1)} %get-tuple-element.26), channel_id=1, source_target_pairs={{0,2},{1,3},{2,0},{3,1},{4,6},{5,7},{6,4},{7,5},{8,10},{9,11},{10,... | collective-permute-start | bytes 196616 | tf_op jit(solution)/shard_map/ppermute | solution.py:149
  35.2 6.9 %collective-permute-start.13 = (bf16[128,256]{1,0:T(8,128)(2,1)S(1)}, bf16[128,256]{1,0:T(8,128)(2,1)S(1)}, u32[]{:S(2)}, u32[]{:S(2)}) collective-permute-start(bf16[128,256]{1,0:T(8,128)(2,1)S(1)} %get-tuple-element.27), channel_id=1, source_target_pairs={{0,16},{1,17},{2,18},{3,19},{4,20},{5,21},{6,22},{7,23},{8,24},{9,... | collective-permute-start | bytes 196616 | tf_op jit(solution)/shard_map/ppermute | solution.py:149
  35.6 7.2 %collective-permute-start.14 = (bf16[128,256]{1,0:T(8,128)(2,1)S(1)}, bf16[128,256]{1,0:T(8,128)(2,1)S(1)}, u32[]{:S(2)}, u32[]{:S(2)}) collective-permute-start(bf16[128,256]{1,0:T(8,128)(2,1)S(1)} %get-tuple-element.28), channel_id=1, source_target_pairs={{0,18},{1,19},{2,16},{3,17},{4,22},{5,23},{6,20},{7,21},{8,26},{9,... | collective-permute-start | bytes 196616 | tf_op jit(solution)/shard_map/ppermute | solution.py:149
  43.1 1.3 %collective-permute-start.15 = (f32[32,256]{1,0:T(8,128)S(1)}, f32[32,256]{1,0:T(8,128)S(1)}, u32[]{:S(2)}, u32[]{:S(2)}) collective-permute-start(f32[32,256]{1,0:T(8,128)S(1)} %get-tuple-element.30), channel_id=1, source_target_pairs={{0,1},{1,0},{2,3},{3,2},{4,5},{5,4},{6,7},{7,6},{8,9},{9,8},{10,11... | collective-permute-start | bytes 98312 | tf_op jit(solution)/shard_map/ppermute | solution.py:149

commit v5 on v4

--- a/solution.py
+++ b/solution.py
@@ -21,23 +21,21 @@
 
 
 def pack_kernel(picks, listed, integrals, green, half_green, *rest):
-    *messages, names, done = rest
+    whole, *messages, names, done = rest
     half = half_green.shape[0]
+    size = messages[0].shape[0]
     tile_rows = integrals.shape[0] // len(messages)
-    label_rows = messages[0].shape[0] - tile_rows
+    label_rows = size - tile_rows
     start = pl.multiple_of(position()[2] * half, half)
     copies = [
         pltpu.make_async_copy(listed, names, done.at[0]),
         pltpu.make_async_copy(green.at[pl.ds(start, half), :], half_green, done.at[1]),
     ]
     for m, message in enumerate(messages):
-        copies.append(
-            pltpu.make_async_copy(
-                integrals.at[m * tile_rows : (m + 1) * tile_rows, :],
-                message.at[label_rows:, :],
-                done.at[m + 2],
-            )
-        )
+        tiles = integrals.at[m * tile_rows : (m + 1) * tile_rows, :]
+        copies.append(pltpu.make_async_copy(tiles, message.at[label_rows:, :], done.at[2 * m + 2]))
+        place = whole.at[m * size + label_rows : (m + 1) * size, :]
+        copies.append(pltpu.make_async_copy(tiles, place, done.at[2 * m + 3]))
     for copy in copies:
         copy.start()
     copies[0].wait()
@@ -48,7 +46,9 @@
             for s in range(picks):
                 tile = m * CHUNK + n
                 value = jnp.where(line == n * picks + s, names[s : s + 1, tile : tile + 1], value)
-        message[:label_rows, :] = value.astype(jnp.float32).astype(message.dtype)
+        labels = value.astype(jnp.float32).astype(message.dtype)
+        message[:label_rows, :] = labels
+        whole[m * size : m * size + label_rows, :] = labels
     for copy in copies[1:]:
         copy.wait()
 
@@ -57,31 +57,32 @@
     *halves, panels = rest
     half = halves[0].shape[0]
     core = position()[2]
-    panels[0] = own[...]
+    panels[len(halves) // 2] = own[...]
     for n in range(len(halves) // 2):
         for h, array in enumerate(halves[2 * n : 2 * n + 2]):
             start = pl.multiple_of((core ^ h) * half, half)
-            panels[1 + n, pl.ds(start, half), :] = array[...]
-
-
-def sums_kernel(picks, fars, own, first, second, corner, panels, after, *rest):
+            panels[n, pl.ds(start, half), :] = array[...]
+
+
+def sums_kernel(picks, fars, chunk, own, first, second, corner, panels, after, *rest):
     *messages, total = rest
     pairs = len(messages) // len(fars)
     share = messages[0].shape[0] // CHUNK
     rows, width = share * pairs, panels.shape[2]
     labels = own.shape[0] - CHUNK * rows
     place, x, _ = position()
-    sources = [own, first, second, corner]
-    names = [source[:labels, :width].astype(jnp.float32) for source in sources]
+    sources = [(own, 0), (first, chunk * own.shape[0]), (second, 0), (corner, 0)]
+    names = [source[at : at + labels, :width].astype(jnp.float32) for source, at in sources]
     for p, far in enumerate(fars):
         wanted = (place ^ far).astype(jnp.float32)
         green = panels[p]
         for n in range(CHUNK):
             sums = jnp.zeros((rows, width), jnp.float32)
-            for source, name in zip(sources, names):
+            for (source, at), name in zip(sources, names):
                 named = (name[n * picks : (n + 1) * picks] == wanted).astype(jnp.float32)
                 hit = jnp.max(named, axis=0, keepdims=True)
-                tile = source[labels + n * rows : labels + (n + 1) * rows, :]
+                start = at + labels + n * rows
+                tile = source[start : start + rows, :]
                 product = jnp.dot(tile, green, preferred_element_type=jnp.float32) * hit
                 sums = sums + product.astype(jnp.bfloat16).astype(jnp.float32)
             total[n] = sums
@@ -155,35 +156,32 @@
     chunks = range(tile_count // CHUNK)
     half = green_occ.shape[0] // 2
     outs = [like((half, green_occ.shape[1]), green_occ.dtype)]
-    outs += [like((label_rows + CHUNK * rows, depth), integrals.dtype) for _ in chunks]
+    size = label_rows + CHUNK * rows
+    outs.append(like((len(chunks) * size, depth), integrals.dtype))
+    outs += [like((size, depth), integrals.dtype) for _ in chunks]
     scratch = [
         pltpu.VMEM((picks, tile_count), jnp.int32),
-        pltpu.SemaphoreType.DMA((2 + len(chunks),)),
+        pltpu.SemaphoreType.DMA((2 + 2 * len(chunks),)),
     ]
     pack = call(lambda *refs: pack_kernel(picks, *refs), "pack", outs, [HBM] * 3, 0, scratch, PACK_VMEM)
-    mine, *own = pack(tile_panels.T, integrals, green_occ)
+    mine, whole, *own = pack(tile_panels.T, integrals, green_occ)
 
     near = [n % 2 == 1 for n in chunks]
-    first, second, corner = {}, {}, {}
-    for wanted in (True, False):
-        for n in chunks:
-            if near[n] == wanted:
-                second[n] = send(own[n], 2)
-            else:
-                first[n] = send(own[n], 1)
-        if wanted:
-            fars = list(range(SQUARE, grid_count, SQUARE))
-            kept = [send(mine, far) for far in fars]
+    first = send(whole, 1)
+    second = {n: send(own[n], 2) for wanted in (True, False) for n in chunks if near[n] == wanted}
+    fars = list(range(SQUARE, grid_count, SQUARE))
+    kept = [send(mine, far) for far in fars]
+    corner = {}
     for n in chunks:
-        corner[n] = send(second[n], 1) if near[n] else send(first[n], 2)
+        corner[n] = send(second[n], 1) if near[n] else send(first[n * size : (n + 1) * size], 2)
     halves = [array for one in kept for array in (one, send(one, 0, 1))]
-    fars = [0] + fars
+    fars = fars + [0]
     join = call(
         join_kernel,
         "join",
         like((len(fars),) + green_occ.shape, green_occ.dtype),
         [VMEM] * (1 + len(halves)),
-        5 * 10**9,
+        0,
     )
     panels = join(green_occ, *halves)
 
@@ -195,14 +193,14 @@
     for n in ordered:
         outs = [like((CHUNK * share, width), jnp.bfloat16)] * (len(fars) * pairs)
         sums = call(
-            lambda *refs: sums_kernel(picks, fars, *refs),
+            lambda *refs, n=n: sums_kernel(picks, fars, n, *refs),
             "sums",
             outs,
             [VMEM] * 5 + [ANY],
-            2 * 10**9,
+            0,
             [pltpu.VMEM((CHUNK, rows, width), jnp.float32)],
         )
-        parts = sums(own[n], first[n], second[n], corner[n], panels, after)
+        parts = sums(own[n], first, second[n], corner[n], panels, after)
         after = parts[0]
         operands[n] = []
         for p, far in enumerate(fars):
@@ -214,7 +212,7 @@
     *early, late = ordered
     operands_of = [array for n in early for array in operands[n]]
     part = call(
-        first_kernel, "virtual_first", like((share, columns), jnp.float32), [VMEM] * len(operands_of), 10**10
+        first_kernel, "virtual_first", like((share, columns), jnp.float32), [VMEM] * len(operands_of), 10**9
     )(*operands_of)
     last = call(
         last_kernel,

time: 45.1 us -> 44 us (0.976)
  waiting for transfers between devices: 19 us -> 17.6 us
    ppermute x16 -> x15, waiting for transfers between devices: 19 us -> 17.6 us  [send(): return lax.ppermute(array, AXES, order)]
    ppermute x16 -> x15, starting transfers between devices: 21 us -> 20.8 us  [send(): return lax.ppermute(array, AXES, order)]
  transfers between devices with their start and end apart: 16 -> 15, of which waited for: 9 -> 8; matrix products, arithmetic and copies ran while one was open for 0% -> 0% of each run, Pallas kernels for 4% -> 4%
where the time goes in v5:
time: 44 us; the launch traced here: 43.9 us
  starting transfers between devices  20.8 us (47%)
  waiting for transfers between devices  17.6 us (40%)
  Pallas kernels  4.56 us (10%)
  other arithmetic  0.62 us (1%)
    ppermute x15, starting transfers between devices, send(): return lax.ppermute(array, AXES, order)  20.8 us
    ppermute x15, waiting for transfers between devices, send(): return lax.ppermute(array, AXES, order)  17.6 us
    pallas_call x6, Pallas kernels, run(): pl.pallas_call(kernel, out_shape=out, in_specs=specs, out_specs=jax.tree....  4.56 us
  transfers between devices with their start and end apart: 15, of which 8 were waited for; matrix products, arithmetic and copies ran while one was open for 0% of the time, Pallas kernels for 4%

profile of v5, /device:TPU:0, one launch (start us, length us, event | category | flops | bytes accessed | tf_op | source)
XLA Modules:
  0.0 43.9 jit_solution(8071430409243680691)
XLA Ops:
  0.0 0.0 copy-start.4
  0.0 2.4 %pack.1 = (bf16[256,256]{1,0:T(8,128)(2,1)}, bf16[544,512]{1,0:T(8,128)(2,1)}, bf16[272,512]{1,0:T(8,128)(2,1)}, bf16[272,512]{1,0:T(8,128)(2,1)}) custom-call(s32[2,4]{1,0:T(2,128)} %bitcast.9, bf16[512,512]{1,0:T(8,128)(2,1)} %refs_1_.1, bf16[512,256]{1,0:T(8,128)(2,1)} %own.1), custom_call_target="tpu_custom_call" | custom-call | tf_op jit(solution)/shard_map/pack/pallas_call | solution.py:123
  2.4 3.0 %collective-permute-start = (bf16[544,512]{1,0:T(8,128)(2,1)}, bf16[544,512]{1,0:T(8,128)(2,1)S(1)}, u32[]{:S(2)}, u32[]{:S(2)}) collective-permute-start(bf16[544,512]{1,0:T(8,128)(2,1)} %get-tuple-element.20), channel_id=1, source_target_pairs={{0,4},{1,5},{2,6},{3,7},{4,0},{5,1},{6,2},{7,3},{8,12},{9,13},{10,... | collective-permute-start | bytes 1671176 | tf_op jit(solution)/shard_map/ppermute | solution.py:150
  5.5 1.6 %collective-permute-start.1 = (bf16[272,512]{1,0:T(8,128)(2,1)}, bf16[272,512]{1,0:T(8,128)(2,1)S(1)}, u32[]{:S(2)}, u32[]{:S(2)}) collective-permute-start(bf16[272,512]{1,0:T(8,128)(2,1)} %get-tuple-element.19.refs_0_), channel_id=1, source_target_pairs={{0,8},{1,9},{2,10},{3,11},{4,12},{5,13},{6,14},{7,15},{8,0},{9,1},... | collective-permute-start | bytes 835592 | tf_op jit(solution)/shard_map/ppermute | solution.py:150
  7.1 0.0 copy-done.4
  7.1 1.5 %collective-permute-start.7 = (bf16[4,256,256]{2,1,0:T(8,128)(2,1)S(1)}, bf16[4,256,256]{2,1,0:T(8,128)(2,1)S(1)}, u32[]{:S(2)}, u32[]{:S(2)}) collective-permute-start(bf16[4,256,256]{2,1,0:T(8,128)(2,1)S(1)} %bitcast.8), channel_id=1, source_target_pairs={{0,2},{1,3},{2,0},{3,1},{4,6},{5,7},{6,4},{7,5},{8,10},{9,11},{10,... | collective-permute-start | bytes 1572872 | tf_op jit(solution)/shard_map/ppermute | solution.py:150
  8.5 2.6 %collective-permute-start.3 = (bf16[256,256]{1,0:T(8,128)(2,1)}, bf16[256,256]{1,0:T(8,128)(2,1)S(1)}, u32[]{:S(2)}, u32[]{:S(2)}) collective-permute-start(bf16[256,256]{1,0:T(8,128)(2,1)} %get-tuple-element.21.refs_5_), channel_id=1, source_target_pairs={{0,16},{1,17},{2,18},{3,19},{4,20},{5,21},{6,22},{7,23},{8,24},{9,... | collective-permute-start | bytes 393224 | tf_op jit(solution)/shard_map/ppermute | solution.py:150
  11.1 5.5 %collective-permute-done.1.refs_2_ = bf16[272,512]{1,0:T(8,128)(2,1)S(1)} collective-permute-done((bf16[272,512]{1,0:T(8,128)(2,1)}, bf16[272,512]{1,0:T(8,128)(2,1)S(1)}, u32[]{:S(2)}, u32[]{:S(2)}) %collective-permute-start.1) | collective-permute-done | bytes 278560 | tf_op jit(solution)/shard_map/ppermute | solution.py:150
  16.6 0.4 collective-permute-start.2
  17.0 0.3 collective-permute-start.9
  17.3 0.0 collective-permute-done.3.rest_0_
  17.3 0.0 collective-permute-start.4
  17.3 1.5 %collective-permute-done.refs_1_ = bf16[544,512]{1,0:T(8,128)(2,1)S(1)} collective-permute-done((bf16[544,512]{1,0:T(8,128)(2,1)}, bf16[544,512]{1,0:T(8,128)(2,1)S(1)}, u32[]{:S(2)}, u32[]{:S(2)}) %collective-permute-start) | collective-permute-done | bytes 557088 | tf_op jit(solution)/shard_map/ppermute | solution.py:150
  18.8 0.0 copy-start
  18.9 2.5 %collective-permute-start.10 = (bf16[272,512]{1,0:T(8,128)(2,1)S(1)}, bf16[272,512]{1,0:T(8,128)(2,1)S(1)}, u32[]{:S(2)}, u32[]{:S(2)}) collective-permute-start(bf16[272,512]{1,0:T(8,128)(2,1)S(1)} %slice.33), channel_id=1, source_target_pairs={{0,8},{1,9},{2,10},{3,11},{4,12},{5,13},{6,14},{7,15},{8,0},{9,1},... | collective-permute-start | bytes 835592 | tf_op jit(solution)/shard_map/ppermute | solution.py:150
  21.4 0.0 copy-start.2
  21.4 0.0 copy-start.3
  21.4 0.0 collective-permute-done.4.rest_1_
  21.4 0.0 copy-done
  21.5 2.8 %collective-permute-done.2.refs_3_ = bf16[272,512]{1,0:T(8,128)(2,1)S(1)} collective-permute-done((bf16[272,512]{1,0:T(8,128)(2,1)S(1)}, bf16[272,512]{1,0:T(8,128)(2,1)S(1)}, u32[]{:S(2)}, u32[]{:S(2)}) %collective-permute-start.2) | collective-permute-done | bytes 278560 | tf_op jit(solution)/shard_map/ppermute | solution.py:150
  24.3 0.0 copy-done.2
  24.3 0.0 copy-done.3
  24.3 0.7 %sums.2 = (bf16[128,256]{1,0:T(8,128)(2,1)S(1)}, bf16[128,256]{1,0:T(8,128)(2,1)S(1)}, bf16[128,256]{1,0:T(8,128)(2,1)S(1)}, bf16[128,256]{1,0:T(8,128)(2,1)S(1)}) custom-call(bf16[272,512]{1,0:T(8,128)(2,1)S(1)} %copy-done.2, bf16[544,512]{1,0:T(8,128)(2,1)S(1)} %collective-permute-done.refs_1_, bf16[272,512]{1,0:T(8,128)(2,1)S(1)} %collective-permute-done.1.refs_2_, ...), custom_call_target="tpu_custom_call" | custom-call | tf_op jit(solution)/shard_map/sums/pallas_call | solution.py:123
  25.1 2.9 %collective-permute-start.5 = (bf16[128,256]{1,0:T(8,128)(2,1)S(1)}, bf16[128,256]{1,0:T(8,128)(2,1)S(1)}, u32[]{:S(2)}, u32[]{:S(2)}) collective-permute-start(bf16[128,256]{1,0:T(8,128)(2,1)S(1)} %get-tuple-element.22.refs_5_), channel_id=1, source_target_pairs={{0,16},{1,17},{2,18},{3,19},{4,20},{5,21},{6,22},{7,23},{8,24},{9,... | collective-permute-start | bytes 196616 | tf_op jit(solution)/shard_map/ppermute | solution.py:150
  27.9 1.3 %collective-permute-start.6 = (bf16[128,256]{1,0:T(8,128)(2,1)S(1)}, bf16[128,256]{1,0:T(8,128)(2,1)S(1)}, u32[]{:S(2)}, u32[]{:S(2)}) collective-permute-start(bf16[128,256]{1,0:T(8,128)(2,1)S(1)} %get-tuple-element.23), channel_id=1, source_target_pairs={{0,18},{1,19},{2,16},{3,17},{4,22},{5,23},{6,20},{7,21},{8,26},{9,... | collective-permute-start | bytes 196616 | tf_op jit(solution)/shard_map/ppermute | solution.py:150
  29.2 0.0 collective-permute-done.7
  29.2 0.0 copy-start.1
  29.2 0.3 collective-permute-start.8
  29.6 0.0 collective-permute-done.9.refs_2_
  29.6 3.0 %collective-permute-done.10.refs_3_ = bf16[272,512]{1,0:T(8,128)(2,1)S(1)} collective-permute-done((bf16[272,512]{1,0:T(8,128)(2,1)S(1)}, bf16[272,512]{1,0:T(8,128)(2,1)S(1)}, u32[]{:S(2)}, u32[]{:S(2)}) %collective-permute-start.10) | collective-permute-done | bytes 278560 | tf_op jit(solution)/shard_map/ppermute | solution.py:150
  32.5 0.0 copy-done.1
  32.5 0.7 %sums.3 = (bf16[128,256]{1,0:T(8,128)(2,1)S(1)}, bf16[128,256]{1,0:T(8,128)(2,1)S(1)}, bf16[128,256]{1,0:T(8,128)(2,1)S(1)}, bf16[128,256]{1,0:T(8,128)(2,1)S(1)}) custom-call(bf16[272,512]{1,0:T(8,128)(2,1)S(1)} %copy-done.1, bf16[544,512]{1,0:T(8,128)(2,1)S(1)} %collective-permute-done.refs_1_, bf16[272,512]{1,0:T(8,128)(2,1)S(1)} %collective-permute-done.9.refs_2_, ...), custom_call_target="tpu_custom_call" | custom-call | tf_op jit(solution)/shard_map/sums/pallas_call | solution.py:123
  33.3 1.6 %collective-permute-start.11 = (bf16[128,256]{1,0:T(8,128)(2,1)S(1)}, bf16[128,256]{1,0:T(8,128)(2,1)S(1)}, u32[]{:S(2)}, u32[]{:S(2)}) collective-permute-start(bf16[128,256]{1,0:T(8,128)(2,1)S(1)} %get-tuple-element.27), channel_id=1, source_target_pairs={{0,16},{1,17},{2,18},{3,19},{4,20},{5,21},{6,22},{7,23},{8,24},{9,... | collective-permute-start | bytes 196616 | tf_op jit(solution)/shard_map/ppermute | solution.py:150
  34.9 2.1 %collective-permute-start.12 = (bf16[128,256]{1,0:T(8,128)(2,1)S(1)}, bf16[128,256]{1,0:T(8,128)(2,1)S(1)}, u32[]{:S(2)}, u32[]{:S(2)}) collective-permute-start(bf16[128,256]{1,0:T(8,128)(2,1)S(1)} %get-tuple-element.28), channel_id=1, source_target_pairs={{0,18},{1,19},{2,16},{3,17},{4,22},{5,23},{6,20},{7,21},{8,26},{9,... | collective-permute-start | bytes 196616 | tf_op jit(solution)/shard_map/ppermute | solution.py:150
  37.0 0.0 collective-permute-done.5.refs_0_
  37.0 0.8 %collective-permute-start.13 = (bf16[128,256]{1,0:T(8,128)(2,1)S(1)}, bf16[128,256]{1,0:T(8,128)(2,1)S(1)}, u32[]{:S(2)}, u32[]{:S(2)}) collective-permute-start(bf16[128,256]{1,0:T(8,128)(2,1)S(1)} %get-tuple-element.30), channel_id=1, source_target_pairs={{0,2},{1,3},{2,0},{3,1},{4,6},{5,7},{6,4},{7,5},{8,10},{9,11},{10,... | collective-permute-start | bytes 196616 | tf_op jit(solution)/shard_map/ppermute | solution.py:150
  37.7 0.0 collective-permute-done.6.refs_2_
  37.8 0.0 collective-permute-done.8.refs_6_
  37.8 0.3 virtual_first.1.before
  38.1 1.5 %collective-permute-done.11.refs_0_ = bf16[128,256]{1,0:T(8,128)(2,1)S(1)} collective-permute-done((bf16[128,256]{1,0:T(8,128)(2,1)S(1)}, bf16[128,256]{1,0:T(8,128)(2,1)S(1)}, u32[]{:S(2)}, u32[]{:S(2)}) %collective-permute-start.11) | collective-permute-done | bytes 65568 | tf_op jit(solution)/shard_map/ppermute | solution.py:150
  39.5 1.5 %collective-permute-done.12.refs_2_ = bf16[128,256]{1,0:T(8,128)(2,1)S(1)} collective-permute-done((bf16[128,256]{1,0:T(8,128)(2,1)S(1)}, bf16[128,256]{1,0:T(8,128)(2,1)S(1)}, u32[]{:S(2)}, u32[]{:S(2)}) %collective-permute-start.12) | collective-permute-done | bytes 65568 | tf_op jit(solution)/shard_map/ppermute | solution.py:150
  41.0 0.7 %collective-permute-done.13.refs_6_ = bf16[128,256]{1,0:T(8,128)(2,1)S(1)} collective-permute-done((bf16[128,256]{1,0:T(8,128)(2,1)S(1)}, bf16[128,256]{1,0:T(8,128)(2,1)S(1)}, u32[]{:S(2)}, u32[]{:S(2)}) %collective-permute-start.13) | collective-permute-done | bytes 65568 | tf_op jit(solution)/shard_map/ppermute | solution.py:150
  41.7 0.3 virtual_last.1
  42.0 0.1 collective-permute-start.14
  42.1 1.2 %collective-permute-done.14 = f32[32,256]{1,0:T(8,128)S(1)} collective-permute-done((f32[32,256]{1,0:T(8,128)S(1)}, f32[32,256]{1,0:T(8,128)S(1)}, u32[]{:S(2)}, u32[]{:S(2)}) %collective-permute-start.14) | collective-permute-done | bytes 32800 | tf_op jit(solution)/shard_map/ppermute | solution.py:150
  43.2 0.6 %add_bitcast_fusion = f32[1,32,256]{2,1,0:T(8,128)} fusion(f32[32,256]{1,0:T(8,128)S(1)} %get-tuple-element.31, f32[32,256]{1,0:T(8,128)S(1)} %collective-permute-done.14), kind=kLoop, calls=%fused_computation.2 | loop fusion | flops 8192 | bytes 98304 | tf_op jit(solution)/shard_map/broadcast_in_dim | solution.py:226
  (4 shorter events, 0.1 us)
Async XLA Ops:
  0.0 7.1 %copy-start.4 = (bf16[1,4,256,256]{3,2,1,0:T(8,128)(2,1)S(1)}, bf16[1,4,256,256]{3,2,1,0:T(8,128)(2,1)}, u32[]{:S(2)}) copy-start(bf16[1,4,256,256]{3,2,1,0:T(8,128)(2,1)} %param.7) | copy-start | bytes 1572868
  2.4 16.4 %collective-permute-start = (bf16[544,512]{1,0:T(8,128)(2,1)}, bf16[544,512]{1,0:T(8,128)(2,1)S(1)}, u32[]{:S(2)}, u32[]{:S(2)}) collective-permute-start(bf16[544,512]{1,0:T(8,128)(2,1)} %get-tuple-element.20), channel_id=1, source_target_pairs={{0,4},{1,5},{2,6},{3,7},{4,0},{5,1},{6,2},{7,3},{8,12},{9,13},{10,... | collective-permute-start | bytes 1671176 | tf_op jit(solution)/shard_map/ppermute | solution.py:150
  5.5 11.2 %collective-permute-start.1 = (bf16[272,512]{1,0:T(8,128)(2,1)}, bf16[272,512]{1,0:T(8,128)(2,1)S(1)}, u32[]{:S(2)}, u32[]{:S(2)}) collective-permute-start(bf16[272,512]{1,0:T(8,128)(2,1)} %get-tuple-element.19.refs_0_), channel_id=1, source_target_pairs={{0,8},{1,9},{2,10},{3,11},{4,12},{5,13},{6,14},{7,15},{8,0},{9,1},... | collective-permute-start | bytes 835592 | tf_op jit(solution)/shard_map/ppermute | solution.py:150
  7.1 22.1 %collective-permute-start.7 = (bf16[4,256,256]{2,1,0:T(8,128)(2,1)S(1)}, bf16[4,256,256]{2,1,0:T(8,128)(2,1)S(1)}, u32[]{:S(2)}, u32[]{:S(2)}) collective-permute-start(bf16[4,256,256]{2,1,0:T(8,128)(2,1)S(1)} %bitcast.8), channel_id=1, source_target_pairs={{0,2},{1,3},{2,0},{3,1},{4,6},{5,7},{6,4},{7,5},{8,10},{9,11},{10,... | collective-permute-start | bytes 1572872 | tf_op jit(solution)/shard_map/ppermute | solution.py:150
  8.5 8.8 %collective-permute-start.3 = (bf16[256,256]{1,0:T(8,128)(2,1)}, bf16[256,256]{1,0:T(8,128)(2,1)S(1)}, u32[]{:S(2)}, u32[]{:S(2)}) collective-permute-start(bf16[256,256]{1,0:T(8,128)(2,1)} %get-tuple-element.21.refs_5_), channel_id=1, source_target_pairs={{0,16},{1,17},{2,18},{3,19},{4,20},{5,21},{6,22},{7,23},{8,24},{9,... | collective-permute-start | bytes 393224 | tf_op jit(solution)/shard_map/ppermute | solution.py:150
  16.6 7.7 %collective-permute-start.2 = (bf16[272,512]{1,0:T(8,128)(2,1)S(1)}, bf16[272,512]{1,0:T(8,128)(2,1)S(1)}, u32[]{:S(2)}, u32[]{:S(2)}) collective-permute-start(bf16[272,512]{1,0:T(8,128)(2,1)S(1)} %collective-permute-done.1.refs_2_), channel_id=1, source_target_pairs={{0,4},{1,5},{2,6},{3,7},{4,0},{5,1},{6,2},{7,3},{8,12},{9,13},{10,... | collective-permute-start | bytes 835592 | tf_op jit(solution)/shard_map/ppermute | solution.py:150
  17.0 12.6 %collective-permute-start.9 = (bf16[272,512]{1,0:T(8,128)(2,1)}, bf16[272,512]{1,0:T(8,128)(2,1)S(1)}, u32[]{:S(2)}, u32[]{:S(2)}) collective-permute-start(bf16[272,512]{1,0:T(8,128)(2,1)} %get-tuple-element.26.refs_0_), channel_id=1, source_target_pairs={{0,8},{1,9},{2,10},{3,11},{4,12},{5,13},{6,14},{7,15},{8,0},{9,1},... | collective-permute-start | bytes 835592 | tf_op jit(solution)/shard_map/ppermute | solution.py:150
  17.3 4.1 %collective-permute-start.4 = (bf16[256,256]{1,0:T(8,128)(2,1)S(1)}, bf16[256,256]{1,0:T(8,128)(2,1)S(1)}, u32[]{:S(2)}, u32[]{:S(2)}) collective-permute-start(bf16[256,256]{1,0:T(8,128)(2,1)S(1)} %collective-permute-done.3.rest_0_), channel_id=1, source_target_pairs={{0,1},{1,0},{2,3},{3,2},{4,5},{5,4},{6,7},{7,6},{8,9},{9,8},{10,11... | collective-permute-start | bytes 393224 | tf_op jit(solution)/shard_map/ppermute | solution.py:150
  18.8 2.6 %copy-start = (bf16[512,256]{1,0:T(8,128)(2,1)S(1)}, bf16[512,256]{1,0:T(8,128)(2,1)}, u32[]{:S(2)}) copy-start(bf16[512,256]{1,0:T(8,128)(2,1)} %own.1) | copy-start | bytes 786436
  18.9 13.7 %collective-permute-start.10 = (bf16[272,512]{1,0:T(8,128)(2,1)S(1)}, bf16[272,512]{1,0:T(8,128)(2,1)S(1)}, u32[]{:S(2)}, u32[]{:S(2)}) collective-permute-start(bf16[272,512]{1,0:T(8,128)(2,1)S(1)} %slice.33), channel_id=1, source_target_pairs={{0,8},{1,9},{2,10},{3,11},{4,12},{5,13},{6,14},{7,15},{8,0},{9,1},... | collective-permute-start | bytes 835592 | tf_op jit(solution)/shard_map/ppermute | solution.py:150
  21.4 2.9 %copy-start.2 = (bf16[272,512]{1,0:T(8,128)(2,1)S(1)}, bf16[272,512]{1,0:T(8,128)(2,1)}, u32[]{:S(2)}) copy-start(bf16[272,512]{1,0:T(8,128)(2,1)} %get-tuple-element.19.refs_0_) | copy-start | bytes 835588
  21.4 2.9 %copy-start.3 = (bf16[256,256]{1,0:T(8,128)(2,1)S(1)}, bf16[256,256]{1,0:T(8,128)(2,1)}, u32[]{:S(2)}) copy-start(bf16[256,256]{1,0:T(8,128)(2,1)} %get-tuple-element.21.refs_5_) | copy-start | bytes 393220
  25.1 11.9 %collective-permute-start.5 = (bf16[128,256]{1,0:T(8,128)(2,1)S(1)}, bf16[128,256]{1,0:T(8,128)(2,1)S(1)}, u32[]{:S(2)}, u32[]{:S(2)}) collective-permute-start(bf16[128,256]{1,0:T(8,128)(2,1)S(1)} %get-tuple-element.22.refs_5_), channel_id=1, source_target_pairs={{0,16},{1,17},{2,18},{3,19},{4,20},{5,21},{6,22},{7,23},{8,24},{9,... | collective-permute-start | bytes 196616 | tf_op jit(solution)/shard_map/ppermute | solution.py:150
  27.9 9.8 %collective-permute-start.6 = (bf16[128,256]{1,0:T(8,128)(2,1)S(1)}, bf16[128,256]{1,0:T(8,128)(2,1)S(1)}, u32[]{:S(2)}, u32[]{:S(2)}) collective-permute-start(bf16[128,256]{1,0:T(8,128)(2,1)S(1)} %get-tuple-element.23), channel_id=1, source_target_pairs={{0,18},{1,19},{2,16},{3,17},{4,22},{5,23},{6,20},{7,21},{8,26},{9,... | collective-permute-start | bytes 196616 | tf_op jit(solution)/shard_map/ppermute | solution.py:150
  29.2 3.3 %copy-start.1 = (bf16[272,512]{1,0:T(8,128)(2,1)S(1)}, bf16[272,512]{1,0:T(8,128)(2,1)}, u32[]{:S(2)}) copy-start(bf16[272,512]{1,0:T(8,128)(2,1)} %get-tuple-element.26.refs_0_) | copy-start | bytes 835588
  29.2 8.6 %collective-permute-start.8 = (bf16[128,256]{1,0:T(8,128)(2,1)S(1)}, bf16[128,256]{1,0:T(8,128)(2,1)S(1)}, u32[]{:S(2)}, u32[]{:S(2)}) collective-permute-start(bf16[128,256]{1,0:T(8,128)(2,1)S(1)} %get-tuple-element.25), channel_id=1, source_target_pairs={{0,2},{1,3},{2,0},{3,1},{4,6},{5,7},{6,4},{7,5},{8,10},{9,11},{10,... | collective-permute-start | bytes 196616 | tf_op jit(solution)/shard_map/ppermute | solution.py:150
  33.3 6.3 %collective-permute-start.11 = (bf16[128,256]{1,0:T(8,128)(2,1)S(1)}, bf16[128,256]{1,0:T(8,128)(2,1)S(1)}, u32[]{:S(2)}, u32[]{:S(2)}) collective-permute-start(bf16[128,256]{1,0:T(8,128)(2,1)S(1)} %get-tuple-element.27), channel_id=1, source_target_pairs={{0,16},{1,17},{2,18},{3,19},{4,20},{5,21},{6,22},{7,23},{8,24},{9,... | collective-permute-start | bytes 196616 | tf_op jit(solution)/shard_map/ppermute | solution.py:150
  34.9 6.1 %collective-permute-start.12 = (bf16[128,256]{1,0:T(8,128)(2,1)S(1)}, bf16[128,256]{1,0:T(8,128)(2,1)S(1)}, u32[]{:S(2)}, u32[]{:S(2)}) collective-permute-start(bf16[128,256]{1,0:T(8,128)(2,1)S(1)} %get-tuple-element.28), channel_id=1, source_target_pairs={{0,18},{1,19},{2,16},{3,17},{4,22},{5,23},{6,20},{7,21},{8,26},{9,... | collective-permute-start | bytes 196616 | tf_op jit(solution)/shard_map/ppermute | solution.py:150
  37.0 4.7 %collective-permute-start.13 = (bf16[128,256]{1,0:T(8,128)(2,1)S(1)}, bf16[128,256]{1,0:T(8,128)(2,1)S(1)}, u32[]{:S(2)}, u32[]{:S(2)}) collective-permute-start(bf16[128,256]{1,0:T(8,128)(2,1)S(1)} %get-tuple-element.30), channel_id=1, source_target_pairs={{0,2},{1,3},{2,0},{3,1},{4,6},{5,7},{6,4},{7,5},{8,10},{9,11},{10,... | collective-permute-start | bytes 196616 | tf_op jit(solution)/shard_map/ppermute | solution.py:150
  42.0 1.3 %collective-permute-start.14 = (f32[32,256]{1,0:T(8,128)S(1)}, f32[32,256]{1,0:T(8,128)S(1)}, u32[]{:S(2)}, u32[]{:S(2)}) collective-permute-start(f32[32,256]{1,0:T(8,128)S(1)} %get-tuple-element.32), channel_id=1, source_target_pairs={{0,1},{1,0},{2,3},{3,2},{4,5},{5,4},{6,7},{7,6},{8,9},{9,8},{10,11... | collective-permute-start | bytes 98312 | tf_op jit(solution)/shard_map/ppermute | solution.py:150

commit v6 on v5

--- a/solution.py
+++ b/solution.py
@@ -7,12 +7,10 @@
 
 AXES = ("grid", "rep")
 KERNEL_VMEM = 16 << 20
-PACK_VMEM = 56 << 20
 SQUARE = 4
 CHUNK = 2
 VMEM = pl.BlockSpec(memory_space=pltpu.VMEM)
 ANY = pl.BlockSpec(memory_space=pl.ANY)
-HBM = pl.BlockSpec(memory_space=pltpu.HBM)
 
 
 def position():
@@ -20,37 +18,9 @@
     return lax.axis_index("grid"), rep // 2, rep % 2
 
 
-def pack_kernel(picks, listed, integrals, green, half_green, *rest):
-    whole, *messages, names, done = rest
+def half_kernel(green, half_green):
     half = half_green.shape[0]
-    size = messages[0].shape[0]
-    tile_rows = integrals.shape[0] // len(messages)
-    label_rows = size - tile_rows
-    start = pl.multiple_of(position()[2] * half, half)
-    copies = [
-        pltpu.make_async_copy(listed, names, done.at[0]),
-        pltpu.make_async_copy(green.at[pl.ds(start, half), :], half_green, done.at[1]),
-    ]
-    for m, message in enumerate(messages):
-        tiles = integrals.at[m * tile_rows : (m + 1) * tile_rows, :]
-        copies.append(pltpu.make_async_copy(tiles, message.at[label_rows:, :], done.at[2 * m + 2]))
-        place = whole.at[m * size + label_rows : (m + 1) * size, :]
-        copies.append(pltpu.make_async_copy(tiles, place, done.at[2 * m + 3]))
-    for copy in copies:
-        copy.start()
-    copies[0].wait()
-    line = lax.broadcasted_iota(jnp.int32, (label_rows, messages[0].shape[1]), 0)
-    for m, message in enumerate(messages):
-        value = jnp.full(line.shape, -1, jnp.int32)
-        for n in range(CHUNK):
-            for s in range(picks):
-                tile = m * CHUNK + n
-                value = jnp.where(line == n * picks + s, names[s : s + 1, tile : tile + 1], value)
-        labels = value.astype(jnp.float32).astype(message.dtype)
-        message[:label_rows, :] = labels
-        whole[m * size : m * size + label_rows, :] = labels
-    for copy in copies[1:]:
-        copy.wait()
+    half_green[...] = green[pl.ds(pl.multiple_of(position()[2] * half, half), half), :]
 
 
 def join_kernel(own, *rest):
@@ -64,28 +34,43 @@
             panels[n, pl.ds(start, half), :] = array[...]
 
 
-def sums_kernel(picks, fars, chunk, own, first, second, corner, panels, after, *rest):
+def add_products(picks, panel, green, sources, rows, sums):
+    wanted, width = panel.astype(jnp.float32), green.shape[1]
+    result = list(sums)
+    for source, start, size in sources:
+        labels = size - CHUNK * rows
+        names = source[start : start + labels, :width].astype(jnp.float32)
+        for n in range(CHUNK):
+            named = (names[n * picks : (n + 1) * picks] == wanted).astype(jnp.float32)
+            tile = source[start + labels + n * rows : start + labels + (n + 1) * rows, :]
+            product = jnp.dot(tile, green, preferred_element_type=jnp.float32)
+            product = (product * jnp.max(named, axis=0, keepdims=True)).astype(jnp.bfloat16)
+            result[n] = result[n] + product.astype(jnp.float32)
+    return result
+
+
+def near_kernel(picks, chunk, own, first, second, green, total):
+    rows, size = total.shape[1], own.shape[0]
+    sources = [(own, 0, size), (first, chunk * size, size), (second, 0, size)]
+    zeros = [jnp.zeros(total.shape[1:], jnp.float32)] * CHUNK
+    for n, sums in enumerate(add_products(picks, position()[0], green[...], sources, rows, zeros)):
+        total[n] = sums
+
+
+def sums_kernel(picks, fars, chunk, own, first, second, corner, panels, near, after, *rest):
     *messages, total = rest
     pairs = len(messages) // len(fars)
     share = messages[0].shape[0] // CHUNK
-    rows, width = share * pairs, panels.shape[2]
-    labels = own.shape[0] - CHUNK * rows
+    rows, width, size = share * pairs, panels.shape[2], own.shape[0]
     place, x, _ = position()
-    sources = [(own, 0), (first, chunk * own.shape[0]), (second, 0), (corner, 0)]
-    names = [source[at : at + labels, :width].astype(jnp.float32) for source, at in sources]
+    every = [(own, 0, size), (first, chunk * size, size), (second, 0, size), (corner, 0, size)]
     for p, far in enumerate(fars):
-        wanted = (place ^ far).astype(jnp.float32)
-        green = panels[p]
-        for n in range(CHUNK):
-            sums = jnp.zeros((rows, width), jnp.float32)
-            for (source, at), name in zip(sources, names):
-                named = (name[n * picks : (n + 1) * picks] == wanted).astype(jnp.float32)
-                hit = jnp.max(named, axis=0, keepdims=True)
-                start = at + labels + n * rows
-                tile = source[start : start + rows, :]
-                product = jnp.dot(tile, green, preferred_element_type=jnp.float32) * hit
-                sums = sums + product.astype(jnp.bfloat16).astype(jnp.float32)
-            total[n] = sums
+        if far:
+            sums, sources = [jnp.zeros((rows, width), jnp.float32)] * CHUNK, every
+        else:
+            sums, sources = [near[n] for n in range(CHUNK)], every[-1:]
+        for n, one in enumerate(add_products(picks, place ^ far, panels[p], sources, rows, sums)):
+            total[n] = one
         for t in range(pairs):
             start = pl.multiple_of((x ^ t) * share, share)
             for n in range(CHUNK):
@@ -118,7 +103,7 @@
     leaves[...] = total[pl.ds(pl.multiple_of((1 - core) * middle, middle), middle), :]
 
 
-def call(kernel, name, out, specs, flops, scratch=(), vmem=KERNEL_VMEM):
+def call(kernel, name, out, specs, flops, scratch=()):
     def run(*operands):
         return pl.pallas_call(
             kernel,
@@ -127,7 +112,7 @@
             out_specs=jax.tree.map(lambda _: VMEM, out),
             scratch_shapes=scratch,
             cost_estimate=pl.CostEstimate(flops=flops, bytes_accessed=0, transcendentals=0),
-            compiler_params=pltpu.CompilerParams(vmem_limit_bytes=vmem),
+            compiler_params=pltpu.CompilerParams(vmem_limit_bytes=KERNEL_VMEM),
             name=name,
         )(*operands)
 
@@ -154,17 +139,16 @@
 
     label_rows = -(-CHUNK * picks // 16) * 16
     chunks = range(tile_count // CHUNK)
-    half = green_occ.shape[0] // 2
-    outs = [like((half, green_occ.shape[1]), green_occ.dtype)]
     size = label_rows + CHUNK * rows
-    outs.append(like((len(chunks) * size, depth), integrals.dtype))
-    outs += [like((size, depth), integrals.dtype) for _ in chunks]
-    scratch = [
-        pltpu.VMEM((picks, tile_count), jnp.int32),
-        pltpu.SemaphoreType.DMA((2 + 2 * len(chunks),)),
-    ]
-    pack = call(lambda *refs: pack_kernel(picks, *refs), "pack", outs, [HBM] * 3, 0, scratch, PACK_VMEM)
-    mine, whole, *own = pack(tile_panels.T, integrals, green_occ)
+    half = like((green_occ.shape[0] // 2, green_occ.shape[1]), green_occ.dtype)
+    mine = call(half_kernel, "half", half, [VMEM], 0)(green_occ)
+    blocks = integrals.reshape(len(chunks), CHUNK * rows, depth)
+    named = tile_panels.reshape(len(chunks), CHUNK * picks, 1).astype(jnp.bfloat16)
+    named = jnp.pad(named, ((0, 0), (0, label_rows - CHUNK * picks), (0, 0)), constant_values=-1)
+    named = jnp.broadcast_to(named, (len(chunks), label_rows, depth))
+    whole = jnp.concatenate([named, blocks], axis=1)
+    own = [whole[n] for n in chunks]
+    whole = whole.reshape(len(chunks) * size, depth)
 
     near = [n % 2 == 1 for n in chunks]
     first = send(whole, 1)
@@ -196,11 +180,15 @@
             lambda *refs, n=n: sums_kernel(picks, fars, n, *refs),
             "sums",
             outs,
-            [VMEM] * 5 + [ANY],
+            [VMEM] * 6 + [ANY],
             0,
             [pltpu.VMEM((CHUNK, rows, width), jnp.float32)],
         )
-        parts = sums(own[n], first, second[n], corner[n], panels, after)
+        near_shape = like((CHUNK, rows, width), jnp.float32)
+        part = call(
+            lambda *refs, n=n: near_kernel(picks, n, *refs), "near", near_shape, [VMEM] * 4, 0
+        )(own[n], first, second[n], green_occ)
+        parts = sums(own[n], first, second[n], corner[n], panels, part, after)
         after = parts[0]
         operands[n] = []
         for p, far in enumerate(fars):

time: 44 us -> 43.2 us (0.982)
  Pallas kernels: 4.56 us -> 2.51 us
  other arithmetic: 0.62 us -> 2.49 us
  waiting for transfers between devices: 17.6 us -> 16.4 us
    pallas_call x6 -> x8, Pallas kernels: 4.56 us -> 2.51 us  [run(): pl.pallas_call(kernel, out_shape=out, in_specs=specs, out_specs=jax.tree....]
    ppermute x15, waiting for transfers between devices: 17.6 us -> 16.4 us  [send(): return lax.ppermute(array, AXES, order)]
    concatenate x0 -> x1, other arithmetic: none -> 1.15 us  [shards(): whole = jnp.concatenate([named, blocks], axis=1)]
    convert_element_type x0 -> x1, other arithmetic: none -> 0.68 us  [shards(): tile_panels.reshape(len(chunks), CHUNK * picks, 1).astype(jnp.bfloat16)]
  transfers between devices with their start and end apart: 15 -> 15, of which waited for: 8 -> 9; matrix products, arithmetic and copies ran while one was open for 0% -> 0% of each run, Pallas kernels for 4% -> 5%
where the time goes in v6:
time: 43.2 us; the launch traced here: 43 us
  starting transfers between devices  21.1 us (49%)
  waiting for transfers between devices  16.4 us (38%)
  Pallas kernels  2.51 us (6%)
  other arithmetic  2.49 us (6%)
    ppermute x15, starting transfers between devices, send(): return lax.ppermute(array, AXES, order)  21.1 us
    ppermute x15, waiting for transfers between devices, send(): return lax.ppermute(array, AXES, order)  16.4 us
    pallas_call x8, Pallas kernels, run(): pl.pallas_call(kernel, out_shape=out, in_specs=specs, out_specs=jax.tree....  2.51 us
    concatenate x1, other arithmetic, shards(): whole = jnp.concatenate([named, blocks], axis=1)  1.15 us
  transfers between devices with their start and end apart: 15, of which 9 were waited for; matrix products, arithmetic and copies ran while one was open for 0% of the time, Pallas kernels for 5%

profile of v6, /device:TPU:0, one launch (start us, length us, event | category | flops | bytes accessed | tf_op | source)
XLA Modules:
  0.0 43.0 jit_solution(2771920366354449122)
XLA Ops:
  0.0 0.7 %convert_element_type.16 = bf16[4,2]{0,1:T(2,128)(2,1)S(1)} convert(s32[4,2]{0,1:T(2,128)} %param.6) | non-fusion elementwise | flops 8 | bytes 48 | tf_op jit(solution)/shard_map/convert_element_type | solution.py:146
  0.7 0.1 copy.6
  0.8 0.1 convert_element_type.17
  0.9 0.1 broadcast_in_dim.11
  1.0 0.0 copy-start.1
  1.0 1.2 %pad_maximum_fusion = bf16[2,272,512]{2,1,0:T(8,128)(2,1)S(1)} fusion(bf16[2,16,512]{2,1,0:T(8,128)(2,1)S(1)} %broadcast_in_dim.11, bf16[2,256,512]{2,1,0:T(8,128)(2,1)} %bitcast.15), kind=kLoop, calls=%fused_computation.2 | loop fusion | flops 1114112 | bytes 1114112 | tf_op jit(solution)/shard_map/concatenate | solution.py:149
  2.1 0.0 copy-start.2
  2.1 0.0 copy-start
  2.1 3.0 %collective-permute-start = (bf16[544,512]{1,0:T(8,128)(2,1)S(1)}, bf16[544,512]{1,0:T(8,128)(2,1)S(1)}, u32[]{:S(2)}, u32[]{:S(2)}) collective-permute-start(bf16[544,512]{1,0:T(8,128)(2,1)S(1)} %bitcast.17), channel_id=1, source_target_pairs={{0,4},{1,5},{2,6},{3,7},{4,0},{5,1},{6,2},{7,3},{8,12},{9,13},{10,... | collective-permute-start | bytes 1671176 | tf_op jit(solution)/shard_map/ppermute | solution.py:135
  5.2 0.0 copy-done.1
  5.2 1.6 %collective-permute-start.1 = (bf16[272,512]{1,0:T(8,128)(2,1)S(1)}, bf16[272,512]{1,0:T(8,128)(2,1)S(1)}, u32[]{:S(2)}, u32[]{:S(2)}) collective-permute-start(bf16[272,512]{1,0:T(8,128)(2,1)S(1)} %get-tuple-element.26.refs_0_), channel_id=1, source_target_pairs={{0,8},{1,9},{2,10},{3,11},{4,12},{5,13},{6,14},{7,15},{8,0},{9,1},... | collective-permute-start | bytes 835592 | tf_op jit(solution)/shard_map/ppermute | solution.py:135
  6.9 0.0 copy-done.2
  6.9 1.5 %collective-permute-start.7 = (bf16[4,256,256]{2,1,0:T(8,128)(2,1)S(1)}, bf16[4,256,256]{2,1,0:T(8,128)(2,1)S(1)}, u32[]{:S(2)}, u32[]{:S(2)}) collective-permute-start(bf16[4,256,256]{2,1,0:T(8,128)(2,1)S(1)} %bitcast.18), channel_id=1, source_target_pairs={{0,2},{1,3},{2,0},{3,1},{4,6},{5,7},{6,4},{7,5},{8,10},{9,11},{10,... | collective-permute-start | bytes 1572872 | tf_op jit(solution)/shard_map/ppermute | solution.py:135
  8.4 0.0 copy-done
  8.4 2.7 %collective-permute-start.3 = (bf16[256,256]{1,0:T(8,128)(2,1)S(1)}, bf16[256,256]{1,0:T(8,128)(2,1)S(1)}, u32[]{:S(2)}, u32[]{:S(2)}) collective-permute-start(bf16[256,256]{1,0:T(8,128)(2,1)S(1)} %half.1.refs_6_), channel_id=1, source_target_pairs={{0,16},{1,17},{2,18},{3,19},{4,20},{5,21},{6,22},{7,23},{8,24},{9,... | collective-permute-start | bytes 393224 | tf_op jit(solution)/shard_map/ppermute | solution.py:135
  11.0 5.2 %collective-permute-done.1.refs_2_ = bf16[272,512]{1,0:T(8,128)(2,1)S(1)} collective-permute-done((bf16[272,512]{1,0:T(8,128)(2,1)S(1)}, bf16[272,512]{1,0:T(8,128)(2,1)S(1)}, u32[]{:S(2)}, u32[]{:S(2)}) %collective-permute-start.1) | collective-permute-done | bytes 278560 | tf_op jit(solution)/shard_map/ppermute | solution.py:135
  16.2 0.3 collective-permute-start.2
  16.6 0.3 collective-permute-start.9
  16.9 0.0 collective-permute-done.3.rest_0_
  16.9 0.0 collective-permute-start.4
  16.9 1.3 %collective-permute-done.refs_1_ = bf16[544,512]{1,0:T(8,128)(2,1)S(1)} collective-permute-done((bf16[544,512]{1,0:T(8,128)(2,1)S(1)}, bf16[544,512]{1,0:T(8,128)(2,1)S(1)}, u32[]{:S(2)}, u32[]{:S(2)}) %collective-permute-start) | collective-permute-done | bytes 557088 | tf_op jit(solution)/shard_map/ppermute | solution.py:135
  18.2 2.6 %collective-permute-start.10 = (bf16[272,512]{1,0:T(8,128)(2,1)S(1)}, bf16[272,512]{1,0:T(8,128)(2,1)S(1)}, u32[]{:S(2)}, u32[]{:S(2)}) collective-permute-start(bf16[272,512]{1,0:T(8,128)(2,1)S(1)} %slice.45), channel_id=1, source_target_pairs={{0,8},{1,9},{2,10},{3,11},{4,12},{5,13},{6,14},{7,15},{8,0},{9,1},... | collective-permute-start | bytes 835592 | tf_op jit(solution)/shard_map/ppermute | solution.py:135
  20.9 0.0 collective-permute-done.4.rest_1_
  20.9 0.4 near.2.refs_5_
  21.3 2.5 %collective-permute-done.2.refs_3_ = bf16[272,512]{1,0:T(8,128)(2,1)S(1)} collective-permute-done((bf16[272,512]{1,0:T(8,128)(2,1)S(1)}, bf16[272,512]{1,0:T(8,128)(2,1)S(1)}, u32[]{:S(2)}, u32[]{:S(2)}) %collective-permute-start.2) | collective-permute-done | bytes 278560 | tf_op jit(solution)/shard_map/ppermute | solution.py:135
  23.8 0.5 %sums.2 = (bf16[128,256]{1,0:T(8,128)(2,1)S(1)}, bf16[128,256]{1,0:T(8,128)(2,1)S(1)}, bf16[128,256]{1,0:T(8,128)(2,1)S(1)}, bf16[128,256]{1,0:T(8,128)(2,1)S(1)}) custom-call(bf16[272,512]{1,0:T(8,128)(2,1)S(1)} %get-tuple-element.26.refs_0_, bf16[544,512]{1,0:T(8,128)(2,1)S(1)} %collective-permute-done.refs_1_, ...), custom_call_target="tpu_custom_call" | custom-call | tf_op jit(solution)/shard_map/sums/pallas_call | solution.py:108
  24.3 2.9 %collective-permute-start.5 = (bf16[128,256]{1,0:T(8,128)(2,1)S(1)}, bf16[128,256]{1,0:T(8,128)(2,1)S(1)}, u32[]{:S(2)}, u32[]{:S(2)}) collective-permute-start(bf16[128,256]{1,0:T(8,128)(2,1)S(1)} %get-tuple-element.15.refs_6_), channel_id=1, source_target_pairs={{0,16},{1,17},{2,18},{3,19},{4,20},{5,21},{6,22},{7,23},{8,24},{9,... | collective-permute-start | bytes 196616 | tf_op jit(solution)/shard_map/ppermute | solution.py:135
  27.2 1.3 %collective-permute-start.6 = (bf16[128,256]{1,0:T(8,128)(2,1)S(1)}, bf16[128,256]{1,0:T(8,128)(2,1)S(1)}, u32[]{:S(2)}, u32[]{:S(2)}) collective-permute-start(bf16[128,256]{1,0:T(8,128)(2,1)S(1)} %get-tuple-element.16), channel_id=1, source_target_pairs={{0,18},{1,19},{2,16},{3,17},{4,22},{5,23},{6,20},{7,21},{8,26},{9,... | collective-permute-start | bytes 196616 | tf_op jit(solution)/shard_map/ppermute | solution.py:135
  28.5 0.0 collective-permute-done.7
  28.5 0.3 collective-permute-start.8
  28.8 0.0 collective-permute-done.9.refs_2_
  28.8 0.4 near.3.refs_5_
  29.2 2.6 %collective-permute-done.10.refs_3_ = bf16[272,512]{1,0:T(8,128)(2,1)S(1)} collective-permute-done((bf16[272,512]{1,0:T(8,128)(2,1)S(1)}, bf16[272,512]{1,0:T(8,128)(2,1)S(1)}, u32[]{:S(2)}, u32[]{:S(2)}) %collective-permute-start.10) | collective-permute-done | bytes 278560 | tf_op jit(solution)/shard_map/ppermute | solution.py:135
  31.9 0.5 %sums.3 = (bf16[128,256]{1,0:T(8,128)(2,1)S(1)}, bf16[128,256]{1,0:T(8,128)(2,1)S(1)}, bf16[128,256]{1,0:T(8,128)(2,1)S(1)}, bf16[128,256]{1,0:T(8,128)(2,1)S(1)}) custom-call(bf16[272,512]{1,0:T(8,128)(2,1)S(1)} %get-tuple-element.25.refs_0_, bf16[544,512]{1,0:T(8,128)(2,1)S(1)} %collective-permute-done.refs_1_, ...), custom_call_target="tpu_custom_call" | custom-call | tf_op jit(solution)/shard_map/sums/pallas_call | solution.py:108
  32.4 1.6 %collective-permute-start.11 = (bf16[128,256]{1,0:T(8,128)(2,1)S(1)}, bf16[128,256]{1,0:T(8,128)(2,1)S(1)}, u32[]{:S(2)}, u32[]{:S(2)}) collective-permute-start(bf16[128,256]{1,0:T(8,128)(2,1)S(1)} %get-tuple-element.19), channel_id=1, source_target_pairs={{0,16},{1,17},{2,18},{3,19},{4,20},{5,21},{6,22},{7,23},{8,24},{9,... | collective-permute-start | bytes 196616 | tf_op jit(solution)/shard_map/ppermute | solution.py:135
  34.1 2.2 %collective-permute-start.12 = (bf16[128,256]{1,0:T(8,128)(2,1)S(1)}, bf16[128,256]{1,0:T(8,128)(2,1)S(1)}, u32[]{:S(2)}, u32[]{:S(2)}) collective-permute-start(bf16[128,256]{1,0:T(8,128)(2,1)S(1)} %get-tuple-element.20), channel_id=1, source_target_pairs={{0,18},{1,19},{2,16},{3,17},{4,22},{5,23},{6,20},{7,21},{8,26},{9,... | collective-permute-start | bytes 196616 | tf_op jit(solution)/shard_map/ppermute | solution.py:135
  36.3 0.0 collective-permute-done.5.refs_0_
  36.3 0.6 %collective-permute-start.13 = (bf16[128,256]{1,0:T(8,128)(2,1)S(1)}, bf16[128,256]{1,0:T(8,128)(2,1)S(1)}, u32[]{:S(2)}, u32[]{:S(2)}) collective-permute-start(bf16[128,256]{1,0:T(8,128)(2,1)S(1)} %get-tuple-element.22), channel_id=1, source_target_pairs={{0,2},{1,3},{2,0},{3,1},{4,6},{5,7},{6,4},{7,5},{8,10},{9,11},{10,... | collective-permute-start | bytes 196616 | tf_op jit(solution)/shard_map/ppermute | solution.py:135
  36.9 0.2 collective-permute-done.6.refs_2_
  37.1 0.0 collective-permute-done.8.refs_6_
  37.1 0.3 virtual_first.1.before
  37.4 1.3 %collective-permute-done.11.refs_0_ = bf16[128,256]{1,0:T(8,128)(2,1)S(1)} collective-permute-done((bf16[128,256]{1,0:T(8,128)(2,1)S(1)}, bf16[128,256]{1,0:T(8,128)(2,1)S(1)}, u32[]{:S(2)}, u32[]{:S(2)}) %collective-permute-start.11) | collective-permute-done | bytes 65568 | tf_op jit(solution)/shard_map/ppermute | solution.py:135
  38.7 1.4 %collective-permute-done.12.refs_2_ = bf16[128,256]{1,0:T(8,128)(2,1)S(1)} collective-permute-done((bf16[128,256]{1,0:T(8,128)(2,1)S(1)}, bf16[128,256]{1,0:T(8,128)(2,1)S(1)}, u32[]{:S(2)}, u32[]{:S(2)}) %collective-permute-start.12) | collective-permute-done | bytes 65568 | tf_op jit(solution)/shard_map/ppermute | solution.py:135
  40.1 0.7 %collective-permute-done.13.refs_6_ = bf16[128,256]{1,0:T(8,128)(2,1)S(1)} collective-permute-done((bf16[128,256]{1,0:T(8,128)(2,1)S(1)}, bf16[128,256]{1,0:T(8,128)(2,1)S(1)}, u32[]{:S(2)}, u32[]{:S(2)}) %collective-permute-start.13) | collective-permute-done | bytes 65568 | tf_op jit(solution)/shard_map/ppermute | solution.py:135
  40.8 0.3 virtual_last.1
  41.1 0.1 collective-permute-start.14
  41.2 1.2 %collective-permute-done.14 = f32[32,256]{1,0:T(8,128)S(1)} collective-permute-done((f32[32,256]{1,0:T(8,128)S(1)}, f32[32,256]{1,0:T(8,128)S(1)}, u32[]{:S(2)}, u32[]{:S(2)}) %collective-permute-start.14) | collective-permute-done | bytes 32800 | tf_op jit(solution)/shard_map/ppermute | solution.py:135
  42.4 0.6 %add_bitcast_fusion = f32[1,32,256]{2,1,0:T(8,128)} fusion(f32[32,256]{1,0:T(8,128)S(1)} %get-tuple-element.23, f32[32,256]{1,0:T(8,128)S(1)} %collective-permute-done.14), kind=kLoop, calls=%fused_computation.11 | loop fusion | flops 8192 | bytes 98304 | tf_op jit(solution)/shard_map/broadcast_in_dim | solution.py:214
  (7 shorter events, 0.2 us)
Async XLA Ops:
  1.0 4.2 %copy-start.1 = (bf16[512,512]{1,0:T(8,128)(2,1)S(1)}, bf16[512,512]{1,0:T(8,128)(2,1)}, u32[]{:S(2)}) copy-start(bf16[512,512]{1,0:T(8,128)(2,1)} %param.4) | copy-start | bytes 1572868
  2.1 4.7 %copy-start.2 = (bf16[1,4,256,256]{3,2,1,0:T(8,128)(2,1)S(1)}, bf16[1,4,256,256]{3,2,1,0:T(8,128)(2,1)}, u32[]{:S(2)}) copy-start(bf16[1,4,256,256]{3,2,1,0:T(8,128)(2,1)} %param.7) | copy-start | bytes 1572868
  2.1 6.2 %copy-start = (bf16[512,256]{1,0:T(8,128)(2,1)S(1)}, bf16[512,256]{1,0:T(8,128)(2,1)}, u32[]{:S(2)}) copy-start(bf16[512,256]{1,0:T(8,128)(2,1)} %refs_3_.3) | copy-start | bytes 786436
  2.1 16.1 %collective-permute-start = (bf16[544,512]{1,0:T(8,128)(2,1)S(1)}, bf16[544,512]{1,0:T(8,128)(2,1)S(1)}, u32[]{:S(2)}, u32[]{:S(2)}) collective-permute-start(bf16[544,512]{1,0:T(8,128)(2,1)S(1)} %bitcast.17), channel_id=1, source_target_pairs={{0,4},{1,5},{2,6},{3,7},{4,0},{5,1},{6,2},{7,3},{8,12},{9,13},{10,... | collective-permute-start | bytes 1671176 | tf_op jit(solution)/shard_map/ppermute | solution.py:135
  5.2 11.0 %collective-permute-start.1 = (bf16[272,512]{1,0:T(8,128)(2,1)S(1)}, bf16[272,512]{1,0:T(8,128)(2,1)S(1)}, u32[]{:S(2)}, u32[]{:S(2)}) collective-permute-start(bf16[272,512]{1,0:T(8,128)(2,1)S(1)} %get-tuple-element.26.refs_0_), channel_id=1, source_target_pairs={{0,8},{1,9},{2,10},{3,11},{4,12},{5,13},{6,14},{7,15},{8,0},{9,1},... | collective-permute-start | bytes 835592 | tf_op jit(solution)/shard_map/ppermute | solution.py:135
  6.9 21.6 %collective-permute-start.7 = (bf16[4,256,256]{2,1,0:T(8,128)(2,1)S(1)}, bf16[4,256,256]{2,1,0:T(8,128)(2,1)S(1)}, u32[]{:S(2)}, u32[]{:S(2)}) collective-permute-start(bf16[4,256,256]{2,1,0:T(8,128)(2,1)S(1)} %bitcast.18), channel_id=1, source_target_pairs={{0,2},{1,3},{2,0},{3,1},{4,6},{5,7},{6,4},{7,5},{8,10},{9,11},{10,... | collective-permute-start | bytes 1572872 | tf_op jit(solution)/shard_map/ppermute | solution.py:135
  8.4 8.5 %collective-permute-start.3 = (bf16[256,256]{1,0:T(8,128)(2,1)S(1)}, bf16[256,256]{1,0:T(8,128)(2,1)S(1)}, u32[]{:S(2)}, u32[]{:S(2)}) collective-permute-start(bf16[256,256]{1,0:T(8,128)(2,1)S(1)} %half.1.refs_6_), channel_id=1, source_target_pairs={{0,16},{1,17},{2,18},{3,19},{4,20},{5,21},{6,22},{7,23},{8,24},{9,... | collective-permute-start | bytes 393224 | tf_op jit(solution)/shard_map/ppermute | solution.py:135
  16.2 7.6 %collective-permute-start.2 = (bf16[272,512]{1,0:T(8,128)(2,1)S(1)}, bf16[272,512]{1,0:T(8,128)(2,1)S(1)}, u32[]{:S(2)}, u32[]{:S(2)}) collective-permute-start(bf16[272,512]{1,0:T(8,128)(2,1)S(1)} %collective-permute-done.1.refs_2_), channel_id=1, source_target_pairs={{0,4},{1,5},{2,6},{3,7},{4,0},{5,1},{6,2},{7,3},{8,12},{9,13},{10,... | collective-permute-start | bytes 835592 | tf_op jit(solution)/shard_map/ppermute | solution.py:135
  16.6 12.3 %collective-permute-start.9 = (bf16[272,512]{1,0:T(8,128)(2,1)S(1)}, bf16[272,512]{1,0:T(8,128)(2,1)S(1)}, u32[]{:S(2)}, u32[]{:S(2)}) collective-permute-start(bf16[272,512]{1,0:T(8,128)(2,1)S(1)} %get-tuple-element.25.refs_0_), channel_id=1, source_target_pairs={{0,8},{1,9},{2,10},{3,11},{4,12},{5,13},{6,14},{7,15},{8,0},{9,1},... | collective-permute-start | bytes 835592 | tf_op jit(solution)/shard_map/ppermute | solution.py:135
  16.9 4.0 %collective-permute-start.4 = (bf16[256,256]{1,0:T(8,128)(2,1)S(1)}, bf16[256,256]{1,0:T(8,128)(2,1)S(1)}, u32[]{:S(2)}, u32[]{:S(2)}) collective-permute-start(bf16[256,256]{1,0:T(8,128)(2,1)S(1)} %collective-permute-done.3.rest_0_), channel_id=1, source_target_pairs={{0,1},{1,0},{2,3},{3,2},{4,5},{5,4},{6,7},{7,6},{8,9},{9,8},{10,11... | collective-permute-start | bytes 393224 | tf_op jit(solution)/shard_map/ppermute | solution.py:135
  18.2 13.6 %collective-permute-start.10 = (bf16[272,512]{1,0:T(8,128)(2,1)S(1)}, bf16[272,512]{1,0:T(8,128)(2,1)S(1)}, u32[]{:S(2)}, u32[]{:S(2)}) collective-permute-start(bf16[272,512]{1,0:T(8,128)(2,1)S(1)} %slice.45), channel_id=1, source_target_pairs={{0,8},{1,9},{2,10},{3,11},{4,12},{5,13},{6,14},{7,15},{8,0},{9,1},... | collective-permute-start | bytes 835592 | tf_op jit(solution)/shard_map/ppermute | solution.py:135
  24.3 12.0 %collective-permute-start.5 = (bf16[128,256]{1,0:T(8,128)(2,1)S(1)}, bf16[128,256]{1,0:T(8,128)(2,1)S(1)}, u32[]{:S(2)}, u32[]{:S(2)}) collective-permute-start(bf16[128,256]{1,0:T(8,128)(2,1)S(1)} %get-tuple-element.15.refs_6_), channel_id=1, source_target_pairs={{0,16},{1,17},{2,18},{3,19},{4,20},{5,21},{6,22},{7,23},{8,24},{9,... | collective-permute-start | bytes 196616 | tf_op jit(solution)/shard_map/ppermute | solution.py:135
  27.2 9.9 %collective-permute-start.6 = (bf16[128,256]{1,0:T(8,128)(2,1)S(1)}, bf16[128,256]{1,0:T(8,128)(2,1)S(1)}, u32[]{:S(2)}, u32[]{:S(2)}) collective-permute-start(bf16[128,256]{1,0:T(8,128)(2,1)S(1)} %get-tuple-element.16), channel_id=1, source_target_pairs={{0,18},{1,19},{2,16},{3,17},{4,22},{5,23},{6,20},{7,21},{8,26},{9,... | collective-permute-start | bytes 196616 | tf_op jit(solution)/shard_map/ppermute | solution.py:135
  28.5 8.6 %collective-permute-start.8 = (bf16[128,256]{1,0:T(8,128)(2,1)S(1)}, bf16[128,256]{1,0:T(8,128)(2,1)S(1)}, u32[]{:S(2)}, u32[]{:S(2)}) collective-permute-start(bf16[128,256]{1,0:T(8,128)(2,1)S(1)} %get-tuple-element.18), channel_id=1, source_target_pairs={{0,2},{1,3},{2,0},{3,1},{4,6},{5,7},{6,4},{7,5},{8,10},{9,11},{10,... | collective-permute-start | bytes 196616 | tf_op jit(solution)/shard_map/ppermute | solution.py:135
  32.4 6.3 %collective-permute-start.11 = (bf16[128,256]{1,0:T(8,128)(2,1)S(1)}, bf16[128,256]{1,0:T(8,128)(2,1)S(1)}, u32[]{:S(2)}, u32[]{:S(2)}) collective-permute-start(bf16[128,256]{1,0:T(8,128)(2,1)S(1)} %get-tuple-element.19), channel_id=1, source_target_pairs={{0,16},{1,17},{2,18},{3,19},{4,20},{5,21},{6,22},{7,23},{8,24},{9,... | collective-permute-start | bytes 196616 | tf_op jit(solution)/shard_map/ppermute | solution.py:135
  34.1 6.1 %collective-permute-start.12 = (bf16[128,256]{1,0:T(8,128)(2,1)S(1)}, bf16[128,256]{1,0:T(8,128)(2,1)S(1)}, u32[]{:S(2)}, u32[]{:S(2)}) collective-permute-start(bf16[128,256]{1,0:T(8,128)(2,1)S(1)} %get-tuple-element.20), channel_id=1, source_target_pairs={{0,18},{1,19},{2,16},{3,17},{4,22},{5,23},{6,20},{7,21},{8,26},{9,... | collective-permute-start | bytes 196616 | tf_op jit(solution)/shard_map/ppermute | solution.py:135
  36.3 4.5 %collective-permute-start.13 = (bf16[128,256]{1,0:T(8,128)(2,1)S(1)}, bf16[128,256]{1,0:T(8,128)(2,1)S(1)}, u32[]{:S(2)}, u32[]{:S(2)}) collective-permute-start(bf16[128,256]{1,0:T(8,128)(2,1)S(1)} %get-tuple-element.22), channel_id=1, source_target_pairs={{0,2},{1,3},{2,0},{3,1},{4,6},{5,7},{6,4},{7,5},{8,10},{9,11},{10,... | collective-permute-start | bytes 196616 | tf_op jit(solution)/shard_map/ppermute | solution.py:135
  41.1 1.3 %collective-permute-start.14 = (f32[32,256]{1,0:T(8,128)S(1)}, f32[32,256]{1,0:T(8,128)S(1)}, u32[]{:S(2)}, u32[]{:S(2)}) collective-permute-start(f32[32,256]{1,0:T(8,128)S(1)} %get-tuple-element.24), channel_id=1, source_target_pairs={{0,1},{1,0},{2,3},{3,2},{4,5},{5,4},{6,7},{7,6},{8,9},{9,8},{10,11... | collective-permute-start | bytes 98312 | tf_op jit(solution)/shard_map/ppermute | solution.py:135

commit v7 on v6

--- a/solution.py
+++ b/solution.py
@@ -21,6 +21,10 @@
 def half_kernel(green, half_green):
     half = half_green.shape[0]
     half_green[...] = green[pl.ds(pl.multiple_of(position()[2] * half, half), half), :]
+
+
+def hold_kernel(array, after, held):
+    held[...] = array[...]
 
 
 def join_kernel(own, *rest):
@@ -34,42 +38,42 @@
             panels[n, pl.ds(start, half), :] = array[...]
 
 
-def add_products(picks, panel, green, sources, rows, sums):
-    wanted, width = panel.astype(jnp.float32), green.shape[1]
+def source_of(array, start, size, rows, tail=None):
+    labels = size - CHUNK * rows
+    if tail is not None:
+        labels = array.shape[0] - (CHUNK - 1) * rows
+    tiles = [(array, start + labels + n * rows) for n in range(CHUNK)]
+    if tail is not None:
+        tiles[-1] = (tail, 0)
+    return (array, start, labels), tiles
+
+
+def add_products(picks, panel, green, sources, sums):
+    wanted, width, rows = panel.astype(jnp.float32), green.shape[1], sums[0].shape[0]
     result = list(sums)
-    for source, start, size in sources:
-        labels = size - CHUNK * rows
-        names = source[start : start + labels, :width].astype(jnp.float32)
-        for n in range(CHUNK):
+    for (array, start, labels), tiles in sources:
+        names = array[start : start + labels, :width].astype(jnp.float32)
+        for n, (tile, at) in enumerate(tiles):
             named = (names[n * picks : (n + 1) * picks] == wanted).astype(jnp.float32)
-            tile = source[start + labels + n * rows : start + labels + (n + 1) * rows, :]
-            product = jnp.dot(tile, green, preferred_element_type=jnp.float32)
+            product = jnp.dot(tile[at : at + rows, :], green, preferred_element_type=jnp.float32)
             product = (product * jnp.max(named, axis=0, keepdims=True)).astype(jnp.bfloat16)
             result[n] = result[n] + product.astype(jnp.float32)
     return result
 
 
-def near_kernel(picks, chunk, own, first, second, green, total):
-    rows, size = total.shape[1], own.shape[0]
-    sources = [(own, 0, size), (first, chunk * size, size), (second, 0, size)]
-    zeros = [jnp.zeros(total.shape[1:], jnp.float32)] * CHUNK
-    for n, sums in enumerate(add_products(picks, position()[0], green[...], sources, rows, zeros)):
-        total[n] = sums
-
-
-def sums_kernel(picks, fars, chunk, own, first, second, corner, panels, near, after, *rest):
-    *messages, total = rest
+def sums_kernel(picks, fars, chunk, split, own, first, second, corner, *rest):
+    tail, rest = (rest[0], rest[1:]) if split else (None, rest)
+    panels, after, *messages, total = rest
     pairs = len(messages) // len(fars)
     share = messages[0].shape[0] // CHUNK
     rows, width, size = share * pairs, panels.shape[2], own.shape[0]
     place, x, _ = position()
-    every = [(own, 0, size), (first, chunk * size, size), (second, 0, size), (corner, 0, size)]
+    starts = [(own, 0), (first, chunk * size), (second, 0)]
+    every = [source_of(array, start, size, rows) for array, start in starts]
+    every.append(source_of(corner, 0, size, rows, tail))
     for p, far in enumerate(fars):
-        if far:
-            sums, sources = [jnp.zeros((rows, width), jnp.float32)] * CHUNK, every
-        else:
-            sums, sources = [near[n] for n in range(CHUNK)], every[-1:]
-        for n, one in enumerate(add_products(picks, place ^ far, panels[p], sources, rows, sums)):
+        sums = [jnp.zeros((rows, width), jnp.float32)] * CHUNK
+        for n, one in enumerate(add_products(picks, place ^ far, panels[p], every, sums)):
             total[n] = one
         for t in range(pairs):
             start = pl.multiple_of((x ^ t) * share, share)
@@ -155,47 +159,48 @@
     second = {n: send(own[n], 2) for wanted in (True, False) for n in chunks if near[n] == wanted}
     fars = list(range(SQUARE, grid_count, SQUARE))
     kept = [send(mine, far) for far in fars]
-    corner = {}
+    corner, cut = {}, size - rows
     for n in chunks:
-        corner[n] = send(second[n], 1) if near[n] else send(first[n * size : (n + 1) * size], 2)
-    halves = [array for one in kept for array in (one, send(one, 0, 1))]
+        if near[n]:
+            corner[n] = [send(second[n], 1)]
+        else:
+            corner[n] = [send(first[n * size : n * size + cut], 2), send(second[n][cut:], 1)]
+    hold = call(hold_kernel, "hold", half, [VMEM, ANY], 0)
+    halves = [array for one in kept for array in (one, send(hold(one, first), 0, 1))]
     fars = fars + [0]
     join = call(
         join_kernel,
         "join",
         like((len(fars),) + green_occ.shape, green_occ.dtype),
         [VMEM] * (1 + len(halves)),
-        0,
+        10**9,
     )
     panels = join(green_occ, *halves)
 
     virtual = [virtual_blocks[0]]
     virtual += [send(virtual[0], 0, 2 * t) for t in range(1, pairs)]
+    virtual = [[array[n * CHUNK : (n + 1) * CHUNK] for n in chunks] for array in virtual]
 
     after, operands = mine, {}
     ordered = sorted(chunks, key=lambda n: not near[n])
     for n in ordered:
         outs = [like((CHUNK * share, width), jnp.bfloat16)] * (len(fars) * pairs)
         sums = call(
-            lambda *refs, n=n: sums_kernel(picks, fars, n, *refs),
+            lambda *refs, n=n: sums_kernel(picks, fars, n, not near[n], *refs),
             "sums",
             outs,
-            [VMEM] * 6 + [ANY],
+            [VMEM] * (4 + len(corner[n])) + [ANY],
             0,
             [pltpu.VMEM((CHUNK, rows, width), jnp.float32)],
         )
-        near_shape = like((CHUNK, rows, width), jnp.float32)
-        part = call(
-            lambda *refs, n=n: near_kernel(picks, n, *refs), "near", near_shape, [VMEM] * 4, 0
-        )(own[n], first, second[n], green_occ)
-        parts = sums(own[n], first, second[n], corner[n], panels, part, after)
+        parts = sums(own[n], first, second[n], *corner[n], panels, after)
         after = parts[0]
         operands[n] = []
         for p, far in enumerate(fars):
             for t in range(pairs):
                 part = parts[p * pairs + t]
                 message = send(part, far, 2 * t) if far or t else part
-                operands[n] += [message, virtual[t][n * CHUNK : (n + 1) * CHUNK]]
+                operands[n] += [message, virtual[t][n]]
 
     *early, late = ordered
     operands_of = [array for n in early for array in operands[n]]

time: 43.2 us -> 42.2 us (0.977)
  starting transfers between devices: 21.1 us -> 20.6 us
    ppermute x15 -> x16, starting transfers between devices: 21.1 us -> 20.6 us  [send(): return lax.ppermute(array, AXES, order)]
    pallas_call x8 -> x7, Pallas kernels: 2.51 us -> 2.18 us  [run(): pl.pallas_call(kernel, out_shape=out, in_specs=specs, out_specs=jax.tree....]
    ppermute x15 -> x16, waiting for transfers between devices: 16.4 us -> 16.3 us  [send(): return lax.ppermute(array, AXES, order)]
  transfers between devices with their start and end apart: 15 -> 16, of which waited for: 9 -> 9; matrix products, arithmetic and copies ran while one was open for 0% -> 0% of each run, Pallas kernels for 5% -> 4%
where the time goes in v7:
time: 42.2 us; the launch traced here: 42 us
  starting transfers between devices  20.6 us (49%)
  waiting for transfers between devices  16.3 us (39%)
  other arithmetic  2.49 us (6%)
  Pallas kernels  2.18 us (5%)
    ppermute x16, starting transfers between devices, send(): return lax.ppermute(array, AXES, order)  20.6 us
    ppermute x16, waiting for transfers between devices, send(): return lax.ppermute(array, AXES, order)  16.3 us
    pallas_call x7, Pallas kernels, run(): pl.pallas_call(kernel, out_shape=out, in_specs=specs, out_specs=jax.tree....  2.18 us
    concatenate x1, other arithmetic, shards(): whole = jnp.concatenate([named, blocks], axis=1)  1.15 us
  transfers between devices with their start and end apart: 16, of which 9 were waited for; matrix products, arithmetic and copies ran while one was open for 0% of the time, Pallas kernels for 4%

profile of v7, /device:TPU:0, one launch (start us, length us, event | category | flops | bytes accessed | tf_op | source)
XLA Modules:
  0.0 42.0 jit_solution(14431164193409459545)
XLA Ops:
  0.0 0.7 %convert_element_type.16 = bf16[4,2]{0,1:T(2,128)(2,1)S(1)} convert(s32[4,2]{0,1:T(2,128)} %param.6) | non-fusion elementwise | flops 8 | bytes 48 | tf_op jit(solution)/shard_map/convert_element_type | solution.py:150
  0.7 0.1 copy.6
  0.8 0.1 convert_element_type.17
  0.9 0.1 broadcast_in_dim.11
  1.0 0.0 copy-start.1
  1.0 1.2 %pad_maximum_fusion = bf16[2,272,512]{2,1,0:T(8,128)(2,1)S(1)} fusion(bf16[2,16,512]{2,1,0:T(8,128)(2,1)S(1)} %broadcast_in_dim.11, bf16[2,256,512]{2,1,0:T(8,128)(2,1)} %bitcast.15), kind=kLoop, calls=%fused_computation.2 | loop fusion | flops 1114112 | bytes 1114112 | tf_op jit(solution)/shard_map/concatenate | solution.py:153
  2.1 0.0 copy-start.2
  2.1 0.0 copy-start
  2.1 3.0 %collective-permute-start = (bf16[544,512]{1,0:T(8,128)(2,1)S(1)}, bf16[544,512]{1,0:T(8,128)(2,1)S(1)}, u32[]{:S(2)}, u32[]{:S(2)}) collective-permute-start(bf16[544,512]{1,0:T(8,128)(2,1)S(1)} %bitcast.17), channel_id=1, source_target_pairs={{0,4},{1,5},{2,6},{3,7},{4,0},{5,1},{6,2},{7,3},{8,12},{9,13},{10,... | collective-permute-start | bytes 1671176 | tf_op jit(solution)/shard_map/ppermute | solution.py:139
  5.2 0.0 copy-done.1
  5.2 1.6 %collective-permute-start.1 = (bf16[272,512]{1,0:T(8,128)(2,1)S(1)}, bf16[272,512]{1,0:T(8,128)(2,1)S(1)}, u32[]{:S(2)}, u32[]{:S(2)}) collective-permute-start(bf16[272,512]{1,0:T(8,128)(2,1)S(1)} %get-tuple-element.26.refs_0_), channel_id=1, source_target_pairs={{0,8},{1,9},{2,10},{3,11},{4,12},{5,13},{6,14},{7,15},{8,0},{9,1},... | collective-permute-start | bytes 835592 | tf_op jit(solution)/shard_map/ppermute | solution.py:139
  6.9 0.0 copy-done.2
  6.9 1.5 %collective-permute-start.7 = (bf16[4,256,256]{2,1,0:T(8,128)(2,1)S(1)}, bf16[4,256,256]{2,1,0:T(8,128)(2,1)S(1)}, u32[]{:S(2)}, u32[]{:S(2)}) collective-permute-start(bf16[4,256,256]{2,1,0:T(8,128)(2,1)S(1)} %bitcast.18), channel_id=1, source_target_pairs={{0,2},{1,3},{2,0},{3,1},{4,6},{5,7},{6,4},{7,5},{8,10},{9,11},{10,... | collective-permute-start | bytes 1572872 | tf_op jit(solution)/shard_map/ppermute | solution.py:139
  8.4 0.0 copy-done
  8.4 2.7 %collective-permute-start.3 = (bf16[256,256]{1,0:T(8,128)(2,1)S(1)}, bf16[256,256]{1,0:T(8,128)(2,1)S(1)}, u32[]{:S(2)}, u32[]{:S(2)}) collective-permute-start(bf16[256,256]{1,0:T(8,128)(2,1)S(1)} %half.1.refs_5_), channel_id=1, source_target_pairs={{0,16},{1,17},{2,18},{3,19},{4,20},{5,21},{6,22},{7,23},{8,24},{9,... | collective-permute-start | bytes 393224 | tf_op jit(solution)/shard_map/ppermute | solution.py:139
  11.0 0.4 %collective-permute-start.9 = (bf16[272,512]{1,0:T(8,128)(2,1)S(1)}, bf16[272,512]{1,0:T(8,128)(2,1)S(1)}, u32[]{:S(2)}, u32[]{:S(2)}) collective-permute-start(bf16[272,512]{1,0:T(8,128)(2,1)S(1)} %get-tuple-element.25.refs_0_), channel_id=1, source_target_pairs={{0,8},{1,9},{2,10},{3,11},{4,12},{5,13},{6,14},{7,15},{8,0},{9,1},... | collective-permute-start | bytes 835592 | tf_op jit(solution)/shard_map/ppermute | solution.py:139
  11.5 6.2 %collective-permute-done.1.refs_2_ = bf16[272,512]{1,0:T(8,128)(2,1)S(1)} collective-permute-done((bf16[272,512]{1,0:T(8,128)(2,1)S(1)}, bf16[272,512]{1,0:T(8,128)(2,1)S(1)}, u32[]{:S(2)}, u32[]{:S(2)}) %collective-permute-start.1) | collective-permute-done | bytes 278560 | tf_op jit(solution)/shard_map/ppermute | solution.py:139
  17.7 0.0 collective-permute-start.2
  17.7 0.0 collective-permute-done.3.array.rest_0_
  17.7 0.5 %collective-permute-done.after.refs_1_ = bf16[544,512]{1,0:T(8,128)(2,1)S(1)} collective-permute-done((bf16[544,512]{1,0:T(8,128)(2,1)S(1)}, bf16[544,512]{1,0:T(8,128)(2,1)S(1)}, u32[]{:S(2)}, u32[]{:S(2)}) %collective-permute-start) | collective-permute-done | bytes 557088 | tf_op jit(solution)/shard_map/ppermute | solution.py:139
  18.2 0.1 collective-permute-start.4
  18.3 3.8 %collective-permute-done.9.refs_2_ = bf16[272,512]{1,0:T(8,128)(2,1)S(1)} collective-permute-done((bf16[272,512]{1,0:T(8,128)(2,1)S(1)}, bf16[272,512]{1,0:T(8,128)(2,1)S(1)}, u32[]{:S(2)}, u32[]{:S(2)}) %collective-permute-start.9) | collective-permute-done | bytes 278560 | tf_op jit(solution)/shard_map/ppermute | solution.py:139
  22.2 0.4 collective-permute-start.11
  22.6 1.8 %collective-permute-start.10 = (bf16[144,512]{1,0:T(8,128)(2,1)S(1)}, bf16[144,512]{1,0:T(8,128)(2,1)S(1)}, u32[]{:S(2)}, u32[]{:S(2)}) collective-permute-start(bf16[144,512]{1,0:T(8,128)(2,1)S(1)} %slice.45), channel_id=1, source_target_pairs={{0,8},{1,9},{2,10},{3,11},{4,12},{5,13},{6,14},{7,15},{8,0},{9,1},... | collective-permute-start | bytes 442376 | tf_op jit(solution)/shard_map/ppermute | solution.py:139
  24.4 0.0 collective-permute-done.4.rest_1_
  24.5 0.4 collective-permute-done.2.refs_3_
  24.9 0.8 %sums.2 = (bf16[128,256]{1,0:T(8,128)(2,1)S(1)}, bf16[128,256]{1,0:T(8,128)(2,1)S(1)}, bf16[128,256]{1,0:T(8,128)(2,1)S(1)}, bf16[128,256]{1,0:T(8,128)(2,1)S(1)}) custom-call(bf16[272,512]{1,0:T(8,128)(2,1)S(1)} %get-tuple-element.26.refs_0_, bf16[544,512]{1,0:T(8,128)(2,1)S(1)} %collective-permute-done.after.refs_1_, ...), custom_call_target="tpu_custom_call" | custom-call | tf_op jit(solution)/shard_map/sums/pallas_call | solution.py:112
  25.6 2.2 %collective-permute-start.5 = (bf16[128,256]{1,0:T(8,128)(2,1)S(1)}, bf16[128,256]{1,0:T(8,128)(2,1)S(1)}, u32[]{:S(2)}, u32[]{:S(2)}) collective-permute-start(bf16[128,256]{1,0:T(8,128)(2,1)S(1)} %get-tuple-element.15.refs_6_), channel_id=1, source_target_pairs={{0,16},{1,17},{2,18},{3,19},{4,20},{5,21},{6,22},{7,23},{8,24},{9,... | collective-permute-start | bytes 196616 | tf_op jit(solution)/shard_map/ppermute | solution.py:139
  27.9 1.7 %collective-permute-start.6 = (bf16[128,256]{1,0:T(8,128)(2,1)S(1)}, bf16[128,256]{1,0:T(8,128)(2,1)S(1)}, u32[]{:S(2)}, u32[]{:S(2)}) collective-permute-start(bf16[128,256]{1,0:T(8,128)(2,1)S(1)} %get-tuple-element.16), channel_id=1, source_target_pairs={{0,18},{1,19},{2,16},{3,17},{4,22},{5,23},{6,20},{7,21},{8,26},{9,... | collective-permute-start | bytes 196616 | tf_op jit(solution)/shard_map/ppermute | solution.py:139
  29.6 0.0 collective-permute-done.7
  29.6 0.5 %collective-permute-start.8 = (bf16[128,256]{1,0:T(8,128)(2,1)S(1)}, bf16[128,256]{1,0:T(8,128)(2,1)S(1)}, u32[]{:S(2)}, u32[]{:S(2)}) collective-permute-start(bf16[128,256]{1,0:T(8,128)(2,1)S(1)} %get-tuple-element.18), channel_id=1, source_target_pairs={{0,2},{1,3},{2,0},{3,1},{4,6},{5,7},{6,4},{7,5},{8,10},{9,11},{10,... | collective-permute-start | bytes 196616 | tf_op jit(solution)/shard_map/ppermute | solution.py:139
  30.1 0.0 collective-permute-done.11.refs_4_
  30.2 0.0 collective-permute-done.10.refs_3_
  30.2 0.8 %sums.3 = (bf16[128,256]{1,0:T(8,128)(2,1)S(1)}, bf16[128,256]{1,0:T(8,128)(2,1)S(1)}, bf16[128,256]{1,0:T(8,128)(2,1)S(1)}, bf16[128,256]{1,0:T(8,128)(2,1)S(1)}) custom-call(bf16[272,512]{1,0:T(8,128)(2,1)S(1)} %get-tuple-element.25.refs_0_, bf16[544,512]{1,0:T(8,128)(2,1)S(1)} %collective-permute-done.after.refs_1_, ...), custom_call_target="tpu_custom_call" | custom-call | tf_op jit(solution)/shard_map/sums/pallas_call | solution.py:112
  30.9 2.2 %collective-permute-start.12 = (bf16[128,256]{1,0:T(8,128)(2,1)S(1)}, bf16[128,256]{1,0:T(8,128)(2,1)S(1)}, u32[]{:S(2)}, u32[]{:S(2)}) collective-permute-start(bf16[128,256]{1,0:T(8,128)(2,1)S(1)} %get-tuple-element.19), channel_id=1, source_target_pairs={{0,16},{1,17},{2,18},{3,19},{4,20},{5,21},{6,22},{7,23},{8,24},{9,... | collective-permute-start | bytes 196616 | tf_op jit(solution)/shard_map/ppermute | solution.py:139
  33.2 1.7 %collective-permute-start.13 = (bf16[128,256]{1,0:T(8,128)(2,1)S(1)}, bf16[128,256]{1,0:T(8,128)(2,1)S(1)}, u32[]{:S(2)}, u32[]{:S(2)}) collective-permute-start(bf16[128,256]{1,0:T(8,128)(2,1)S(1)} %get-tuple-element.20), channel_id=1, source_target_pairs={{0,18},{1,19},{2,16},{3,17},{4,22},{5,23},{6,20},{7,21},{8,26},{9,... | collective-permute-start | bytes 196616 | tf_op jit(solution)/shard_map/ppermute | solution.py:139
  34.9 0.0 collective-permute-done.5.refs_0_
  34.9 0.5 %collective-permute-start.14 = (bf16[128,256]{1,0:T(8,128)(2,1)S(1)}, bf16[128,256]{1,0:T(8,128)(2,1)S(1)}, u32[]{:S(2)}, u32[]{:S(2)}) collective-permute-start(bf16[128,256]{1,0:T(8,128)(2,1)S(1)} %get-tuple-element.22), channel_id=1, source_target_pairs={{0,2},{1,3},{2,0},{3,1},{4,6},{5,7},{6,4},{7,5},{8,10},{9,11},{10,... | collective-permute-start | bytes 196616 | tf_op jit(solution)/shard_map/ppermute | solution.py:139
  35.4 1.4 %collective-permute-done.6.refs_2_ = bf16[128,256]{1,0:T(8,128)(2,1)S(1)} collective-permute-done((bf16[128,256]{1,0:T(8,128)(2,1)S(1)}, bf16[128,256]{1,0:T(8,128)(2,1)S(1)}, u32[]{:S(2)}, u32[]{:S(2)}) %collective-permute-start.6) | collective-permute-done | bytes 65568 | tf_op jit(solution)/shard_map/ppermute | solution.py:139
  36.8 0.0 collective-permute-done.8.refs_6_
  36.8 0.3 virtual_first.1.before
  37.1 1.4 %collective-permute-done.12.refs_0_ = bf16[128,256]{1,0:T(8,128)(2,1)S(1)} collective-permute-done((bf16[128,256]{1,0:T(8,128)(2,1)S(1)}, bf16[128,256]{1,0:T(8,128)(2,1)S(1)}, u32[]{:S(2)}, u32[]{:S(2)}) %collective-permute-start.12) | collective-permute-done | bytes 65568 | tf_op jit(solution)/shard_map/ppermute | solution.py:139
  38.5 0.9 %collective-permute-done.13.refs_2_ = bf16[128,256]{1,0:T(8,128)(2,1)S(1)} collective-permute-done((bf16[128,256]{1,0:T(8,128)(2,1)S(1)}, bf16[128,256]{1,0:T(8,128)(2,1)S(1)}, u32[]{:S(2)}, u32[]{:S(2)}) %collective-permute-start.13) | collective-permute-done | bytes 65568 | tf_op jit(solution)/shard_map/ppermute | solution.py:139
  39.4 0.4 collective-permute-done.14.refs_6_
  39.8 0.3 virtual_last.1
  40.1 0.1 collective-permute-start.15
  40.2 1.2 %collective-permute-done.15 = f32[32,256]{1,0:T(8,128)S(1)} collective-permute-done((f32[32,256]{1,0:T(8,128)S(1)}, f32[32,256]{1,0:T(8,128)S(1)}, u32[]{:S(2)}, u32[]{:S(2)}) %collective-permute-start.15) | collective-permute-done | bytes 32800 | tf_op jit(solution)/shard_map/ppermute | solution.py:139
  41.4 0.6 %add_bitcast_fusion = f32[1,32,256]{2,1,0:T(8,128)} fusion(f32[32,256]{1,0:T(8,128)S(1)} %get-tuple-element.23, f32[32,256]{1,0:T(8,128)S(1)} %collective-permute-done.15), kind=kLoop, calls=%fused_computation.11 | loop fusion | flops 8192 | bytes 98304 | tf_op jit(solution)/shard_map/broadcast_in_dim | solution.py:219
  (9 shorter events, 0.2 us)
Async XLA Ops:
  1.0 4.2 %copy-start.1 = (bf16[512,512]{1,0:T(8,128)(2,1)S(1)}, bf16[512,512]{1,0:T(8,128)(2,1)}, u32[]{:S(2)}) copy-start(bf16[512,512]{1,0:T(8,128)(2,1)} %param.4) | copy-start | bytes 1572868
  2.1 4.7 %copy-start.2 = (bf16[1,4,256,256]{3,2,1,0:T(8,128)(2,1)S(1)}, bf16[1,4,256,256]{3,2,1,0:T(8,128)(2,1)}, u32[]{:S(2)}) copy-start(bf16[1,4,256,256]{3,2,1,0:T(8,128)(2,1)} %param.7) | copy-start | bytes 1572868
  2.1 6.2 %copy-start = (bf16[512,256]{1,0:T(8,128)(2,1)S(1)}, bf16[512,256]{1,0:T(8,128)(2,1)}, u32[]{:S(2)}) copy-start(bf16[512,256]{1,0:T(8,128)(2,1)} %own.1) | copy-start | bytes 786436
  2.1 16.1 %collective-permute-start = (bf16[544,512]{1,0:T(8,128)(2,1)S(1)}, bf16[544,512]{1,0:T(8,128)(2,1)S(1)}, u32[]{:S(2)}, u32[]{:S(2)}) collective-permute-start(bf16[544,512]{1,0:T(8,128)(2,1)S(1)} %bitcast.17), channel_id=1, source_target_pairs={{0,4},{1,5},{2,6},{3,7},{4,0},{5,1},{6,2},{7,3},{8,12},{9,13},{10,... | collective-permute-start | bytes 1671176 | tf_op jit(solution)/shard_map/ppermute | solution.py:139
  5.2 12.5 %collective-permute-start.1 = (bf16[272,512]{1,0:T(8,128)(2,1)S(1)}, bf16[272,512]{1,0:T(8,128)(2,1)S(1)}, u32[]{:S(2)}, u32[]{:S(2)}) collective-permute-start(bf16[272,512]{1,0:T(8,128)(2,1)S(1)} %get-tuple-element.26.refs_0_), channel_id=1, source_target_pairs={{0,8},{1,9},{2,10},{3,11},{4,12},{5,13},{6,14},{7,15},{8,0},{9,1},... | collective-permute-start | bytes 835592 | tf_op jit(solution)/shard_map/ppermute | solution.py:139
  6.9 22.7 %collective-permute-start.7 = (bf16[4,256,256]{2,1,0:T(8,128)(2,1)S(1)}, bf16[4,256,256]{2,1,0:T(8,128)(2,1)S(1)}, u32[]{:S(2)}, u32[]{:S(2)}) collective-permute-start(bf16[4,256,256]{2,1,0:T(8,128)(2,1)S(1)} %bitcast.18), channel_id=1, source_target_pairs={{0,2},{1,3},{2,0},{3,1},{4,6},{5,7},{6,4},{7,5},{8,10},{9,11},{10,... | collective-permute-start | bytes 1572872 | tf_op jit(solution)/shard_map/ppermute | solution.py:139
  8.4 9.3 %collective-permute-start.3 = (bf16[256,256]{1,0:T(8,128)(2,1)S(1)}, bf16[256,256]{1,0:T(8,128)(2,1)S(1)}, u32[]{:S(2)}, u32[]{:S(2)}) collective-permute-start(bf16[256,256]{1,0:T(8,128)(2,1)S(1)} %half.1.refs_5_), channel_id=1, source_target_pairs={{0,16},{1,17},{2,18},{3,19},{4,20},{5,21},{6,22},{7,23},{8,24},{9,... | collective-permute-start | bytes 393224 | tf_op jit(solution)/shard_map/ppermute | solution.py:139
  11.0 11.2 %collective-permute-start.9 = (bf16[272,512]{1,0:T(8,128)(2,1)S(1)}, bf16[272,512]{1,0:T(8,128)(2,1)S(1)}, u32[]{:S(2)}, u32[]{:S(2)}) collective-permute-start(bf16[272,512]{1,0:T(8,128)(2,1)S(1)} %get-tuple-element.25.refs_0_), channel_id=1, source_target_pairs={{0,8},{1,9},{2,10},{3,11},{4,12},{5,13},{6,14},{7,15},{8,0},{9,1},... | collective-permute-start | bytes 835592 | tf_op jit(solution)/shard_map/ppermute | solution.py:139
  17.7 7.2 %collective-permute-start.2 = (bf16[272,512]{1,0:T(8,128)(2,1)S(1)}, bf16[272,512]{1,0:T(8,128)(2,1)S(1)}, u32[]{:S(2)}, u32[]{:S(2)}) collective-permute-start(bf16[272,512]{1,0:T(8,128)(2,1)S(1)} %collective-permute-done.1.refs_2_), channel_id=1, source_target_pairs={{0,4},{1,5},{2,6},{3,7},{4,0},{5,1},{6,2},{7,3},{8,12},{9,13},{10,... | collective-permute-start | bytes 835592 | tf_op jit(solution)/shard_map/ppermute | solution.py:139
  18.2 6.2 %collective-permute-start.4 = (bf16[256,256]{1,0:T(8,128)(2,1)S(1)}, bf16[256,256]{1,0:T(8,128)(2,1)S(1)}, u32[]{:S(2)}, u32[]{:S(2)}) collective-permute-start(bf16[256,256]{1,0:T(8,128)(2,1)S(1)} %hold.1), channel_id=1, source_target_pairs={{0,1},{1,0},{2,3},{3,2},{4,5},{5,4},{6,7},{7,6},{8,9},{9,8},{10,11... | collective-permute-start | bytes 393224 | tf_op jit(solution)/shard_map/ppermute | solution.py:139
  22.2 8.0 %collective-permute-start.11 = (bf16[128,512]{1,0:T(8,128)(2,1)S(1)}, bf16[128,512]{1,0:T(8,128)(2,1)S(1)}, u32[]{:S(2)}, u32[]{:S(2)}) collective-permute-start(bf16[128,512]{1,0:T(8,128)(2,1)S(1)} %slice.46), channel_id=1, source_target_pairs={{0,4},{1,5},{2,6},{3,7},{4,0},{5,1},{6,2},{7,3},{8,12},{9,13},{10,... | collective-permute-start | bytes 393224 | tf_op jit(solution)/shard_map/ppermute | solution.py:139
  22.6 7.5 %collective-permute-start.10 = (bf16[144,512]{1,0:T(8,128)(2,1)S(1)}, bf16[144,512]{1,0:T(8,128)(2,1)S(1)}, u32[]{:S(2)}, u32[]{:S(2)}) collective-permute-start(bf16[144,512]{1,0:T(8,128)(2,1)S(1)} %slice.45), channel_id=1, source_target_pairs={{0,8},{1,9},{2,10},{3,11},{4,12},{5,13},{6,14},{7,15},{8,0},{9,1},... | collective-permute-start | bytes 442376 | tf_op jit(solution)/shard_map/ppermute | solution.py:139
  25.6 9.2 %collective-permute-start.5 = (bf16[128,256]{1,0:T(8,128)(2,1)S(1)}, bf16[128,256]{1,0:T(8,128)(2,1)S(1)}, u32[]{:S(2)}, u32[]{:S(2)}) collective-permute-start(bf16[128,256]{1,0:T(8,128)(2,1)S(1)} %get-tuple-element.15.refs_6_), channel_id=1, source_target_pairs={{0,16},{1,17},{2,18},{3,19},{4,20},{5,21},{6,22},{7,23},{8,24},{9,... | collective-permute-start | bytes 196616 | tf_op jit(solution)/shard_map/ppermute | solution.py:139
  27.9 8.9 %collective-permute-start.6 = (bf16[128,256]{1,0:T(8,128)(2,1)S(1)}, bf16[128,256]{1,0:T(8,128)(2,1)S(1)}, u32[]{:S(2)}, u32[]{:S(2)}) collective-permute-start(bf16[128,256]{1,0:T(8,128)(2,1)S(1)} %get-tuple-element.16), channel_id=1, source_target_pairs={{0,18},{1,19},{2,16},{3,17},{4,22},{5,23},{6,20},{7,21},{8,26},{9,... | collective-permute-start | bytes 196616 | tf_op jit(solution)/shard_map/ppermute | solution.py:139
  29.6 7.2 %collective-permute-start.8 = (bf16[128,256]{1,0:T(8,128)(2,1)S(1)}, bf16[128,256]{1,0:T(8,128)(2,1)S(1)}, u32[]{:S(2)}, u32[]{:S(2)}) collective-permute-start(bf16[128,256]{1,0:T(8,128)(2,1)S(1)} %get-tuple-element.18), channel_id=1, source_target_pairs={{0,2},{1,3},{2,0},{3,1},{4,6},{5,7},{6,4},{7,5},{8,10},{9,11},{10,... | collective-permute-start | bytes 196616 | tf_op jit(solution)/shard_map/ppermute | solution.py:139
  30.9 7.6 %collective-permute-start.12 = (bf16[128,256]{1,0:T(8,128)(2,1)S(1)}, bf16[128,256]{1,0:T(8,128)(2,1)S(1)}, u32[]{:S(2)}, u32[]{:S(2)}) collective-permute-start(bf16[128,256]{1,0:T(8,128)(2,1)S(1)} %get-tuple-element.19), channel_id=1, source_target_pairs={{0,16},{1,17},{2,18},{3,19},{4,20},{5,21},{6,22},{7,23},{8,24},{9,... | collective-permute-start | bytes 196616 | tf_op jit(solution)/shard_map/ppermute | solution.py:139
  33.2 6.3 %collective-permute-start.13 = (bf16[128,256]{1,0:T(8,128)(2,1)S(1)}, bf16[128,256]{1,0:T(8,128)(2,1)S(1)}, u32[]{:S(2)}, u32[]{:S(2)}) collective-permute-start(bf16[128,256]{1,0:T(8,128)(2,1)S(1)} %get-tuple-element.20), channel_id=1, source_target_pairs={{0,18},{1,19},{2,16},{3,17},{4,22},{5,23},{6,20},{7,21},{8,26},{9,... | collective-permute-start | bytes 196616 | tf_op jit(solution)/shard_map/ppermute | solution.py:139
  34.9 5.0 %collective-permute-start.14 = (bf16[128,256]{1,0:T(8,128)(2,1)S(1)}, bf16[128,256]{1,0:T(8,128)(2,1)S(1)}, u32[]{:S(2)}, u32[]{:S(2)}) collective-permute-start(bf16[128,256]{1,0:T(8,128)(2,1)S(1)} %get-tuple-element.22), channel_id=1, source_target_pairs={{0,2},{1,3},{2,0},{3,1},{4,6},{5,7},{6,4},{7,5},{8,10},{9,11},{10,... | collective-permute-start | bytes 196616 | tf_op jit(solution)/shard_map/ppermute | solution.py:139
  40.1 1.3 %collective-permute-start.15 = (f32[32,256]{1,0:T(8,128)S(1)}, f32[32,256]{1,0:T(8,128)S(1)}, u32[]{:S(2)}, u32[]{:S(2)}) collective-permute-start(f32[32,256]{1,0:T(8,128)S(1)} %get-tuple-element.24), channel_id=1, source_target_pairs={{0,1},{1,0},{2,3},{3,2},{4,5},{5,4},{6,7},{7,6},{8,9},{9,8},{10,11... | collective-permute-start | bytes 98312 | tf_op jit(solution)/shard_map/ppermute | solution.py:139

commit v8 on v7

--- a/solution.py
+++ b/solution.py
@@ -197,7 +197,7 @@
         after = parts[0]
         operands[n] = []
         for p, far in enumerate(fars):
-            for t in range(pairs):
+            for t in reversed(range(pairs)):
                 part = parts[p * pairs + t]
                 message = send(part, far, 2 * t) if far or t else part
                 operands[n] += [message, virtual[t][n]]

time: 42.2 us -> 41.7 us (0.988)
  waiting for transfers between devices: 16.3 us -> 15.8 us
    ppermute x16, waiting for transfers between devices: 16.3 us -> 15.8 us  [send(): return lax.ppermute(array, AXES, order)]
  transfers between devices with their start and end apart: 16 -> 16, of which waited for: 9 -> 9; matrix products, arithmetic and copies ran while one was open for 0% -> 0% of each run, Pallas kernels for 4% -> 5%
where the time goes in v8:
time: 41.7 us; the launch traced here: 41.5 us
  starting transfers between devices  20.6 us (49%)
  waiting for transfers between devices  15.8 us (38%)
  other arithmetic  2.49 us (6%)
  Pallas kernels  2.18 us (5%)
    ppermute x16, starting transfers between devices, send(): return lax.ppermute(array, AXES, order)  20.6 us
    ppermute x16, waiting for transfers between devices, send(): return lax.ppermute(array, AXES, order)  15.8 us
    pallas_call x7, Pallas kernels, run(): pl.pallas_call(kernel, out_shape=out, in_specs=specs, out_specs=jax.tree....  2.18 us
    concatenate x1, other arithmetic, shards(): whole = jnp.concatenate([named, blocks], axis=1)  1.15 us
  transfers between devices with their start and end apart: 16, of which 9 were waited for; matrix products, arithmetic and copies ran while one was open for 0% of the time, Pallas kernels for 5%

profile of v8, /device:TPU:0, one launch (start us, length us, event | category | flops | bytes accessed | tf_op | source)
XLA Modules:
  0.0 41.5 jit_solution(994561957111115485)
XLA Ops:
  0.0 0.7 %convert_element_type.16 = bf16[4,2]{0,1:T(2,128)(2,1)S(1)} convert(s32[4,2]{0,1:T(2,128)} %param.6) | non-fusion elementwise | flops 8 | bytes 48 | tf_op jit(solution)/shard_map/convert_element_type | solution.py:150
  0.7 0.1 copy.6
  0.8 0.1 convert_element_type.17
  0.9 0.1 broadcast_in_dim.11
  1.0 0.0 copy-start.1
  1.0 1.2 %pad_maximum_fusion = bf16[2,272,512]{2,1,0:T(8,128)(2,1)S(1)} fusion(bf16[2,16,512]{2,1,0:T(8,128)(2,1)S(1)} %broadcast_in_dim.11, bf16[2,256,512]{2,1,0:T(8,128)(2,1)} %bitcast.15), kind=kLoop, calls=%fused_computation.2 | loop fusion | flops 1114112 | bytes 1114112 | tf_op jit(solution)/shard_map/concatenate | solution.py:153
  2.1 0.0 copy-start.2
  2.1 0.0 copy-start
  2.1 3.0 %collective-permute-start = (bf16[544,512]{1,0:T(8,128)(2,1)S(1)}, bf16[544,512]{1,0:T(8,128)(2,1)S(1)}, u32[]{:S(2)}, u32[]{:S(2)}) collective-permute-start(bf16[544,512]{1,0:T(8,128)(2,1)S(1)} %bitcast.17), channel_id=1, source_target_pairs={{0,4},{1,5},{2,6},{3,7},{4,0},{5,1},{6,2},{7,3},{8,12},{9,13},{10,... | collective-permute-start | bytes 1671176 | tf_op jit(solution)/shard_map/ppermute | solution.py:139
  5.2 0.0 copy-done.1
  5.2 1.6 %collective-permute-start.1 = (bf16[272,512]{1,0:T(8,128)(2,1)S(1)}, bf16[272,512]{1,0:T(8,128)(2,1)S(1)}, u32[]{:S(2)}, u32[]{:S(2)}) collective-permute-start(bf16[272,512]{1,0:T(8,128)(2,1)S(1)} %get-tuple-element.26.refs_0_), channel_id=1, source_target_pairs={{0,8},{1,9},{2,10},{3,11},{4,12},{5,13},{6,14},{7,15},{8,0},{9,1},... | collective-permute-start | bytes 835592 | tf_op jit(solution)/shard_map/ppermute | solution.py:139
  6.9 0.0 copy-done.2
  6.9 1.5 %collective-permute-start.6 = (bf16[4,256,256]{2,1,0:T(8,128)(2,1)S(1)}, bf16[4,256,256]{2,1,0:T(8,128)(2,1)S(1)}, u32[]{:S(2)}, u32[]{:S(2)}) collective-permute-start(bf16[4,256,256]{2,1,0:T(8,128)(2,1)S(1)} %bitcast.18), channel_id=1, source_target_pairs={{0,2},{1,3},{2,0},{3,1},{4,6},{5,7},{6,4},{7,5},{8,10},{9,11},{10,... | collective-permute-start | bytes 1572872 | tf_op jit(solution)/shard_map/ppermute | solution.py:139
  8.4 0.0 copy-done
  8.4 2.7 %collective-permute-start.3 = (bf16[256,256]{1,0:T(8,128)(2,1)S(1)}, bf16[256,256]{1,0:T(8,128)(2,1)S(1)}, u32[]{:S(2)}, u32[]{:S(2)}) collective-permute-start(bf16[256,256]{1,0:T(8,128)(2,1)S(1)} %half.1.refs_5_), channel_id=1, source_target_pairs={{0,16},{1,17},{2,18},{3,19},{4,20},{5,21},{6,22},{7,23},{8,24},{9,... | collective-permute-start | bytes 393224 | tf_op jit(solution)/shard_map/ppermute | solution.py:139
  11.0 0.4 %collective-permute-start.9 = (bf16[272,512]{1,0:T(8,128)(2,1)S(1)}, bf16[272,512]{1,0:T(8,128)(2,1)S(1)}, u32[]{:S(2)}, u32[]{:S(2)}) collective-permute-start(bf16[272,512]{1,0:T(8,128)(2,1)S(1)} %get-tuple-element.25.refs_0_), channel_id=1, source_target_pairs={{0,8},{1,9},{2,10},{3,11},{4,12},{5,13},{6,14},{7,15},{8,0},{9,1},... | collective-permute-start | bytes 835592 | tf_op jit(solution)/shard_map/ppermute | solution.py:139
  11.5 6.2 %collective-permute-done.1.refs_2_ = bf16[272,512]{1,0:T(8,128)(2,1)S(1)} collective-permute-done((bf16[272,512]{1,0:T(8,128)(2,1)S(1)}, bf16[272,512]{1,0:T(8,128)(2,1)S(1)}, u32[]{:S(2)}, u32[]{:S(2)}) %collective-permute-start.1) | collective-permute-done | bytes 278560 | tf_op jit(solution)/shard_map/ppermute | solution.py:139
  17.7 0.0 collective-permute-start.2
  17.7 0.0 collective-permute-done.3.array.rest_0_
  17.7 0.5 %collective-permute-done.after.refs_1_ = bf16[544,512]{1,0:T(8,128)(2,1)S(1)} collective-permute-done((bf16[544,512]{1,0:T(8,128)(2,1)S(1)}, bf16[544,512]{1,0:T(8,128)(2,1)S(1)}, u32[]{:S(2)}, u32[]{:S(2)}) %collective-permute-start) | collective-permute-done | bytes 557088 | tf_op jit(solution)/shard_map/ppermute | solution.py:139
  18.2 0.1 collective-permute-start.4
  18.3 3.8 %collective-permute-done.9.refs_2_ = bf16[272,512]{1,0:T(8,128)(2,1)S(1)} collective-permute-done((bf16[272,512]{1,0:T(8,128)(2,1)S(1)}, bf16[272,512]{1,0:T(8,128)(2,1)S(1)}, u32[]{:S(2)}, u32[]{:S(2)}) %collective-permute-start.9) | collective-permute-done | bytes 278560 | tf_op jit(solution)/shard_map/ppermute | solution.py:139
  22.2 0.4 collective-permute-start.11
  22.6 1.8 %collective-permute-start.10 = (bf16[144,512]{1,0:T(8,128)(2,1)S(1)}, bf16[144,512]{1,0:T(8,128)(2,1)S(1)}, u32[]{:S(2)}, u32[]{:S(2)}) collective-permute-start(bf16[144,512]{1,0:T(8,128)(2,1)S(1)} %slice.45), channel_id=1, source_target_pairs={{0,8},{1,9},{2,10},{3,11},{4,12},{5,13},{6,14},{7,15},{8,0},{9,1},... | collective-permute-start | bytes 442376 | tf_op jit(solution)/shard_map/ppermute | solution.py:139
  24.4 0.0 collective-permute-done.4.rest_1_
  24.5 0.4 %collective-permute-done.2.refs_3_ = bf16[272,512]{1,0:T(8,128)(2,1)S(1)} collective-permute-done((bf16[272,512]{1,0:T(8,128)(2,1)S(1)}, bf16[272,512]{1,0:T(8,128)(2,1)S(1)}, u32[]{:S(2)}, u32[]{:S(2)}) %collective-permute-start.2) | collective-permute-done | bytes 278560 | tf_op jit(solution)/shard_map/ppermute | solution.py:139
  24.9 0.8 %sums.2 = (bf16[128,256]{1,0:T(8,128)(2,1)S(1)}, bf16[128,256]{1,0:T(8,128)(2,1)S(1)}, bf16[128,256]{1,0:T(8,128)(2,1)S(1)}, bf16[128,256]{1,0:T(8,128)(2,1)S(1)}) custom-call(bf16[272,512]{1,0:T(8,128)(2,1)S(1)} %get-tuple-element.26.refs_0_, bf16[544,512]{1,0:T(8,128)(2,1)S(1)} %collective-permute-done.after.refs_1_, ...), custom_call_target="tpu_custom_call" | custom-call | tf_op jit(solution)/shard_map/sums/pallas_call | solution.py:112
  25.6 2.2 %collective-permute-start.7 = (bf16[128,256]{1,0:T(8,128)(2,1)S(1)}, bf16[128,256]{1,0:T(8,128)(2,1)S(1)}, u32[]{:S(2)}, u32[]{:S(2)}) collective-permute-start(bf16[128,256]{1,0:T(8,128)(2,1)S(1)} %get-tuple-element.16.refs_6_), channel_id=1, source_target_pairs={{0,16},{1,17},{2,18},{3,19},{4,20},{5,21},{6,22},{7,23},{8,24},{9,... | collective-permute-start | bytes 196616 | tf_op jit(solution)/shard_map/ppermute | solution.py:139
  27.9 1.7 %collective-permute-start.5 = (bf16[128,256]{1,0:T(8,128)(2,1)S(1)}, bf16[128,256]{1,0:T(8,128)(2,1)S(1)}, u32[]{:S(2)}, u32[]{:S(2)}) collective-permute-start(bf16[128,256]{1,0:T(8,128)(2,1)S(1)} %get-tuple-element.15), channel_id=1, source_target_pairs={{0,18},{1,19},{2,16},{3,17},{4,22},{5,23},{6,20},{7,21},{8,26},{9,... | collective-permute-start | bytes 196616 | tf_op jit(solution)/shard_map/ppermute | solution.py:139
  29.6 0.0 collective-permute-done.6
  29.6 0.5 %collective-permute-start.8 = (bf16[128,256]{1,0:T(8,128)(2,1)S(1)}, bf16[128,256]{1,0:T(8,128)(2,1)S(1)}, u32[]{:S(2)}, u32[]{:S(2)}) collective-permute-start(bf16[128,256]{1,0:T(8,128)(2,1)S(1)} %get-tuple-element.17), channel_id=1, source_target_pairs={{0,2},{1,3},{2,0},{3,1},{4,6},{5,7},{6,4},{7,5},{8,10},{9,11},{10,... | collective-permute-start | bytes 196616 | tf_op jit(solution)/shard_map/ppermute | solution.py:139
  30.1 0.0 collective-permute-done.11.refs_4_
  30.2 0.0 collective-permute-done.10.refs_3_
  30.2 0.8 %sums.3 = (bf16[128,256]{1,0:T(8,128)(2,1)S(1)}, bf16[128,256]{1,0:T(8,128)(2,1)S(1)}, bf16[128,256]{1,0:T(8,128)(2,1)S(1)}, bf16[128,256]{1,0:T(8,128)(2,1)S(1)}) custom-call(bf16[272,512]{1,0:T(8,128)(2,1)S(1)} %get-tuple-element.25.refs_0_, bf16[544,512]{1,0:T(8,128)(2,1)S(1)} %collective-permute-done.after.refs_1_, ...), custom_call_target="tpu_custom_call" | custom-call | tf_op jit(solution)/shard_map/sums/pallas_call | solution.py:112
  30.9 3.2 %collective-permute-start.12 = (bf16[128,256]{1,0:T(8,128)(2,1)S(1)}, bf16[128,256]{1,0:T(8,128)(2,1)S(1)}, u32[]{:S(2)}, u32[]{:S(2)}) collective-permute-start(bf16[128,256]{1,0:T(8,128)(2,1)S(1)} %get-tuple-element.19), channel_id=1, source_target_pairs={{0,18},{1,19},{2,16},{3,17},{4,22},{5,23},{6,20},{7,21},{8,26},{9,... | collective-permute-start | bytes 196616 | tf_op jit(solution)/shard_map/ppermute | solution.py:139
  34.1 0.8 %collective-permute-start.13 = (bf16[128,256]{1,0:T(8,128)(2,1)S(1)}, bf16[128,256]{1,0:T(8,128)(2,1)S(1)}, u32[]{:S(2)}, u32[]{:S(2)}) collective-permute-start(bf16[128,256]{1,0:T(8,128)(2,1)S(1)} %get-tuple-element.20), channel_id=1, source_target_pairs={{0,16},{1,17},{2,18},{3,19},{4,20},{5,21},{6,22},{7,23},{8,24},{9,... | collective-permute-start | bytes 196616 | tf_op jit(solution)/shard_map/ppermute | solution.py:139
  34.9 0.0 collective-permute-done.7.refs_2_
  34.9 0.5 %collective-permute-start.14 = (bf16[128,256]{1,0:T(8,128)(2,1)S(1)}, bf16[128,256]{1,0:T(8,128)(2,1)S(1)}, u32[]{:S(2)}, u32[]{:S(2)}) collective-permute-start(bf16[128,256]{1,0:T(8,128)(2,1)S(1)} %get-tuple-element.21), channel_id=1, source_target_pairs={{0,2},{1,3},{2,0},{3,1},{4,6},{5,7},{6,4},{7,5},{8,10},{9,11},{10,... | collective-permute-start | bytes 196616 | tf_op jit(solution)/shard_map/ppermute | solution.py:139
  35.4 1.4 %collective-permute-done.5.refs_0_ = bf16[128,256]{1,0:T(8,128)(2,1)S(1)} collective-permute-done((bf16[128,256]{1,0:T(8,128)(2,1)S(1)}, bf16[128,256]{1,0:T(8,128)(2,1)S(1)}, u32[]{:S(2)}, u32[]{:S(2)}) %collective-permute-start.5) | collective-permute-done | bytes 65568 | tf_op jit(solution)/shard_map/ppermute | solution.py:139
  36.8 0.0 collective-permute-done.8.refs_4_
  36.8 0.3 virtual_first.1.before
  37.1 1.6 %collective-permute-done.12.refs_0_ = bf16[128,256]{1,0:T(8,128)(2,1)S(1)} collective-permute-done((bf16[128,256]{1,0:T(8,128)(2,1)S(1)}, bf16[128,256]{1,0:T(8,128)(2,1)S(1)}, u32[]{:S(2)}, u32[]{:S(2)}) %collective-permute-start.12) | collective-permute-done | bytes 65568 | tf_op jit(solution)/shard_map/ppermute | solution.py:139
  38.6 0.6 %collective-permute-done.13.refs_2_ = bf16[128,256]{1,0:T(8,128)(2,1)S(1)} collective-permute-done((bf16[128,256]{1,0:T(8,128)(2,1)S(1)}, bf16[128,256]{1,0:T(8,128)(2,1)S(1)}, u32[]{:S(2)}, u32[]{:S(2)}) %collective-permute-start.13) | collective-permute-done | bytes 65568 | tf_op jit(solution)/shard_map/ppermute | solution.py:139
  39.3 0.1 collective-permute-done.14.refs_4_
  39.3 0.3 virtual_last.1
  39.6 0.1 collective-permute-start.15
  39.7 1.2 %collective-permute-done.15 = f32[32,256]{1,0:T(8,128)S(1)} collective-permute-done((f32[32,256]{1,0:T(8,128)S(1)}, f32[32,256]{1,0:T(8,128)S(1)}, u32[]{:S(2)}, u32[]{:S(2)}) %collective-permute-start.15) | collective-permute-done | bytes 32800 | tf_op jit(solution)/shard_map/ppermute | solution.py:139
  40.9 0.6 %add_bitcast_fusion = f32[1,32,256]{2,1,0:T(8,128)} fusion(f32[32,256]{1,0:T(8,128)S(1)} %get-tuple-element.23, f32[32,256]{1,0:T(8,128)S(1)} %collective-permute-done.15), kind=kLoop, calls=%fused_computation.11 | loop fusion | flops 8192 | bytes 98304 | tf_op jit(solution)/shard_map/broadcast_in_dim | solution.py:219
  (9 shorter events, 0.2 us)
Async XLA Ops:
  1.0 4.2 %copy-start.1 = (bf16[512,512]{1,0:T(8,128)(2,1)S(1)}, bf16[512,512]{1,0:T(8,128)(2,1)}, u32[]{:S(2)}) copy-start(bf16[512,512]{1,0:T(8,128)(2,1)} %param.4) | copy-start | bytes 1572868
  2.1 4.7 %copy-start.2 = (bf16[1,4,256,256]{3,2,1,0:T(8,128)(2,1)S(1)}, bf16[1,4,256,256]{3,2,1,0:T(8,128)(2,1)}, u32[]{:S(2)}) copy-start(bf16[1,4,256,256]{3,2,1,0:T(8,128)(2,1)} %param.7) | copy-start | bytes 1572868
  2.1 6.2 %copy-start = (bf16[512,256]{1,0:T(8,128)(2,1)S(1)}, bf16[512,256]{1,0:T(8,128)(2,1)}, u32[]{:S(2)}) copy-start(bf16[512,256]{1,0:T(8,128)(2,1)} %own.1) | copy-start | bytes 786436
  2.1 16.1 %collective-permute-start = (bf16[544,512]{1,0:T(8,128)(2,1)S(1)}, bf16[544,512]{1,0:T(8,128)(2,1)S(1)}, u32[]{:S(2)}, u32[]{:S(2)}) collective-permute-start(bf16[544,512]{1,0:T(8,128)(2,1)S(1)} %bitcast.17), channel_id=1, source_target_pairs={{0,4},{1,5},{2,6},{3,7},{4,0},{5,1},{6,2},{7,3},{8,12},{9,13},{10,... | collective-permute-start | bytes 1671176 | tf_op jit(solution)/shard_map/ppermute | solution.py:139
  5.2 12.5 %collective-permute-start.1 = (bf16[272,512]{1,0:T(8,128)(2,1)S(1)}, bf16[272,512]{1,0:T(8,128)(2,1)S(1)}, u32[]{:S(2)}, u32[]{:S(2)}) collective-permute-start(bf16[272,512]{1,0:T(8,128)(2,1)S(1)} %get-tuple-element.26.refs_0_), channel_id=1, source_target_pairs={{0,8},{1,9},{2,10},{3,11},{4,12},{5,13},{6,14},{7,15},{8,0},{9,1},... | collective-permute-start | bytes 835592 | tf_op jit(solution)/shard_map/ppermute | solution.py:139
  6.9 22.7 %collective-permute-start.6 = (bf16[4,256,256]{2,1,0:T(8,128)(2,1)S(1)}, bf16[4,256,256]{2,1,0:T(8,128)(2,1)S(1)}, u32[]{:S(2)}, u32[]{:S(2)}) collective-permute-start(bf16[4,256,256]{2,1,0:T(8,128)(2,1)S(1)} %bitcast.18), channel_id=1, source_target_pairs={{0,2},{1,3},{2,0},{3,1},{4,6},{5,7},{6,4},{7,5},{8,10},{9,11},{10,... | collective-permute-start | bytes 1572872 | tf_op jit(solution)/shard_map/ppermute | solution.py:139
  8.4 9.3 %collective-permute-start.3 = (bf16[256,256]{1,0:T(8,128)(2,1)S(1)}, bf16[256,256]{1,0:T(8,128)(2,1)S(1)}, u32[]{:S(2)}, u32[]{:S(2)}) collective-permute-start(bf16[256,256]{1,0:T(8,128)(2,1)S(1)} %half.1.refs_5_), channel_id=1, source_target_pairs={{0,16},{1,17},{2,18},{3,19},{4,20},{5,21},{6,22},{7,23},{8,24},{9,... | collective-permute-start | bytes 393224 | tf_op jit(solution)/shard_map/ppermute | solution.py:139
  11.0 11.2 %collective-permute-start.9 = (bf16[272,512]{1,0:T(8,128)(2,1)S(1)}, bf16[272,512]{1,0:T(8,128)(2,1)S(1)}, u32[]{:S(2)}, u32[]{:S(2)}) collective-permute-start(bf16[272,512]{1,0:T(8,128)(2,1)S(1)} %get-tuple-element.25.refs_0_), channel_id=1, source_target_pairs={{0,8},{1,9},{2,10},{3,11},{4,12},{5,13},{6,14},{7,15},{8,0},{9,1},... | collective-permute-start | bytes 835592 | tf_op jit(solution)/shard_map/ppermute | solution.py:139
  17.7 7.2 %collective-permute-start.2 = (bf16[272,512]{1,0:T(8,128)(2,1)S(1)}, bf16[272,512]{1,0:T(8,128)(2,1)S(1)}, u32[]{:S(2)}, u32[]{:S(2)}) collective-permute-start(bf16[272,512]{1,0:T(8,128)(2,1)S(1)} %collective-permute-done.1.refs_2_), channel_id=1, source_target_pairs={{0,4},{1,5},{2,6},{3,7},{4,0},{5,1},{6,2},{7,3},{8,12},{9,13},{10,... | collective-permute-start | bytes 835592 | tf_op jit(solution)/shard_map/ppermute | solution.py:139
  18.2 6.2 %collective-permute-start.4 = (bf16[256,256]{1,0:T(8,128)(2,1)S(1)}, bf16[256,256]{1,0:T(8,128)(2,1)S(1)}, u32[]{:S(2)}, u32[]{:S(2)}) collective-permute-start(bf16[256,256]{1,0:T(8,128)(2,1)S(1)} %hold.1), channel_id=1, source_target_pairs={{0,1},{1,0},{2,3},{3,2},{4,5},{5,4},{6,7},{7,6},{8,9},{9,8},{10,11... | collective-permute-start | bytes 393224 | tf_op jit(solution)/shard_map/ppermute | solution.py:139
  22.2 8.0 %collective-permute-start.11 = (bf16[128,512]{1,0:T(8,128)(2,1)S(1)}, bf16[128,512]{1,0:T(8,128)(2,1)S(1)}, u32[]{:S(2)}, u32[]{:S(2)}) collective-permute-start(bf16[128,512]{1,0:T(8,128)(2,1)S(1)} %slice.46), channel_id=1, source_target_pairs={{0,4},{1,5},{2,6},{3,7},{4,0},{5,1},{6,2},{7,3},{8,12},{9,13},{10,... | collective-permute-start | bytes 393224 | tf_op jit(solution)/shard_map/ppermute | solution.py:139
  22.6 7.5 %collective-permute-start.10 = (bf16[144,512]{1,0:T(8,128)(2,1)S(1)}, bf16[144,512]{1,0:T(8,128)(2,1)S(1)}, u32[]{:S(2)}, u32[]{:S(2)}) collective-permute-start(bf16[144,512]{1,0:T(8,128)(2,1)S(1)} %slice.45), channel_id=1, source_target_pairs={{0,8},{1,9},{2,10},{3,11},{4,12},{5,13},{6,14},{7,15},{8,0},{9,1},... | collective-permute-start | bytes 442376 | tf_op jit(solution)/shard_map/ppermute | solution.py:139
  25.6 9.2 %collective-permute-start.7 = (bf16[128,256]{1,0:T(8,128)(2,1)S(1)}, bf16[128,256]{1,0:T(8,128)(2,1)S(1)}, u32[]{:S(2)}, u32[]{:S(2)}) collective-permute-start(bf16[128,256]{1,0:T(8,128)(2,1)S(1)} %get-tuple-element.16.refs_6_), channel_id=1, source_target_pairs={{0,16},{1,17},{2,18},{3,19},{4,20},{5,21},{6,22},{7,23},{8,24},{9,... | collective-permute-start | bytes 196616 | tf_op jit(solution)/shard_map/ppermute | solution.py:139
  27.9 8.9 %collective-permute-start.5 = (bf16[128,256]{1,0:T(8,128)(2,1)S(1)}, bf16[128,256]{1,0:T(8,128)(2,1)S(1)}, u32[]{:S(2)}, u32[]{:S(2)}) collective-permute-start(bf16[128,256]{1,0:T(8,128)(2,1)S(1)} %get-tuple-element.15), channel_id=1, source_target_pairs={{0,18},{1,19},{2,16},{3,17},{4,22},{5,23},{6,20},{7,21},{8,26},{9,... | collective-permute-start | bytes 196616 | tf_op jit(solution)/shard_map/ppermute | solution.py:139
  29.6 7.2 %collective-permute-start.8 = (bf16[128,256]{1,0:T(8,128)(2,1)S(1)}, bf16[128,256]{1,0:T(8,128)(2,1)S(1)}, u32[]{:S(2)}, u32[]{:S(2)}) collective-permute-start(bf16[128,256]{1,0:T(8,128)(2,1)S(1)} %get-tuple-element.17), channel_id=1, source_target_pairs={{0,2},{1,3},{2,0},{3,1},{4,6},{5,7},{6,4},{7,5},{8,10},{9,11},{10,... | collective-permute-start | bytes 196616 | tf_op jit(solution)/shard_map/ppermute | solution.py:139
  30.9 7.7 %collective-permute-start.12 = (bf16[128,256]{1,0:T(8,128)(2,1)S(1)}, bf16[128,256]{1,0:T(8,128)(2,1)S(1)}, u32[]{:S(2)}, u32[]{:S(2)}) collective-permute-start(bf16[128,256]{1,0:T(8,128)(2,1)S(1)} %get-tuple-element.19), channel_id=1, source_target_pairs={{0,18},{1,19},{2,16},{3,17},{4,22},{5,23},{6,20},{7,21},{8,26},{9,... | collective-permute-start | bytes 196616 | tf_op jit(solution)/shard_map/ppermute | solution.py:139
  34.1 5.2 %collective-permute-start.13 = (bf16[128,256]{1,0:T(8,128)(2,1)S(1)}, bf16[128,256]{1,0:T(8,128)(2,1)S(1)}, u32[]{:S(2)}, u32[]{:S(2)}) collective-permute-start(bf16[128,256]{1,0:T(8,128)(2,1)S(1)} %get-tuple-element.20), channel_id=1, source_target_pairs={{0,16},{1,17},{2,18},{3,19},{4,20},{5,21},{6,22},{7,23},{8,24},{9,... | collective-permute-start | bytes 196616 | tf_op jit(solution)/shard_map/ppermute | solution.py:139
  34.9 4.5 %collective-permute-start.14 = (bf16[128,256]{1,0:T(8,128)(2,1)S(1)}, bf16[128,256]{1,0:T(8,128)(2,1)S(1)}, u32[]{:S(2)}, u32[]{:S(2)}) collective-permute-start(bf16[128,256]{1,0:T(8,128)(2,1)S(1)} %get-tuple-element.21), channel_id=1, source_target_pairs={{0,2},{1,3},{2,0},{3,1},{4,6},{5,7},{6,4},{7,5},{8,10},{9,11},{10,... | collective-permute-start | bytes 196616 | tf_op jit(solution)/shard_map/ppermute | solution.py:139
  39.6 1.3 %collective-permute-start.15 = (f32[32,256]{1,0:T(8,128)S(1)}, f32[32,256]{1,0:T(8,128)S(1)}, u32[]{:S(2)}, u32[]{:S(2)}) collective-permute-start(f32[32,256]{1,0:T(8,128)S(1)} %get-tuple-element.24), channel_id=1, source_target_pairs={{0,1},{1,0},{2,3},{3,2},{4,5},{5,4},{6,7},{7,6},{8,9},{9,8},{10,11... | collective-permute-start | bytes 98312 | tf_op jit(solution)/shard_map/ppermute | solution.py:139

commit v9 on v8

--- a/solution.py
+++ b/solution.py
@@ -9,6 +9,7 @@
 KERNEL_VMEM = 16 << 20
 SQUARE = 4
 CHUNK = 2
+SOON, FIRST = 10**9, 10**10
 VMEM = pl.BlockSpec(memory_space=pltpu.VMEM)
 ANY = pl.BlockSpec(memory_space=pl.ANY)
 
@@ -64,23 +65,29 @@
 def sums_kernel(picks, fars, chunk, split, own, first, second, corner, *rest):
     tail, rest = (rest[0], rest[1:]) if split else (None, rest)
     panels, after, *messages, total = rest
-    pairs = len(messages) // len(fars)
-    share = messages[0].shape[0] // CHUNK
-    rows, width, size = share * pairs, panels.shape[2], own.shape[0]
+    rows, width, size = total.shape[1], panels.shape[2], own.shape[0]
     place, x, _ = position()
     starts = [(own, 0), (first, chunk * size), (second, 0)]
-    every = [source_of(array, start, size, rows) for array, start in starts]
-    every.append(source_of(corner, 0, size, rows, tail))
+    sources = [source_of(array, start, size, rows) for array, start in starts]
+    sources.append(source_of(corner, 0, size, rows, tail))
+    zeros = [jnp.zeros((rows, width), jnp.float32)] * CHUNK
+    at = 0
     for p, far in enumerate(fars):
-        sums = [jnp.zeros((rows, width), jnp.float32)] * CHUNK
-        for n, one in enumerate(add_products(picks, place ^ far, panels[p], every, sums)):
+        sums = add_products(picks, place ^ far, panels[p], sources, zeros)
+        if not far:
+            for n, one in enumerate(sums):
+                messages[at][n * rows : (n + 1) * rows, :] = one.astype(messages[at].dtype)
+            at += 1
+            continue
+        for n, one in enumerate(sums):
             total[n] = one
-        for t in range(pairs):
+        share = messages[at].shape[0] // CHUNK
+        for t in range(rows // share):
             start = pl.multiple_of((x ^ t) * share, share)
             for n in range(CHUNK):
                 block = total[n, pl.ds(start, share), :]
-                message = messages[p * pairs + t]
-                message[n * share : (n + 1) * share, :] = block.astype(message.dtype)
+                messages[at][n * share : (n + 1) * share, :] = block.astype(messages[at].dtype)
+            at += 1
 
 
 def virtual_sum(rows, operands):
@@ -93,15 +100,24 @@
     return result
 
 
-def first_kernel(*refs):
+def whole_kernel(count, *refs):
+    operands, pieces, total = refs[:count], refs[count:-1], refs[-1]
+    total[...] = virtual_sum(total.shape[0], operands)
+    share = pieces[0].shape[0]
+    x = position()[1]
+    for t, piece in enumerate(pieces):
+        piece[...] = total[pl.ds(pl.multiple_of((x ^ t) * share, share), share), :]
+
+
+def far_kernel(*refs):
     *operands, total = refs
     total[...] = virtual_sum(total.shape[0], operands)
 
 
-def last_kernel(before, *refs):
-    *operands, stays, leaves, total = refs
+def split_kernel(*refs):
+    *parts, stays, leaves, total = refs
     middle = stays.shape[0]
-    total[...] = before[...] + virtual_sum(total.shape[0], operands)
+    total[...] = sum(part[...] for part in parts)
     core = position()[2]
     stays[...] = total[pl.ds(pl.multiple_of(core * middle, middle), middle), :]
     leaves[...] = total[pl.ds(pl.multiple_of((1 - core) * middle, middle), middle), :]
@@ -173,18 +189,22 @@
         "join",
         like((len(fars),) + green_occ.shape, green_occ.dtype),
         [VMEM] * (1 + len(halves)),
-        10**9,
+        SOON,
     )
     panels = join(green_occ, *halves)
 
+    blocks = [virtual_blocks[0, n * CHUNK : (n + 1) * CHUNK] for n in chunks]
+    ordered = sorted(chunks, key=lambda n: not near[n])
     virtual = [virtual_blocks[0]]
     virtual += [send(virtual[0], 0, 2 * t) for t in range(1, pairs)]
     virtual = [[array[n * CHUNK : (n + 1) * CHUNK] for n in chunks] for array in virtual]
 
-    after, operands = mine, {}
-    ordered = sorted(chunks, key=lambda n: not near[n])
+    after, own_operands, far_operands = mine, [], []
     for n in ordered:
-        outs = [like((CHUNK * share, width), jnp.bfloat16)] * (len(fars) * pairs)
+        kept_rows, cut_rows = (like((CHUNK * size_of, width), jnp.bfloat16) for size_of in (rows, share))
+        outs = []
+        for far in fars:
+            outs += [cut_rows] * pairs if far else [kept_rows]
         sums = call(
             lambda *refs, n=n: sums_kernel(picks, fars, n, not near[n], *refs),
             "sums",
@@ -193,29 +213,34 @@
             0,
             [pltpu.VMEM((CHUNK, rows, width), jnp.float32)],
         )
-        parts = sums(own[n], first, second[n], *corner[n], panels, after)
+        parts = list(sums(own[n], first, second[n], *corner[n], panels, after))
         after = parts[0]
-        operands[n] = []
-        for p, far in enumerate(fars):
-            for t in reversed(range(pairs)):
-                part = parts[p * pairs + t]
-                message = send(part, far, 2 * t) if far or t else part
-                operands[n] += [message, virtual[t][n]]
-
-    *early, late = ordered
-    operands_of = [array for n in early for array in operands[n]]
-    part = call(
-        first_kernel, "virtual_first", like((share, columns), jnp.float32), [VMEM] * len(operands_of), 10**9
-    )(*operands_of)
-    last = call(
-        last_kernel,
-        "virtual_last",
-        [like((share // 2, columns), jnp.float32)] * 2,
-        [VMEM] * (1 + len(operands[late])),
+        far_operands.append([])
+        for far in fars:
+            if far:
+                cut_parts, parts = parts[:pairs], parts[pairs:]
+                for t in range(pairs):
+                    far_operands[-1] += [send(cut_parts[t], far, 2 * t), virtual[t][n]]
+            else:
+                own_operands += [parts.pop(0), blocks[n]]
+
+    piece = like((share, columns), jnp.float32)
+    whole_product = call(
+        lambda *refs: whole_kernel(len(own_operands), *refs),
+        "virtual_own",
+        [piece] * pairs,
+        [VMEM] * len(own_operands),
         0,
-        [pltpu.VMEM((share, columns), jnp.float32)],
+        [pltpu.VMEM((rows, columns), jnp.float32)],
     )
-    stays, leaves = last(part, *operands[late])
+    pieces = whole_product(*own_operands)
+    pieces = [pieces[0]] + [send(pieces[t], 0, 2 * t) for t in range(1, pairs)]
+    for each in far_operands:
+        pieces.append(call(far_kernel, "virtual_far", piece, [VMEM] * len(each), FIRST)(*each))
+    half_piece = like((share // 2, columns), jnp.float32)
+    scratch = [pltpu.VMEM(piece.shape, piece.dtype)]
+    split = call(split_kernel, "split", [half_piece] * 2, [VMEM] * len(pieces), 0, scratch)
+    stays, leaves = split(*pieces)
     return (stays + send(leaves, 0, 1))[None]
 
 

time: 41.7 us -> 41.6 us (level)
  starting transfers between devices: 20.6 us -> 20.1 us
    ppermute x16 -> x15, starting transfers between devices: 20.6 us -> 20.1 us  [send(): return lax.ppermute(array, AXES, order)]
    ppermute x16 -> x15, waiting for transfers between devices: 15.8 us -> 16.1 us  [send(): return lax.ppermute(array, AXES, order)]
    pallas_call x7 -> x9, Pallas kernels: 2.18 us -> 2.21 us  [run(): pl.pallas_call(kernel, out_shape=out, in_specs=specs, out_specs=jax.tree....]
  transfers between devices with their start and end apart: 16 -> 15, of which waited for: 9 -> 8; matrix products, arithmetic and copies ran while one was open for 0% -> 0% of each run, Pallas kernels for 5% -> 5%
where the time goes in v9:
time: 41.6 us; the launch traced here: 41.4 us
  starting transfers between devices  20.1 us (48%)
  waiting for transfers between devices  16.1 us (39%)
  other arithmetic  2.49 us (6%)
  Pallas kernels  2.21 us (5%)
    ppermute x15, starting transfers between devices, send(): return lax.ppermute(array, AXES, order)  20.1 us
    ppermute x15, waiting for transfers between devices, send(): return lax.ppermute(array, AXES, order)  16.1 us
    pallas_call x9, Pallas kernels, run(): pl.pallas_call(kernel, out_shape=out, in_specs=specs, out_specs=jax.tree....  2.21 us
    concatenate x1, other arithmetic, shards(): whole = jnp.concatenate([named, blocks], axis=1)  1.15 us
  transfers between devices with their start and end apart: 15, of which 8 were waited for; matrix products, arithmetic and copies ran while one was open for 0% of the time, Pallas kernels for 5%

profile of v9, /device:TPU:0, one launch (start us, length us, event | category | flops | bytes accessed | tf_op | source)
XLA Modules:
  0.0 41.4 jit_solution(8894768518521470584)
XLA Ops:
  0.0 0.7 %convert_element_type.16 = bf16[4,2]{0,1:T(2,128)(2,1)S(1)} convert(s32[4,2]{0,1:T(2,128)} %param.6) | non-fusion elementwise | flops 8 | bytes 48 | tf_op jit(solution)/shard_map/convert_element_type | solution.py:166
  0.7 0.1 copy.6
  0.8 0.1 convert_element_type.17
  0.9 0.1 broadcast_in_dim.11
  1.0 0.0 copy-start.1
  1.0 1.2 %pad_maximum_fusion = bf16[2,272,512]{2,1,0:T(8,128)(2,1)S(1)} fusion(bf16[2,16,512]{2,1,0:T(8,128)(2,1)S(1)} %broadcast_in_dim.11, bf16[2,256,512]{2,1,0:T(8,128)(2,1)} %bitcast.15), kind=kLoop, calls=%fused_computation.2 | loop fusion | flops 1114112 | bytes 1114112 | tf_op jit(solution)/shard_map/concatenate | solution.py:169
  2.1 0.0 copy-start.2
  2.1 0.0 copy-start
  2.1 3.0 %collective-permute-start = (bf16[544,512]{1,0:T(8,128)(2,1)S(1)}, bf16[544,512]{1,0:T(8,128)(2,1)S(1)}, u32[]{:S(2)}, u32[]{:S(2)}) collective-permute-start(bf16[544,512]{1,0:T(8,128)(2,1)S(1)} %bitcast.17), channel_id=1, source_target_pairs={{0,4},{1,5},{2,6},{3,7},{4,0},{5,1},{6,2},{7,3},{8,12},{9,13},{10,... | collective-permute-start | bytes 1671176 | tf_op jit(solution)/shard_map/ppermute | solution.py:155
  5.2 0.0 copy-done.1
  5.2 1.6 %collective-permute-start.1 = (bf16[272,512]{1,0:T(8,128)(2,1)S(1)}, bf16[272,512]{1,0:T(8,128)(2,1)S(1)}, u32[]{:S(2)}, u32[]{:S(2)}) collective-permute-start(bf16[272,512]{1,0:T(8,128)(2,1)S(1)} %get-tuple-element.26.refs_0_), channel_id=1, source_target_pairs={{0,8},{1,9},{2,10},{3,11},{4,12},{5,13},{6,14},{7,15},{8,0},{9,1},... | collective-permute-start | bytes 835592 | tf_op jit(solution)/shard_map/ppermute | solution.py:155
  6.9 0.0 copy-done.2
  6.9 1.5 %collective-permute-start.11 = (bf16[4,256,256]{2,1,0:T(8,128)(2,1)S(1)}, bf16[4,256,256]{2,1,0:T(8,128)(2,1)S(1)}, u32[]{:S(2)}, u32[]{:S(2)}) collective-permute-start(bf16[4,256,256]{2,1,0:T(8,128)(2,1)S(1)} %bitcast.18), channel_id=1, source_target_pairs={{0,2},{1,3},{2,0},{3,1},{4,6},{5,7},{6,4},{7,5},{8,10},{9,11},{10,... | collective-permute-start | bytes 1572872 | tf_op jit(solution)/shard_map/ppermute | solution.py:155
  8.4 0.0 copy-done
  8.4 2.7 %collective-permute-start.3 = (bf16[256,256]{1,0:T(8,128)(2,1)S(1)}, bf16[256,256]{1,0:T(8,128)(2,1)S(1)}, u32[]{:S(2)}, u32[]{:S(2)}) collective-permute-start(bf16[256,256]{1,0:T(8,128)(2,1)S(1)} %half.1.refs_5_), channel_id=1, source_target_pairs={{0,16},{1,17},{2,18},{3,19},{4,20},{5,21},{6,22},{7,23},{8,24},{9,... | collective-permute-start | bytes 393224 | tf_op jit(solution)/shard_map/ppermute | solution.py:155
  11.0 0.4 %collective-permute-start.5 = (bf16[272,512]{1,0:T(8,128)(2,1)S(1)}, bf16[272,512]{1,0:T(8,128)(2,1)S(1)}, u32[]{:S(2)}, u32[]{:S(2)}) collective-permute-start(bf16[272,512]{1,0:T(8,128)(2,1)S(1)} %get-tuple-element.25.refs_0_), channel_id=1, source_target_pairs={{0,8},{1,9},{2,10},{3,11},{4,12},{5,13},{6,14},{7,15},{8,0},{9,1},... | collective-permute-start | bytes 835592 | tf_op jit(solution)/shard_map/ppermute | solution.py:155
  11.5 6.2 %collective-permute-done.1.refs_2_ = bf16[272,512]{1,0:T(8,128)(2,1)S(1)} collective-permute-done((bf16[272,512]{1,0:T(8,128)(2,1)S(1)}, bf16[272,512]{1,0:T(8,128)(2,1)S(1)}, u32[]{:S(2)}, u32[]{:S(2)}) %collective-permute-start.1) | collective-permute-done | bytes 278560 | tf_op jit(solution)/shard_map/ppermute | solution.py:155
  17.7 0.0 collective-permute-start.2
  17.7 0.0 collective-permute-done.3.array.rest_0_
  17.7 0.5 %collective-permute-done.after.refs_1_ = bf16[544,512]{1,0:T(8,128)(2,1)S(1)} collective-permute-done((bf16[544,512]{1,0:T(8,128)(2,1)S(1)}, bf16[544,512]{1,0:T(8,128)(2,1)S(1)}, u32[]{:S(2)}, u32[]{:S(2)}) %collective-permute-start) | collective-permute-done | bytes 557088 | tf_op jit(solution)/shard_map/ppermute | solution.py:155
  18.2 0.1 collective-permute-start.4
  18.3 3.8 %collective-permute-done.5.refs_2_ = bf16[272,512]{1,0:T(8,128)(2,1)S(1)} collective-permute-done((bf16[272,512]{1,0:T(8,128)(2,1)S(1)}, bf16[272,512]{1,0:T(8,128)(2,1)S(1)}, u32[]{:S(2)}, u32[]{:S(2)}) %collective-permute-start.5) | collective-permute-done | bytes 278560 | tf_op jit(solution)/shard_map/ppermute | solution.py:155
  22.2 0.4 collective-permute-start.7
  22.6 1.8 %collective-permute-start.6 = (bf16[144,512]{1,0:T(8,128)(2,1)S(1)}, bf16[144,512]{1,0:T(8,128)(2,1)S(1)}, u32[]{:S(2)}, u32[]{:S(2)}) collective-permute-start(bf16[144,512]{1,0:T(8,128)(2,1)S(1)} %slice.40), channel_id=1, source_target_pairs={{0,8},{1,9},{2,10},{3,11},{4,12},{5,13},{6,14},{7,15},{8,0},{9,1},... | collective-permute-start | bytes 442376 | tf_op jit(solution)/shard_map/ppermute | solution.py:155
  24.4 0.0 collective-permute-done.4.rest_1_
  24.5 0.4 %collective-permute-done.2.refs_3_ = bf16[272,512]{1,0:T(8,128)(2,1)S(1)} collective-permute-done((bf16[272,512]{1,0:T(8,128)(2,1)S(1)}, bf16[272,512]{1,0:T(8,128)(2,1)S(1)}, u32[]{:S(2)}, u32[]{:S(2)}) %collective-permute-start.2) | collective-permute-done | bytes 278560 | tf_op jit(solution)/shard_map/ppermute | solution.py:155
  24.9 0.7 %sums.2 = (bf16[128,256]{1,0:T(8,128)(2,1)S(1)}, bf16[128,256]{1,0:T(8,128)(2,1)S(1)}, bf16[256,256]{1,0:T(8,128)(2,1)S(1)}) custom-call(bf16[272,512]{1,0:T(8,128)(2,1)S(1)} %get-tuple-element.26.refs_0_, bf16[544,512]{1,0:T(8,128)(2,1)S(1)} %collective-permute-done.after.refs_1_, bf16[272,512]{1,0:T(8,128)(2,1)S(1)} %collective-permute-done.1.refs_2_, ...), custom_call_target="tpu_custom_call" | custom-call | tf_op jit(solution)/shard_map/sums/pallas_call | solution.py:128
  25.6 2.2 %collective-permute-start.9 = (bf16[128,256]{1,0:T(8,128)(2,1)S(1)}, bf16[128,256]{1,0:T(8,128)(2,1)S(1)}, u32[]{:S(2)}, u32[]{:S(2)}) collective-permute-start(bf16[128,256]{1,0:T(8,128)(2,1)S(1)} %get-tuple-element.16.refs_6_), channel_id=1, source_target_pairs={{0,16},{1,17},{2,18},{3,19},{4,20},{5,21},{6,22},{7,23},{8,24},{9,... | collective-permute-start | bytes 196616 | tf_op jit(solution)/shard_map/ppermute | solution.py:155
  27.9 1.7 %collective-permute-start.10 = (bf16[128,256]{1,0:T(8,128)(2,1)S(1)}, bf16[128,256]{1,0:T(8,128)(2,1)S(1)}, u32[]{:S(2)}, u32[]{:S(2)}) collective-permute-start(bf16[128,256]{1,0:T(8,128)(2,1)S(1)} %get-tuple-element.20), channel_id=1, source_target_pairs={{0,18},{1,19},{2,16},{3,17},{4,22},{5,23},{6,20},{7,21},{8,26},{9,... | collective-permute-start | bytes 196616 | tf_op jit(solution)/shard_map/ppermute | solution.py:155
  29.6 0.0 collective-permute-done.11
  29.6 0.0 collective-permute-done.7.refs_4_
  29.6 0.0 collective-permute-done.6.refs_3_
  29.6 0.7 %sums.3 = (bf16[128,256]{1,0:T(8,128)(2,1)S(1)}, bf16[128,256]{1,0:T(8,128)(2,1)S(1)}, bf16[256,256]{1,0:T(8,128)(2,1)S(1)}) custom-call(bf16[272,512]{1,0:T(8,128)(2,1)S(1)} %get-tuple-element.25.refs_0_, bf16[544,512]{1,0:T(8,128)(2,1)S(1)} %collective-permute-done.after.refs_1_, bf16[272,512]{1,0:T(8,128)(2,1)S(1)} %collective-permute-done.5.refs_2_, ...), custom_call_target="tpu_custom_call" | custom-call | tf_op jit(solution)/shard_map/sums/pallas_call | solution.py:128
  30.4 2.2 %collective-permute-start.12 = (bf16[128,256]{1,0:T(8,128)(2,1)S(1)}, bf16[128,256]{1,0:T(8,128)(2,1)S(1)}, u32[]{:S(2)}, u32[]{:S(2)}) collective-permute-start(bf16[128,256]{1,0:T(8,128)(2,1)S(1)} %get-tuple-element.21), channel_id=1, source_target_pairs={{0,16},{1,17},{2,18},{3,19},{4,20},{5,21},{6,22},{7,23},{8,24},{9,... | collective-permute-start | bytes 196616 | tf_op jit(solution)/shard_map/ppermute | solution.py:155
  32.6 0.9 %collective-permute-start.13 = (bf16[128,256]{1,0:T(8,128)(2,1)S(1)}, bf16[128,256]{1,0:T(8,128)(2,1)S(1)}, u32[]{:S(2)}, u32[]{:S(2)}) collective-permute-start(bf16[128,256]{1,0:T(8,128)(2,1)S(1)} %get-tuple-element.22), channel_id=1, source_target_pairs={{0,18},{1,19},{2,16},{3,17},{4,22},{5,23},{6,20},{7,21},{8,26},{9,... | collective-permute-start | bytes 196616 | tf_op jit(solution)/shard_map/ppermute | solution.py:155
  33.5 0.2 virtual_own.1
  33.8 1.3 %collective-permute-start.8 = (f32[64,256]{1,0:T(8,128)S(1)}, f32[64,256]{1,0:T(8,128)S(1)}, u32[]{:S(2)}, u32[]{:S(2)}) collective-permute-start(f32[64,256]{1,0:T(8,128)S(1)} %get-tuple-element.19), channel_id=1, source_target_pairs={{0,2},{1,3},{2,0},{3,1},{4,6},{5,7},{6,4},{7,5},{8,10},{9,11},{10,... | collective-permute-start | bytes 196616 | tf_op jit(solution)/shard_map/ppermute | solution.py:155
  35.1 0.0 collective-permute-done.9.refs_0_
  35.1 2.6 %collective-permute-done.10.refs_2_ = bf16[128,256]{1,0:T(8,128)(2,1)S(1)} collective-permute-done((bf16[128,256]{1,0:T(8,128)(2,1)S(1)}, bf16[128,256]{1,0:T(8,128)(2,1)S(1)}, u32[]{:S(2)}, u32[]{:S(2)}) %collective-permute-start.10) | collective-permute-done | bytes 65568 | tf_op jit(solution)/shard_map/ppermute | solution.py:155
  37.7 0.2 virtual_far.2.refs_2_
  37.9 0.6 %collective-permute-done.12.refs_0_ = bf16[128,256]{1,0:T(8,128)(2,1)S(1)} collective-permute-done((bf16[128,256]{1,0:T(8,128)(2,1)S(1)}, bf16[128,256]{1,0:T(8,128)(2,1)S(1)}, u32[]{:S(2)}, u32[]{:S(2)}) %collective-permute-start.12) | collective-permute-done | bytes 65568 | tf_op jit(solution)/shard_map/ppermute | solution.py:155
  38.5 0.8 %collective-permute-done.13.refs_2_ = bf16[128,256]{1,0:T(8,128)(2,1)S(1)} collective-permute-done((bf16[128,256]{1,0:T(8,128)(2,1)S(1)}, bf16[128,256]{1,0:T(8,128)(2,1)S(1)}, u32[]{:S(2)}, u32[]{:S(2)}) %collective-permute-start.13) | collective-permute-done | bytes 65568 | tf_op jit(solution)/shard_map/ppermute | solution.py:155
  39.3 0.2 virtual_far.3.refs_3_
  39.5 0.0 collective-permute-done.8.refs_1_
  39.5 0.1 collective-permute-start.14
  39.6 1.2 %collective-permute-done.14 = f32[32,256]{1,0:T(8,128)S(1)} collective-permute-done((f32[32,256]{1,0:T(8,128)S(1)}, f32[32,256]{1,0:T(8,128)S(1)}, u32[]{:S(2)}, u32[]{:S(2)}) %collective-permute-start.14) | collective-permute-done | bytes 32800 | tf_op jit(solution)/shard_map/ppermute | solution.py:155
  40.8 0.6 %add_bitcast_fusion = f32[1,32,256]{2,1,0:T(8,128)} fusion(f32[32,256]{1,0:T(8,128)S(1)} %get-tuple-element.23, f32[32,256]{1,0:T(8,128)S(1)} %collective-permute-done.14), kind=kLoop, calls=%fused_computation.11 | loop fusion | flops 8192 | bytes 98304 | tf_op jit(solution)/shard_map/broadcast_in_dim | solution.py:244
  (10 shorter events, 0.2 us)
Async XLA Ops:
  1.0 4.2 %copy-start.1 = (bf16[512,512]{1,0:T(8,128)(2,1)S(1)}, bf16[512,512]{1,0:T(8,128)(2,1)}, u32[]{:S(2)}) copy-start(bf16[512,512]{1,0:T(8,128)(2,1)} %param.4) | copy-start | bytes 1572868
  2.1 4.7 %copy-start.2 = (bf16[1,4,256,256]{3,2,1,0:T(8,128)(2,1)S(1)}, bf16[1,4,256,256]{3,2,1,0:T(8,128)(2,1)}, u32[]{:S(2)}) copy-start(bf16[1,4,256,256]{3,2,1,0:T(8,128)(2,1)} %param.7) | copy-start | bytes 1572868
  2.1 6.2 %copy-start = (bf16[512,256]{1,0:T(8,128)(2,1)S(1)}, bf16[512,256]{1,0:T(8,128)(2,1)}, u32[]{:S(2)}) copy-start(bf16[512,256]{1,0:T(8,128)(2,1)} %own.1) | copy-start | bytes 786436
  2.1 16.1 %collective-permute-start = (bf16[544,512]{1,0:T(8,128)(2,1)S(1)}, bf16[544,512]{1,0:T(8,128)(2,1)S(1)}, u32[]{:S(2)}, u32[]{:S(2)}) collective-permute-start(bf16[544,512]{1,0:T(8,128)(2,1)S(1)} %bitcast.17), channel_id=1, source_target_pairs={{0,4},{1,5},{2,6},{3,7},{4,0},{5,1},{6,2},{7,3},{8,12},{9,13},{10,... | collective-permute-start | bytes 1671176 | tf_op jit(solution)/shard_map/ppermute | solution.py:155
  5.2 12.5 %collective-permute-start.1 = (bf16[272,512]{1,0:T(8,128)(2,1)S(1)}, bf16[272,512]{1,0:T(8,128)(2,1)S(1)}, u32[]{:S(2)}, u32[]{:S(2)}) collective-permute-start(bf16[272,512]{1,0:T(8,128)(2,1)S(1)} %get-tuple-element.26.refs_0_), channel_id=1, source_target_pairs={{0,8},{1,9},{2,10},{3,11},{4,12},{5,13},{6,14},{7,15},{8,0},{9,1},... | collective-permute-start | bytes 835592 | tf_op jit(solution)/shard_map/ppermute | solution.py:155
  6.9 22.7 %collective-permute-start.11 = (bf16[4,256,256]{2,1,0:T(8,128)(2,1)S(1)}, bf16[4,256,256]{2,1,0:T(8,128)(2,1)S(1)}, u32[]{:S(2)}, u32[]{:S(2)}) collective-permute-start(bf16[4,256,256]{2,1,0:T(8,128)(2,1)S(1)} %bitcast.18), channel_id=1, source_target_pairs={{0,2},{1,3},{2,0},{3,1},{4,6},{5,7},{6,4},{7,5},{8,10},{9,11},{10,... | collective-permute-start | bytes 1572872 | tf_op jit(solution)/shard_map/ppermute | solution.py:155
  8.4 9.3 %collective-permute-start.3 = (bf16[256,256]{1,0:T(8,128)(2,1)S(1)}, bf16[256,256]{1,0:T(8,128)(2,1)S(1)}, u32[]{:S(2)}, u32[]{:S(2)}) collective-permute-start(bf16[256,256]{1,0:T(8,128)(2,1)S(1)} %half.1.refs_5_), channel_id=1, source_target_pairs={{0,16},{1,17},{2,18},{3,19},{4,20},{5,21},{6,22},{7,23},{8,24},{9,... | collective-permute-start | bytes 393224 | tf_op jit(solution)/shard_map/ppermute | solution.py:155
  11.0 11.2 %collective-permute-start.5 = (bf16[272,512]{1,0:T(8,128)(2,1)S(1)}, bf16[272,512]{1,0:T(8,128)(2,1)S(1)}, u32[]{:S(2)}, u32[]{:S(2)}) collective-permute-start(bf16[272,512]{1,0:T(8,128)(2,1)S(1)} %get-tuple-element.25.refs_0_), channel_id=1, source_target_pairs={{0,8},{1,9},{2,10},{3,11},{4,12},{5,13},{6,14},{7,15},{8,0},{9,1},... | collective-permute-start | bytes 835592 | tf_op jit(solution)/shard_map/ppermute | solution.py:155
  17.7 7.2 %collective-permute-start.2 = (bf16[272,512]{1,0:T(8,128)(2,1)S(1)}, bf16[272,512]{1,0:T(8,128)(2,1)S(1)}, u32[]{:S(2)}, u32[]{:S(2)}) collective-permute-start(bf16[272,512]{1,0:T(8,128)(2,1)S(1)} %collective-permute-done.1.refs_2_), channel_id=1, source_target_pairs={{0,4},{1,5},{2,6},{3,7},{4,0},{5,1},{6,2},{7,3},{8,12},{9,13},{10,... | collective-permute-start | bytes 835592 | tf_op jit(solution)/shard_map/ppermute | solution.py:155
  18.2 6.2 %collective-permute-start.4 = (bf16[256,256]{1,0:T(8,128)(2,1)S(1)}, bf16[256,256]{1,0:T(8,128)(2,1)S(1)}, u32[]{:S(2)}, u32[]{:S(2)}) collective-permute-start(bf16[256,256]{1,0:T(8,128)(2,1)S(1)} %hold.1), channel_id=1, source_target_pairs={{0,1},{1,0},{2,3},{3,2},{4,5},{5,4},{6,7},{7,6},{8,9},{9,8},{10,11... | collective-permute-start | bytes 393224 | tf_op jit(solution)/shard_map/ppermute | solution.py:155
  22.2 7.4 %collective-permute-start.7 = (bf16[128,512]{1,0:T(8,128)(2,1)S(1)}, bf16[128,512]{1,0:T(8,128)(2,1)S(1)}, u32[]{:S(2)}, u32[]{:S(2)}) collective-permute-start(bf16[128,512]{1,0:T(8,128)(2,1)S(1)} %slice.41), channel_id=1, source_target_pairs={{0,4},{1,5},{2,6},{3,7},{4,0},{5,1},{6,2},{7,3},{8,12},{9,13},{10,... | collective-permute-start | bytes 393224 | tf_op jit(solution)/shard_map/ppermute | solution.py:155
  22.6 7.0 %collective-permute-start.6 = (bf16[144,512]{1,0:T(8,128)(2,1)S(1)}, bf16[144,512]{1,0:T(8,128)(2,1)S(1)}, u32[]{:S(2)}, u32[]{:S(2)}) collective-permute-start(bf16[144,512]{1,0:T(8,128)(2,1)S(1)} %slice.40), channel_id=1, source_target_pairs={{0,8},{1,9},{2,10},{3,11},{4,12},{5,13},{6,14},{7,15},{8,0},{9,1},... | collective-permute-start | bytes 442376 | tf_op jit(solution)/shard_map/ppermute | solution.py:155
  25.6 9.5 %collective-permute-start.9 = (bf16[128,256]{1,0:T(8,128)(2,1)S(1)}, bf16[128,256]{1,0:T(8,128)(2,1)S(1)}, u32[]{:S(2)}, u32[]{:S(2)}) collective-permute-start(bf16[128,256]{1,0:T(8,128)(2,1)S(1)} %get-tuple-element.16.refs_6_), channel_id=1, source_target_pairs={{0,16},{1,17},{2,18},{3,19},{4,20},{5,21},{6,22},{7,23},{8,24},{9,... | collective-permute-start | bytes 196616 | tf_op jit(solution)/shard_map/ppermute | solution.py:155
  27.9 9.8 %collective-permute-start.10 = (bf16[128,256]{1,0:T(8,128)(2,1)S(1)}, bf16[128,256]{1,0:T(8,128)(2,1)S(1)}, u32[]{:S(2)}, u32[]{:S(2)}) collective-permute-start(bf16[128,256]{1,0:T(8,128)(2,1)S(1)} %get-tuple-element.20), channel_id=1, source_target_pairs={{0,18},{1,19},{2,16},{3,17},{4,22},{5,23},{6,20},{7,21},{8,26},{9,... | collective-permute-start | bytes 196616 | tf_op jit(solution)/shard_map/ppermute | solution.py:155
  30.4 8.1 %collective-permute-start.12 = (bf16[128,256]{1,0:T(8,128)(2,1)S(1)}, bf16[128,256]{1,0:T(8,128)(2,1)S(1)}, u32[]{:S(2)}, u32[]{:S(2)}) collective-permute-start(bf16[128,256]{1,0:T(8,128)(2,1)S(1)} %get-tuple-element.21), channel_id=1, source_target_pairs={{0,16},{1,17},{2,18},{3,19},{4,20},{5,21},{6,22},{7,23},{8,24},{9,... | collective-permute-start | bytes 196616 | tf_op jit(solution)/shard_map/ppermute | solution.py:155
  32.6 6.7 %collective-permute-start.13 = (bf16[128,256]{1,0:T(8,128)(2,1)S(1)}, bf16[128,256]{1,0:T(8,128)(2,1)S(1)}, u32[]{:S(2)}, u32[]{:S(2)}) collective-permute-start(bf16[128,256]{1,0:T(8,128)(2,1)S(1)} %get-tuple-element.22), channel_id=1, source_target_pairs={{0,18},{1,19},{2,16},{3,17},{4,22},{5,23},{6,20},{7,21},{8,26},{9,... | collective-permute-start | bytes 196616 | tf_op jit(solution)/shard_map/ppermute | solution.py:155
  33.8 5.7 %collective-permute-start.8 = (f32[64,256]{1,0:T(8,128)S(1)}, f32[64,256]{1,0:T(8,128)S(1)}, u32[]{:S(2)}, u32[]{:S(2)}) collective-permute-start(f32[64,256]{1,0:T(8,128)S(1)} %get-tuple-element.19), channel_id=1, source_target_pairs={{0,2},{1,3},{2,0},{3,1},{4,6},{5,7},{6,4},{7,5},{8,10},{9,11},{10,... | collective-permute-start | bytes 196616 | tf_op jit(solution)/shard_map/ppermute | solution.py:155
  39.5 1.3 %collective-permute-start.14 = (f32[32,256]{1,0:T(8,128)S(1)}, f32[32,256]{1,0:T(8,128)S(1)}, u32[]{:S(2)}, u32[]{:S(2)}) collective-permute-start(f32[32,256]{1,0:T(8,128)S(1)} %get-tuple-element.24), channel_id=1, source_target_pairs={{0,1},{1,0},{2,3},{3,2},{4,5},{5,4},{6,7},{7,6},{8,9},{9,8},{10,11... | collective-permute-start | bytes 98312 | tf_op jit(solution)/shard_map/ppermute | solution.py:155

commit v10 on v9

--- a/solution.py
+++ b/solution.py
@@ -101,7 +101,7 @@
 
 
 def whole_kernel(count, *refs):
-    operands, pieces, total = refs[:count], refs[count:-1], refs[-1]
+    operands, pieces, total = refs[:count], refs[count + 1 : -1], refs[-1]
     total[...] = virtual_sum(total.shape[0], operands)
     share = pieces[0].shape[0]
     x = position()[1]
@@ -114,10 +114,10 @@
     total[...] = virtual_sum(total.shape[0], operands)
 
 
-def split_kernel(*refs):
-    *parts, stays, leaves, total = refs
+def last_kernel(count, *refs):
+    parts, (*operands, stays, leaves, total) = refs[:count], refs[count:]
     middle = stays.shape[0]
-    total[...] = sum(part[...] for part in parts)
+    total[...] = virtual_sum(total.shape[0], operands) + sum(part[...] for part in parts)
     core = position()[2]
     stays[...] = total[pl.ds(pl.multiple_of(core * middle, middle), middle), :]
     leaves[...] = total[pl.ds(pl.multiple_of((1 - core) * middle, middle), middle), :]
@@ -229,18 +229,27 @@
         lambda *refs: whole_kernel(len(own_operands), *refs),
         "virtual_own",
         [piece] * pairs,
-        [VMEM] * len(own_operands),
+        [VMEM] * len(own_operands) + [ANY],
         0,
         [pltpu.VMEM((rows, columns), jnp.float32)],
     )
-    pieces = whole_product(*own_operands)
+    pieces = whole_product(*own_operands, far_operands[0][0])
     pieces = [pieces[0]] + [send(pieces[t], 0, 2 * t) for t in range(1, pairs)]
-    for each in far_operands:
+    *early_operands, late_operands = far_operands
+    for each in early_operands:
         pieces.append(call(far_kernel, "virtual_far", piece, [VMEM] * len(each), FIRST)(*each))
     half_piece = like((share // 2, columns), jnp.float32)
     scratch = [pltpu.VMEM(piece.shape, piece.dtype)]
-    split = call(split_kernel, "split", [half_piece] * 2, [VMEM] * len(pieces), 0, scratch)
-    stays, leaves = split(*pieces)
+    count = len(pieces)
+    last = call(
+        lambda *refs: last_kernel(count, *refs),
+        "virtual_last",
+        [half_piece] * 2,
+        [VMEM] * (count + len(late_operands)),
+        FIRST,
+        scratch,
+    )
+    stays, leaves = last(*pieces, *late_operands)
     return (stays + send(leaves, 0, 1))[None]
 
 

time: 41.6 us -> 41.6 us (level)
    pallas_call x9 -> x8, Pallas kernels: 2.21 us -> 2.2 us  [run(): pl.pallas_call(kernel, out_shape=out, in_specs=specs, out_specs=jax.tree....]
  transfers between devices with their start and end apart: 15 -> 15, of which waited for: 8 -> 9; matrix products, arithmetic and copies ran while one was open for 0% -> 0% of each run, Pallas kernels for 5% -> 5%
where the time goes in v10:
time: 41.6 us; the launch traced here: 41.4 us
  starting transfers between devices  20 us (48%)
  waiting for transfers between devices  16.2 us (39%)
  other arithmetic  2.49 us (6%)
  Pallas kernels  2.2 us (5%)
    ppermute x15, starting transfers between devices, send(): return lax.ppermute(array, AXES, order)  20 us
    ppermute x15, waiting for transfers between devices, send(): return lax.ppermute(array, AXES, order)  16.2 us
    pallas_call x8, Pallas kernels, run(): pl.pallas_call(kernel, out_shape=out, in_specs=specs, out_specs=jax.tree....  2.2 us
    concatenate x1, other arithmetic, shards(): whole = jnp.concatenate([named, blocks], axis=1)  1.15 us
  transfers between devices with their start and end apart: 15, of which 9 were waited for; matrix products, arithmetic and copies ran while one was open for 0% of the time, Pallas kernels for 5%

profile of v10, /device:TPU:0, one launch (start us, length us, event | category | flops | bytes accessed | tf_op | source)
XLA Modules:
  0.0 41.4 jit_solution(14341178541303510470)
XLA Ops:
  0.0 0.7 %convert_element_type.16 = bf16[4,2]{0,1:T(2,128)(2,1)S(1)} convert(s32[4,2]{0,1:T(2,128)} %param.6) | non-fusion elementwise | flops 8 | bytes 48 | tf_op jit(solution)/shard_map/convert_element_type | solution.py:166
  0.7 0.1 copy.6
  0.8 0.1 convert_element_type.17
  0.9 0.1 broadcast_in_dim.11
  1.0 0.0 copy-start.1
  1.0 1.2 %pad_maximum_fusion = bf16[2,272,512]{2,1,0:T(8,128)(2,1)S(1)} fusion(bf16[2,16,512]{2,1,0:T(8,128)(2,1)S(1)} %broadcast_in_dim.11, bf16[2,256,512]{2,1,0:T(8,128)(2,1)} %bitcast.15), kind=kLoop, calls=%fused_computation.2 | loop fusion | flops 1114112 | bytes 1114112 | tf_op jit(solution)/shard_map/concatenate | solution.py:169
  2.1 0.0 copy-start.2
  2.1 0.0 copy-start
  2.1 3.0 %collective-permute-start = (bf16[544,512]{1,0:T(8,128)(2,1)S(1)}, bf16[544,512]{1,0:T(8,128)(2,1)S(1)}, u32[]{:S(2)}, u32[]{:S(2)}) collective-permute-start(bf16[544,512]{1,0:T(8,128)(2,1)S(1)} %bitcast.17), channel_id=1, source_target_pairs={{0,4},{1,5},{2,6},{3,7},{4,0},{5,1},{6,2},{7,3},{8,12},{9,13},{10,... | collective-permute-start | bytes 1671176 | tf_op jit(solution)/shard_map/ppermute | solution.py:155
  5.2 0.0 copy-done.1
  5.2 1.6 %collective-permute-start.1 = (bf16[272,512]{1,0:T(8,128)(2,1)S(1)}, bf16[272,512]{1,0:T(8,128)(2,1)S(1)}, u32[]{:S(2)}, u32[]{:S(2)}) collective-permute-start(bf16[272,512]{1,0:T(8,128)(2,1)S(1)} %get-tuple-element.26.refs_0_), channel_id=1, source_target_pairs={{0,8},{1,9},{2,10},{3,11},{4,12},{5,13},{6,14},{7,15},{8,0},{9,1},... | collective-permute-start | bytes 835592 | tf_op jit(solution)/shard_map/ppermute | solution.py:155
  6.9 0.0 copy-done.2
  6.9 1.5 %collective-permute-start.11 = (bf16[4,256,256]{2,1,0:T(8,128)(2,1)S(1)}, bf16[4,256,256]{2,1,0:T(8,128)(2,1)S(1)}, u32[]{:S(2)}, u32[]{:S(2)}) collective-permute-start(bf16[4,256,256]{2,1,0:T(8,128)(2,1)S(1)} %bitcast.18), channel_id=1, source_target_pairs={{0,2},{1,3},{2,0},{3,1},{4,6},{5,7},{6,4},{7,5},{8,10},{9,11},{10,... | collective-permute-start | bytes 1572872 | tf_op jit(solution)/shard_map/ppermute | solution.py:155
  8.4 0.0 copy-done
  8.4 2.7 %collective-permute-start.3 = (bf16[256,256]{1,0:T(8,128)(2,1)S(1)}, bf16[256,256]{1,0:T(8,128)(2,1)S(1)}, u32[]{:S(2)}, u32[]{:S(2)}) collective-permute-start(bf16[256,256]{1,0:T(8,128)(2,1)S(1)} %half.1.refs_5_), channel_id=1, source_target_pairs={{0,16},{1,17},{2,18},{3,19},{4,20},{5,21},{6,22},{7,23},{8,24},{9,... | collective-permute-start | bytes 393224 | tf_op jit(solution)/shard_map/ppermute | solution.py:155
  11.0 0.4 %collective-permute-start.5 = (bf16[272,512]{1,0:T(8,128)(2,1)S(1)}, bf16[272,512]{1,0:T(8,128)(2,1)S(1)}, u32[]{:S(2)}, u32[]{:S(2)}) collective-permute-start(bf16[272,512]{1,0:T(8,128)(2,1)S(1)} %get-tuple-element.25.refs_0_), channel_id=1, source_target_pairs={{0,8},{1,9},{2,10},{3,11},{4,12},{5,13},{6,14},{7,15},{8,0},{9,1},... | collective-permute-start | bytes 835592 | tf_op jit(solution)/shard_map/ppermute | solution.py:155
  11.5 6.2 %collective-permute-done.1.refs_2_ = bf16[272,512]{1,0:T(8,128)(2,1)S(1)} collective-permute-done((bf16[272,512]{1,0:T(8,128)(2,1)S(1)}, bf16[272,512]{1,0:T(8,128)(2,1)S(1)}, u32[]{:S(2)}, u32[]{:S(2)}) %collective-permute-start.1) | collective-permute-done | bytes 278560 | tf_op jit(solution)/shard_map/ppermute | solution.py:155
  17.7 0.0 collective-permute-start.2
  17.7 0.0 collective-permute-done.3.array.rest_0_
  17.7 0.5 %collective-permute-done.after.refs_1_ = bf16[544,512]{1,0:T(8,128)(2,1)S(1)} collective-permute-done((bf16[544,512]{1,0:T(8,128)(2,1)S(1)}, bf16[544,512]{1,0:T(8,128)(2,1)S(1)}, u32[]{:S(2)}, u32[]{:S(2)}) %collective-permute-start) | collective-permute-done | bytes 557088 | tf_op jit(solution)/shard_map/ppermute | solution.py:155
  18.2 0.1 collective-permute-start.4
  18.3 3.8 %collective-permute-done.5.refs_2_ = bf16[272,512]{1,0:T(8,128)(2,1)S(1)} collective-permute-done((bf16[272,512]{1,0:T(8,128)(2,1)S(1)}, bf16[272,512]{1,0:T(8,128)(2,1)S(1)}, u32[]{:S(2)}, u32[]{:S(2)}) %collective-permute-start.5) | collective-permute-done | bytes 278560 | tf_op jit(solution)/shard_map/ppermute | solution.py:155
  22.2 0.4 collective-permute-start.7
  22.6 1.8 %collective-permute-start.6 = (bf16[144,512]{1,0:T(8,128)(2,1)S(1)}, bf16[144,512]{1,0:T(8,128)(2,1)S(1)}, u32[]{:S(2)}, u32[]{:S(2)}) collective-permute-start(bf16[144,512]{1,0:T(8,128)(2,1)S(1)} %slice.40), channel_id=1, source_target_pairs={{0,8},{1,9},{2,10},{3,11},{4,12},{5,13},{6,14},{7,15},{8,0},{9,1},... | collective-permute-start | bytes 442376 | tf_op jit(solution)/shard_map/ppermute | solution.py:155
  24.4 0.0 collective-permute-done.4.rest_1_
  24.5 0.4 %collective-permute-done.2.refs_3_ = bf16[272,512]{1,0:T(8,128)(2,1)S(1)} collective-permute-done((bf16[272,512]{1,0:T(8,128)(2,1)S(1)}, bf16[272,512]{1,0:T(8,128)(2,1)S(1)}, u32[]{:S(2)}, u32[]{:S(2)}) %collective-permute-start.2) | collective-permute-done | bytes 278560 | tf_op jit(solution)/shard_map/ppermute | solution.py:155
  24.9 0.7 %sums.2 = (bf16[128,256]{1,0:T(8,128)(2,1)S(1)}, bf16[128,256]{1,0:T(8,128)(2,1)S(1)}, bf16[256,256]{1,0:T(8,128)(2,1)S(1)}) custom-call(bf16[272,512]{1,0:T(8,128)(2,1)S(1)} %get-tuple-element.26.refs_0_, bf16[544,512]{1,0:T(8,128)(2,1)S(1)} %collective-permute-done.after.refs_1_, bf16[272,512]{1,0:T(8,128)(2,1)S(1)} %collective-permute-done.1.refs_2_, ...), custom_call_target="tpu_custom_call" | custom-call | tf_op jit(solution)/shard_map/sums/pallas_call | solution.py:128
  25.6 2.2 %collective-permute-start.8 = (bf16[128,256]{1,0:T(8,128)(2,1)S(1)}, bf16[128,256]{1,0:T(8,128)(2,1)S(1)}, u32[]{:S(2)}, u32[]{:S(2)}) collective-permute-start(bf16[128,256]{1,0:T(8,128)(2,1)S(1)} %get-tuple-element.16.refs_6_), channel_id=1, source_target_pairs={{0,16},{1,17},{2,18},{3,19},{4,20},{5,21},{6,22},{7,23},{8,24},{9,... | collective-permute-start | bytes 196616 | tf_op jit(solution)/shard_map/ppermute | solution.py:155
  27.9 1.7 %collective-permute-start.10 = (bf16[128,256]{1,0:T(8,128)(2,1)S(1)}, bf16[128,256]{1,0:T(8,128)(2,1)S(1)}, u32[]{:S(2)}, u32[]{:S(2)}) collective-permute-start(bf16[128,256]{1,0:T(8,128)(2,1)S(1)} %get-tuple-element.20), channel_id=1, source_target_pairs={{0,18},{1,19},{2,16},{3,17},{4,22},{5,23},{6,20},{7,21},{8,26},{9,... | collective-permute-start | bytes 196616 | tf_op jit(solution)/shard_map/ppermute | solution.py:155
  29.6 0.0 collective-permute-done.11
  29.6 0.0 collective-permute-done.7.refs_4_
  29.6 0.0 collective-permute-done.6.refs_3_
  29.6 0.7 %sums.3 = (bf16[128,256]{1,0:T(8,128)(2,1)S(1)}, bf16[128,256]{1,0:T(8,128)(2,1)S(1)}, bf16[256,256]{1,0:T(8,128)(2,1)S(1)}) custom-call(bf16[272,512]{1,0:T(8,128)(2,1)S(1)} %get-tuple-element.25.refs_0_, bf16[544,512]{1,0:T(8,128)(2,1)S(1)} %collective-permute-done.after.refs_1_, bf16[272,512]{1,0:T(8,128)(2,1)S(1)} %collective-permute-done.5.refs_2_, ...), custom_call_target="tpu_custom_call" | custom-call | tf_op jit(solution)/shard_map/sums/pallas_call | solution.py:128
  30.4 2.2 %collective-permute-start.12 = (bf16[128,256]{1,0:T(8,128)(2,1)S(1)}, bf16[128,256]{1,0:T(8,128)(2,1)S(1)}, u32[]{:S(2)}, u32[]{:S(2)}) collective-permute-start(bf16[128,256]{1,0:T(8,128)(2,1)S(1)} %get-tuple-element.21), channel_id=1, source_target_pairs={{0,16},{1,17},{2,18},{3,19},{4,20},{5,21},{6,22},{7,23},{8,24},{9,... | collective-permute-start | bytes 196616 | tf_op jit(solution)/shard_map/ppermute | solution.py:155
  32.6 0.9 %collective-permute-start.13 = (bf16[128,256]{1,0:T(8,128)(2,1)S(1)}, bf16[128,256]{1,0:T(8,128)(2,1)S(1)}, u32[]{:S(2)}, u32[]{:S(2)}) collective-permute-start(bf16[128,256]{1,0:T(8,128)(2,1)S(1)} %get-tuple-element.22), channel_id=1, source_target_pairs={{0,18},{1,19},{2,16},{3,17},{4,22},{5,23},{6,20},{7,21},{8,26},{9,... | collective-permute-start | bytes 196616 | tf_op jit(solution)/shard_map/ppermute | solution.py:155
  33.5 0.1 collective-permute-done.8.refs_4_.refs_0_
  33.6 0.2 virtual_own.1
  33.9 1.3 %collective-permute-start.9 = (f32[64,256]{1,0:T(8,128)S(1)}, f32[64,256]{1,0:T(8,128)S(1)}, u32[]{:S(2)}, u32[]{:S(2)}) collective-permute-start(f32[64,256]{1,0:T(8,128)S(1)} %get-tuple-element.19), channel_id=1, source_target_pairs={{0,2},{1,3},{2,0},{3,1},{4,6},{5,7},{6,4},{7,5},{8,10},{9,11},{10,... | collective-permute-start | bytes 196616 | tf_op jit(solution)/shard_map/ppermute | solution.py:155
  35.1 2.6 %collective-permute-done.10.refs_2_ = bf16[128,256]{1,0:T(8,128)(2,1)S(1)} collective-permute-done((bf16[128,256]{1,0:T(8,128)(2,1)S(1)}, bf16[128,256]{1,0:T(8,128)(2,1)S(1)}, u32[]{:S(2)}, u32[]{:S(2)}) %collective-permute-start.10) | collective-permute-done | bytes 65568 | tf_op jit(solution)/shard_map/ppermute | solution.py:155
  37.7 0.2 virtual_far.1.refs_2_
  37.9 0.6 %collective-permute-done.12.refs_3_ = bf16[128,256]{1,0:T(8,128)(2,1)S(1)} collective-permute-done((bf16[128,256]{1,0:T(8,128)(2,1)S(1)}, bf16[128,256]{1,0:T(8,128)(2,1)S(1)}, u32[]{:S(2)}, u32[]{:S(2)}) %collective-permute-start.12) | collective-permute-done | bytes 65568 | tf_op jit(solution)/shard_map/ppermute | solution.py:155
  38.5 0.8 %collective-permute-done.13.refs_5_ = bf16[128,256]{1,0:T(8,128)(2,1)S(1)} collective-permute-done((bf16[128,256]{1,0:T(8,128)(2,1)S(1)}, bf16[128,256]{1,0:T(8,128)(2,1)S(1)}, u32[]{:S(2)}, u32[]{:S(2)}) %collective-permute-start.13) | collective-permute-done | bytes 65568 | tf_op jit(solution)/shard_map/ppermute | solution.py:155
  39.3 0.0 collective-permute-done.9.refs_1_
  39.3 0.2 virtual_last.1
  39.5 0.1 collective-permute-start.14
  39.6 1.2 %collective-permute-done.14 = f32[32,256]{1,0:T(8,128)S(1)} collective-permute-done((f32[32,256]{1,0:T(8,128)S(1)}, f32[32,256]{1,0:T(8,128)S(1)}, u32[]{:S(2)}, u32[]{:S(2)}) %collective-permute-start.14) | collective-permute-done | bytes 32800 | tf_op jit(solution)/shard_map/ppermute | solution.py:155
  40.8 0.6 %add_bitcast_fusion = f32[1,32,256]{2,1,0:T(8,128)} fusion(f32[32,256]{1,0:T(8,128)S(1)} %get-tuple-element.23, f32[32,256]{1,0:T(8,128)S(1)} %collective-permute-done.14), kind=kLoop, calls=%fused_computation.11 | loop fusion | flops 8192 | bytes 98304 | tf_op jit(solution)/shard_map/broadcast_in_dim | solution.py:253
  (9 shorter events, 0.2 us)
Async XLA Ops:
  1.0 4.2 %copy-start.1 = (bf16[512,512]{1,0:T(8,128)(2,1)S(1)}, bf16[512,512]{1,0:T(8,128)(2,1)}, u32[]{:S(2)}) copy-start(bf16[512,512]{1,0:T(8,128)(2,1)} %param.4) | copy-start | bytes 1572868
  2.1 4.7 %copy-start.2 = (bf16[1,4,256,256]{3,2,1,0:T(8,128)(2,1)S(1)}, bf16[1,4,256,256]{3,2,1,0:T(8,128)(2,1)}, u32[]{:S(2)}) copy-start(bf16[1,4,256,256]{3,2,1,0:T(8,128)(2,1)} %param.7) | copy-start | bytes 1572868
  2.1 6.2 %copy-start = (bf16[512,256]{1,0:T(8,128)(2,1)S(1)}, bf16[512,256]{1,0:T(8,128)(2,1)}, u32[]{:S(2)}) copy-start(bf16[512,256]{1,0:T(8,128)(2,1)} %own.1) | copy-start | bytes 786436
  2.1 16.1 %collective-permute-start = (bf16[544,512]{1,0:T(8,128)(2,1)S(1)}, bf16[544,512]{1,0:T(8,128)(2,1)S(1)}, u32[]{:S(2)}, u32[]{:S(2)}) collective-permute-start(bf16[544,512]{1,0:T(8,128)(2,1)S(1)} %bitcast.17), channel_id=1, source_target_pairs={{0,4},{1,5},{2,6},{3,7},{4,0},{5,1},{6,2},{7,3},{8,12},{9,13},{10,... | collective-permute-start | bytes 1671176 | tf_op jit(solution)/shard_map/ppermute | solution.py:155
  5.2 12.5 %collective-permute-start.1 = (bf16[272,512]{1,0:T(8,128)(2,1)S(1)}, bf16[272,512]{1,0:T(8,128)(2,1)S(1)}, u32[]{:S(2)}, u32[]{:S(2)}) collective-permute-start(bf16[272,512]{1,0:T(8,128)(2,1)S(1)} %get-tuple-element.26.refs_0_), channel_id=1, source_target_pairs={{0,8},{1,9},{2,10},{3,11},{4,12},{5,13},{6,14},{7,15},{8,0},{9,1},... | collective-permute-start | bytes 835592 | tf_op jit(solution)/shard_map/ppermute | solution.py:155
  6.9 22.7 %collective-permute-start.11 = (bf16[4,256,256]{2,1,0:T(8,128)(2,1)S(1)}, bf16[4,256,256]{2,1,0:T(8,128)(2,1)S(1)}, u32[]{:S(2)}, u32[]{:S(2)}) collective-permute-start(bf16[4,256,256]{2,1,0:T(8,128)(2,1)S(1)} %bitcast.18), channel_id=1, source_target_pairs={{0,2},{1,3},{2,0},{3,1},{4,6},{5,7},{6,4},{7,5},{8,10},{9,11},{10,... | collective-permute-start | bytes 1572872 | tf_op jit(solution)/shard_map/ppermute | solution.py:155
  8.4 9.3 %collective-permute-start.3 = (bf16[256,256]{1,0:T(8,128)(2,1)S(1)}, bf16[256,256]{1,0:T(8,128)(2,1)S(1)}, u32[]{:S(2)}, u32[]{:S(2)}) collective-permute-start(bf16[256,256]{1,0:T(8,128)(2,1)S(1)} %half.1.refs_5_), channel_id=1, source_target_pairs={{0,16},{1,17},{2,18},{3,19},{4,20},{5,21},{6,22},{7,23},{8,24},{9,... | collective-permute-start | bytes 393224 | tf_op jit(solution)/shard_map/ppermute | solution.py:155
  11.0 11.2 %collective-permute-start.5 = (bf16[272,512]{1,0:T(8,128)(2,1)S(1)}, bf16[272,512]{1,0:T(8,128)(2,1)S(1)}, u32[]{:S(2)}, u32[]{:S(2)}) collective-permute-start(bf16[272,512]{1,0:T(8,128)(2,1)S(1)} %get-tuple-element.25.refs_0_), channel_id=1, source_target_pairs={{0,8},{1,9},{2,10},{3,11},{4,12},{5,13},{6,14},{7,15},{8,0},{9,1},... | collective-permute-start | bytes 835592 | tf_op jit(solution)/shard_map/ppermute | solution.py:155
  17.7 7.2 %collective-permute-start.2 = (bf16[272,512]{1,0:T(8,128)(2,1)S(1)}, bf16[272,512]{1,0:T(8,128)(2,1)S(1)}, u32[]{:S(2)}, u32[]{:S(2)}) collective-permute-start(bf16[272,512]{1,0:T(8,128)(2,1)S(1)} %collective-permute-done.1.refs_2_), channel_id=1, source_target_pairs={{0,4},{1,5},{2,6},{3,7},{4,0},{5,1},{6,2},{7,3},{8,12},{9,13},{10,... | collective-permute-start | bytes 835592 | tf_op jit(solution)/shard_map/ppermute | solution.py:155
  18.2 6.2 %collective-permute-start.4 = (bf16[256,256]{1,0:T(8,128)(2,1)S(1)}, bf16[256,256]{1,0:T(8,128)(2,1)S(1)}, u32[]{:S(2)}, u32[]{:S(2)}) collective-permute-start(bf16[256,256]{1,0:T(8,128)(2,1)S(1)} %hold.1), channel_id=1, source_target_pairs={{0,1},{1,0},{2,3},{3,2},{4,5},{5,4},{6,7},{7,6},{8,9},{9,8},{10,11... | collective-permute-start | bytes 393224 | tf_op jit(solution)/shard_map/ppermute | solution.py:155
  22.2 7.4 %collective-permute-start.7 = (bf16[128,512]{1,0:T(8,128)(2,1)S(1)}, bf16[128,512]{1,0:T(8,128)(2,1)S(1)}, u32[]{:S(2)}, u32[]{:S(2)}) collective-permute-start(bf16[128,512]{1,0:T(8,128)(2,1)S(1)} %slice.41), channel_id=1, source_target_pairs={{0,4},{1,5},{2,6},{3,7},{4,0},{5,1},{6,2},{7,3},{8,12},{9,13},{10,... | collective-permute-start | bytes 393224 | tf_op jit(solution)/shard_map/ppermute | solution.py:155
  22.6 7.0 %collective-permute-start.6 = (bf16[144,512]{1,0:T(8,128)(2,1)S(1)}, bf16[144,512]{1,0:T(8,128)(2,1)S(1)}, u32[]{:S(2)}, u32[]{:S(2)}) collective-permute-start(bf16[144,512]{1,0:T(8,128)(2,1)S(1)} %slice.40), channel_id=1, source_target_pairs={{0,8},{1,9},{2,10},{3,11},{4,12},{5,13},{6,14},{7,15},{8,0},{9,1},... | collective-permute-start | bytes 442376 | tf_op jit(solution)/shard_map/ppermute | solution.py:155
  25.6 8.0 %collective-permute-start.8 = (bf16[128,256]{1,0:T(8,128)(2,1)S(1)}, bf16[128,256]{1,0:T(8,128)(2,1)S(1)}, u32[]{:S(2)}, u32[]{:S(2)}) collective-permute-start(bf16[128,256]{1,0:T(8,128)(2,1)S(1)} %get-tuple-element.16.refs_6_), channel_id=1, source_target_pairs={{0,16},{1,17},{2,18},{3,19},{4,20},{5,21},{6,22},{7,23},{8,24},{9,... | collective-permute-start | bytes 196616 | tf_op jit(solution)/shard_map/ppermute | solution.py:155
  27.9 9.8 %collective-permute-start.10 = (bf16[128,256]{1,0:T(8,128)(2,1)S(1)}, bf16[128,256]{1,0:T(8,128)(2,1)S(1)}, u32[]{:S(2)}, u32[]{:S(2)}) collective-permute-start(bf16[128,256]{1,0:T(8,128)(2,1)S(1)} %get-tuple-element.20), channel_id=1, source_target_pairs={{0,18},{1,19},{2,16},{3,17},{4,22},{5,23},{6,20},{7,21},{8,26},{9,... | collective-permute-start | bytes 196616 | tf_op jit(solution)/shard_map/ppermute | solution.py:155
  30.4 8.1 %collective-permute-start.12 = (bf16[128,256]{1,0:T(8,128)(2,1)S(1)}, bf16[128,256]{1,0:T(8,128)(2,1)S(1)}, u32[]{:S(2)}, u32[]{:S(2)}) collective-permute-start(bf16[128,256]{1,0:T(8,128)(2,1)S(1)} %get-tuple-element.21), channel_id=1, source_target_pairs={{0,16},{1,17},{2,18},{3,19},{4,20},{5,21},{6,22},{7,23},{8,24},{9,... | collective-permute-start | bytes 196616 | tf_op jit(solution)/shard_map/ppermute | solution.py:155
  32.6 6.7 %collective-permute-start.13 = (bf16[128,256]{1,0:T(8,128)(2,1)S(1)}, bf16[128,256]{1,0:T(8,128)(2,1)S(1)}, u32[]{:S(2)}, u32[]{:S(2)}) collective-permute-start(bf16[128,256]{1,0:T(8,128)(2,1)S(1)} %get-tuple-element.22), channel_id=1, source_target_pairs={{0,18},{1,19},{2,16},{3,17},{4,22},{5,23},{6,20},{7,21},{8,26},{9,... | collective-permute-start | bytes 196616 | tf_op jit(solution)/shard_map/ppermute | solution.py:155
  33.9 5.4 %collective-permute-start.9 = (f32[64,256]{1,0:T(8,128)S(1)}, f32[64,256]{1,0:T(8,128)S(1)}, u32[]{:S(2)}, u32[]{:S(2)}) collective-permute-start(f32[64,256]{1,0:T(8,128)S(1)} %get-tuple-element.19), channel_id=1, source_target_pairs={{0,2},{1,3},{2,0},{3,1},{4,6},{5,7},{6,4},{7,5},{8,10},{9,11},{10,... | collective-permute-start | bytes 196616 | tf_op jit(solution)/shard_map/ppermute | solution.py:155
  39.5 1.3 %collective-permute-start.14 = (f32[32,256]{1,0:T(8,128)S(1)}, f32[32,256]{1,0:T(8,128)S(1)}, u32[]{:S(2)}, u32[]{:S(2)}) collective-permute-start(f32[32,256]{1,0:T(8,128)S(1)} %get-tuple-element.24), channel_id=1, source_target_pairs={{0,1},{1,0},{2,3},{3,2},{4,5},{5,4},{6,7},{7,6},{8,9},{9,8},{10,11... | collective-permute-start | bytes 98312 | tf_op jit(solution)/shard_map/ppermute | solution.py:155

commit v11 on v9

--- a/solution.py
+++ b/solution.py
@@ -123,6 +123,10 @@
     leaves[...] = total[pl.ds(pl.multiple_of((1 - core) * middle, middle), middle), :]
 
 
+def add_kernel(kept, came, total):
+    total[0] = kept[...] + came[...]
+
+
 def call(kernel, name, out, specs, flops, scratch=()):
     def run(*operands):
         return pl.pallas_call(
@@ -241,7 +245,8 @@
     scratch = [pltpu.VMEM(piece.shape, piece.dtype)]
     split = call(split_kernel, "split", [half_piece] * 2, [VMEM] * len(pieces), 0, scratch)
     stays, leaves = split(*pieces)
-    return (stays + send(leaves, 0, 1))[None]
+    result = like((1,) + half_piece.shape, half_piece.dtype)
+    return call(add_kernel, "add", result, [VMEM] * 2, 0)(stays, send(leaves, 0, 1))
 
 
 def solution(mesh):

time: 41.6 us -> 41.6 us (level)
  Pallas kernels: 2.21 us -> 2.83 us
  other arithmetic: 2.49 us -> 1.87 us
    pallas_call x9 -> x10, Pallas kernels: 2.21 us -> 2.83 us  [run(): pl.pallas_call(kernel, out_shape=out, in_specs=specs, out_specs=jax.tree....]
    broadcast_in_dim x1 -> x0, other arithmetic: 0.62 us -> none  [shards(): return (stays + send(leaves, 0, 1))[None]]
where the time goes in v11:
time: 41.6 us; the launch traced here: 41.4 us
  starting transfers between devices  20.1 us (48%)
  waiting for transfers between devices  16.1 us (39%)
  Pallas kernels  2.83 us (7%)
  other arithmetic  1.87 us (4%)
    ppermute x15, starting transfers between devices, send(): return lax.ppermute(array, AXES, order)  20.1 us
    ppermute x15, waiting for transfers between devices, send(): return lax.ppermute(array, AXES, order)  16.1 us
    pallas_call x10, Pallas kernels, run(): pl.pallas_call(kernel, out_shape=out, in_specs=specs, out_specs=jax.tree....  2.83 us
    concatenate x1, other arithmetic, shards(): whole = jnp.concatenate([named, blocks], axis=1)  1.15 us
  transfers between devices with their start and end apart: 15, of which 8 were waited for; matrix products, arithmetic and copies ran while one was open for 0% of the time, Pallas kernels for 5%

profile of v11, /device:TPU:0, one launch (start us, length us, event | category | flops | bytes accessed | tf_op | source)
XLA Modules:
  0.0 41.4 jit_solution(11597526481201645481)
XLA Ops:
  0.0 0.7 %convert_element_type.16 = bf16[4,2]{0,1:T(2,128)(2,1)S(1)} convert(s32[4,2]{0,1:T(2,128)} %param.6) | non-fusion elementwise | flops 8 | bytes 48 | tf_op jit(solution)/shard_map/convert_element_type | solution.py:170
  0.7 0.1 copy.6
  0.8 0.1 convert_element_type.17
  0.9 0.1 broadcast_in_dim.8
  1.0 0.0 copy-start.1
  1.0 1.2 %pad_maximum_fusion = bf16[2,272,512]{2,1,0:T(8,128)(2,1)S(1)} fusion(bf16[2,16,512]{2,1,0:T(8,128)(2,1)S(1)} %broadcast_in_dim.8, bf16[2,256,512]{2,1,0:T(8,128)(2,1)} %bitcast.13), kind=kLoop, calls=%fused_computation.2 | loop fusion | flops 1114112 | bytes 1114112 | tf_op jit(solution)/shard_map/concatenate | solution.py:173
  2.1 0.0 copy-start.2
  2.1 0.0 copy-start
  2.1 3.0 %collective-permute-start = (bf16[544,512]{1,0:T(8,128)(2,1)S(1)}, bf16[544,512]{1,0:T(8,128)(2,1)S(1)}, u32[]{:S(2)}, u32[]{:S(2)}) collective-permute-start(bf16[544,512]{1,0:T(8,128)(2,1)S(1)} %bitcast.15), channel_id=1, source_target_pairs={{0,4},{1,5},{2,6},{3,7},{4,0},{5,1},{6,2},{7,3},{8,12},{9,13},{10,... | collective-permute-start | bytes 1671176 | tf_op jit(solution)/shard_map/ppermute | solution.py:159
  5.2 0.0 copy-done.1
  5.2 1.6 %collective-permute-start.1 = (bf16[272,512]{1,0:T(8,128)(2,1)S(1)}, bf16[272,512]{1,0:T(8,128)(2,1)S(1)}, u32[]{:S(2)}, u32[]{:S(2)}) collective-permute-start(bf16[272,512]{1,0:T(8,128)(2,1)S(1)} %get-tuple-element.26.refs_0_), channel_id=1, source_target_pairs={{0,8},{1,9},{2,10},{3,11},{4,12},{5,13},{6,14},{7,15},{8,0},{9,1},... | collective-permute-start | bytes 835592 | tf_op jit(solution)/shard_map/ppermute | solution.py:159
  6.9 0.0 copy-done.2
  6.9 1.5 %collective-permute-start.11 = (bf16[4,256,256]{2,1,0:T(8,128)(2,1)S(1)}, bf16[4,256,256]{2,1,0:T(8,128)(2,1)S(1)}, u32[]{:S(2)}, u32[]{:S(2)}) collective-permute-start(bf16[4,256,256]{2,1,0:T(8,128)(2,1)S(1)} %bitcast.16), channel_id=1, source_target_pairs={{0,2},{1,3},{2,0},{3,1},{4,6},{5,7},{6,4},{7,5},{8,10},{9,11},{10,... | collective-permute-start | bytes 1572872 | tf_op jit(solution)/shard_map/ppermute | solution.py:159
  8.4 0.0 copy-done
  8.4 2.7 %collective-permute-start.3 = (bf16[256,256]{1,0:T(8,128)(2,1)S(1)}, bf16[256,256]{1,0:T(8,128)(2,1)S(1)}, u32[]{:S(2)}, u32[]{:S(2)}) collective-permute-start(bf16[256,256]{1,0:T(8,128)(2,1)S(1)} %half.1.refs_5_), channel_id=1, source_target_pairs={{0,16},{1,17},{2,18},{3,19},{4,20},{5,21},{6,22},{7,23},{8,24},{9,... | collective-permute-start | bytes 393224 | tf_op jit(solution)/shard_map/ppermute | solution.py:159
  11.0 0.4 %collective-permute-start.5 = (bf16[272,512]{1,0:T(8,128)(2,1)S(1)}, bf16[272,512]{1,0:T(8,128)(2,1)S(1)}, u32[]{:S(2)}, u32[]{:S(2)}) collective-permute-start(bf16[272,512]{1,0:T(8,128)(2,1)S(1)} %get-tuple-element.25.refs_0_), channel_id=1, source_target_pairs={{0,8},{1,9},{2,10},{3,11},{4,12},{5,13},{6,14},{7,15},{8,0},{9,1},... | collective-permute-start | bytes 835592 | tf_op jit(solution)/shard_map/ppermute | solution.py:159
  11.5 6.2 %collective-permute-done.1.refs_2_ = bf16[272,512]{1,0:T(8,128)(2,1)S(1)} collective-permute-done((bf16[272,512]{1,0:T(8,128)(2,1)S(1)}, bf16[272,512]{1,0:T(8,128)(2,1)S(1)}, u32[]{:S(2)}, u32[]{:S(2)}) %collective-permute-start.1) | collective-permute-done | bytes 278560 | tf_op jit(solution)/shard_map/ppermute | solution.py:159
  17.7 0.0 collective-permute-start.2
  17.7 0.0 collective-permute-done.3.array.rest_0_
  17.7 0.5 %collective-permute-done.after.refs_1_ = bf16[544,512]{1,0:T(8,128)(2,1)S(1)} collective-permute-done((bf16[544,512]{1,0:T(8,128)(2,1)S(1)}, bf16[544,512]{1,0:T(8,128)(2,1)S(1)}, u32[]{:S(2)}, u32[]{:S(2)}) %collective-permute-start) | collective-permute-done | bytes 557088 | tf_op jit(solution)/shard_map/ppermute | solution.py:159
  18.2 0.1 collective-permute-start.4
  18.3 3.8 %collective-permute-done.5.refs_2_ = bf16[272,512]{1,0:T(8,128)(2,1)S(1)} collective-permute-done((bf16[272,512]{1,0:T(8,128)(2,1)S(1)}, bf16[272,512]{1,0:T(8,128)(2,1)S(1)}, u32[]{:S(2)}, u32[]{:S(2)}) %collective-permute-start.5) | collective-permute-done | bytes 278560 | tf_op jit(solution)/shard_map/ppermute | solution.py:159
  22.2 0.4 collective-permute-start.7
  22.6 1.8 %collective-permute-start.6 = (bf16[144,512]{1,0:T(8,128)(2,1)S(1)}, bf16[144,512]{1,0:T(8,128)(2,1)S(1)}, u32[]{:S(2)}, u32[]{:S(2)}) collective-permute-start(bf16[144,512]{1,0:T(8,128)(2,1)S(1)} %slice.40), channel_id=1, source_target_pairs={{0,8},{1,9},{2,10},{3,11},{4,12},{5,13},{6,14},{7,15},{8,0},{9,1},... | collective-permute-start | bytes 442376 | tf_op jit(solution)/shard_map/ppermute | solution.py:159
  24.4 0.0 collective-permute-done.4.rest_1_
  24.5 0.4 %collective-permute-done.2.refs_3_ = bf16[272,512]{1,0:T(8,128)(2,1)S(1)} collective-permute-done((bf16[272,512]{1,0:T(8,128)(2,1)S(1)}, bf16[272,512]{1,0:T(8,128)(2,1)S(1)}, u32[]{:S(2)}, u32[]{:S(2)}) %collective-permute-start.2) | collective-permute-done | bytes 278560 | tf_op jit(solution)/shard_map/ppermute | solution.py:159
  24.9 0.7 %sums.2 = (bf16[128,256]{1,0:T(8,128)(2,1)S(1)}, bf16[128,256]{1,0:T(8,128)(2,1)S(1)}, bf16[256,256]{1,0:T(8,128)(2,1)S(1)}) custom-call(bf16[272,512]{1,0:T(8,128)(2,1)S(1)} %get-tuple-element.26.refs_0_, bf16[544,512]{1,0:T(8,128)(2,1)S(1)} %collective-permute-done.after.refs_1_, bf16[272,512]{1,0:T(8,128)(2,1)S(1)} %collective-permute-done.1.refs_2_, ...), custom_call_target="tpu_custom_call" | custom-call | tf_op jit(solution)/shard_map/sums/pallas_call | solution.py:132
  25.6 2.2 %collective-permute-start.9 = (bf16[128,256]{1,0:T(8,128)(2,1)S(1)}, bf16[128,256]{1,0:T(8,128)(2,1)S(1)}, u32[]{:S(2)}, u32[]{:S(2)}) collective-permute-start(bf16[128,256]{1,0:T(8,128)(2,1)S(1)} %get-tuple-element.16.refs_6_), channel_id=1, source_target_pairs={{0,16},{1,17},{2,18},{3,19},{4,20},{5,21},{6,22},{7,23},{8,24},{9,... | collective-permute-start | bytes 196616 | tf_op jit(solution)/shard_map/ppermute | solution.py:159
  27.9 1.7 %collective-permute-start.10 = (bf16[128,256]{1,0:T(8,128)(2,1)S(1)}, bf16[128,256]{1,0:T(8,128)(2,1)S(1)}, u32[]{:S(2)}, u32[]{:S(2)}) collective-permute-start(bf16[128,256]{1,0:T(8,128)(2,1)S(1)} %get-tuple-element.20), channel_id=1, source_target_pairs={{0,18},{1,19},{2,16},{3,17},{4,22},{5,23},{6,20},{7,21},{8,26},{9,... | collective-permute-start | bytes 196616 | tf_op jit(solution)/shard_map/ppermute | solution.py:159
  29.6 0.0 collective-permute-done.11
  29.6 0.0 collective-permute-done.7.refs_4_
  29.6 0.0 collective-permute-done.6.refs_3_
  29.6 0.7 %sums.3 = (bf16[128,256]{1,0:T(8,128)(2,1)S(1)}, bf16[128,256]{1,0:T(8,128)(2,1)S(1)}, bf16[256,256]{1,0:T(8,128)(2,1)S(1)}) custom-call(bf16[272,512]{1,0:T(8,128)(2,1)S(1)} %get-tuple-element.25.refs_0_, bf16[544,512]{1,0:T(8,128)(2,1)S(1)} %collective-permute-done.after.refs_1_, bf16[272,512]{1,0:T(8,128)(2,1)S(1)} %collective-permute-done.5.refs_2_, ...), custom_call_target="tpu_custom_call" | custom-call | tf_op jit(solution)/shard_map/sums/pallas_call | solution.py:132
  30.4 2.2 %collective-permute-start.12 = (bf16[128,256]{1,0:T(8,128)(2,1)S(1)}, bf16[128,256]{1,0:T(8,128)(2,1)S(1)}, u32[]{:S(2)}, u32[]{:S(2)}) collective-permute-start(bf16[128,256]{1,0:T(8,128)(2,1)S(1)} %get-tuple-element.21), channel_id=1, source_target_pairs={{0,16},{1,17},{2,18},{3,19},{4,20},{5,21},{6,22},{7,23},{8,24},{9,... | collective-permute-start | bytes 196616 | tf_op jit(solution)/shard_map/ppermute | solution.py:159
  32.6 0.9 %collective-permute-start.13 = (bf16[128,256]{1,0:T(8,128)(2,1)S(1)}, bf16[128,256]{1,0:T(8,128)(2,1)S(1)}, u32[]{:S(2)}, u32[]{:S(2)}) collective-permute-start(bf16[128,256]{1,0:T(8,128)(2,1)S(1)} %get-tuple-element.22), channel_id=1, source_target_pairs={{0,18},{1,19},{2,16},{3,17},{4,22},{5,23},{6,20},{7,21},{8,26},{9,... | collective-permute-start | bytes 196616 | tf_op jit(solution)/shard_map/ppermute | solution.py:159
  33.5 0.2 virtual_own.1
  33.8 1.3 %collective-permute-start.8 = (f32[64,256]{1,0:T(8,128)S(1)}, f32[64,256]{1,0:T(8,128)S(1)}, u32[]{:S(2)}, u32[]{:S(2)}) collective-permute-start(f32[64,256]{1,0:T(8,128)S(1)} %get-tuple-element.19), channel_id=1, source_target_pairs={{0,2},{1,3},{2,0},{3,1},{4,6},{5,7},{6,4},{7,5},{8,10},{9,11},{10,... | collective-permute-start | bytes 196616 | tf_op jit(solution)/shard_map/ppermute | solution.py:159
  35.1 0.0 collective-permute-done.9.refs_0_
  35.1 2.6 %collective-permute-done.10.refs_2_ = bf16[128,256]{1,0:T(8,128)(2,1)S(1)} collective-permute-done((bf16[128,256]{1,0:T(8,128)(2,1)S(1)}, bf16[128,256]{1,0:T(8,128)(2,1)S(1)}, u32[]{:S(2)}, u32[]{:S(2)}) %collective-permute-start.10) | collective-permute-done | bytes 65568 | tf_op jit(solution)/shard_map/ppermute | solution.py:159
  37.7 0.2 virtual_far.2.refs_2_
  37.9 0.6 %collective-permute-done.12.refs_0_ = bf16[128,256]{1,0:T(8,128)(2,1)S(1)} collective-permute-done((bf16[128,256]{1,0:T(8,128)(2,1)S(1)}, bf16[128,256]{1,0:T(8,128)(2,1)S(1)}, u32[]{:S(2)}, u32[]{:S(2)}) %collective-permute-start.12) | collective-permute-done | bytes 65568 | tf_op jit(solution)/shard_map/ppermute | solution.py:159
  38.5 0.8 %collective-permute-done.13.refs_2_ = bf16[128,256]{1,0:T(8,128)(2,1)S(1)} collective-permute-done((bf16[128,256]{1,0:T(8,128)(2,1)S(1)}, bf16[128,256]{1,0:T(8,128)(2,1)S(1)}, u32[]{:S(2)}, u32[]{:S(2)}) %collective-permute-start.13) | collective-permute-done | bytes 65568 | tf_op jit(solution)/shard_map/ppermute | solution.py:159
  39.3 0.2 virtual_far.3.refs_3_
  39.5 0.0 collective-permute-done.8.refs_1_
  39.5 0.1 collective-permute-start.14
  39.6 1.2 %collective-permute-done.14.came = f32[32,256]{1,0:T(8,128)S(1)} collective-permute-done((f32[32,256]{1,0:T(8,128)S(1)}, f32[32,256]{1,0:T(8,128)S(1)}, u32[]{:S(2)}, u32[]{:S(2)}) %collective-permute-start.14) | collective-permute-done | bytes 32800 | tf_op jit(solution)/shard_map/ppermute | solution.py:159
  40.8 0.6 %add.3 = f32[1,32,256]{2,1,0:T(8,128)} custom-call(f32[32,256]{1,0:T(8,128)S(1)} %get-tuple-element.23.kept, f32[32,256]{1,0:T(8,128)S(1)} %collective-permute-done.14.came), custom_call_target="tpu_custom_call" | custom-call | tf_op jit(solution)/shard_map/add/pallas_call | solution.py:132
  (10 shorter events, 0.2 us)
Async XLA Ops:
  1.0 4.2 %copy-start.1 = (bf16[512,512]{1,0:T(8,128)(2,1)S(1)}, bf16[512,512]{1,0:T(8,128)(2,1)}, u32[]{:S(2)}) copy-start(bf16[512,512]{1,0:T(8,128)(2,1)} %param.4) | copy-start | bytes 1572868
  2.1 4.7 %copy-start.2 = (bf16[1,4,256,256]{3,2,1,0:T(8,128)(2,1)S(1)}, bf16[1,4,256,256]{3,2,1,0:T(8,128)(2,1)}, u32[]{:S(2)}) copy-start(bf16[1,4,256,256]{3,2,1,0:T(8,128)(2,1)} %param.7) | copy-start | bytes 1572868
  2.1 6.2 %copy-start = (bf16[512,256]{1,0:T(8,128)(2,1)S(1)}, bf16[512,256]{1,0:T(8,128)(2,1)}, u32[]{:S(2)}) copy-start(bf16[512,256]{1,0:T(8,128)(2,1)} %own.1) | copy-start | bytes 786436
  2.1 16.1 %collective-permute-start = (bf16[544,512]{1,0:T(8,128)(2,1)S(1)}, bf16[544,512]{1,0:T(8,128)(2,1)S(1)}, u32[]{:S(2)}, u32[]{:S(2)}) collective-permute-start(bf16[544,512]{1,0:T(8,128)(2,1)S(1)} %bitcast.15), channel_id=1, source_target_pairs={{0,4},{1,5},{2,6},{3,7},{4,0},{5,1},{6,2},{7,3},{8,12},{9,13},{10,... | collective-permute-start | bytes 1671176 | tf_op jit(solution)/shard_map/ppermute | solution.py:159
  5.2 12.5 %collective-permute-start.1 = (bf16[272,512]{1,0:T(8,128)(2,1)S(1)}, bf16[272,512]{1,0:T(8,128)(2,1)S(1)}, u32[]{:S(2)}, u32[]{:S(2)}) collective-permute-start(bf16[272,512]{1,0:T(8,128)(2,1)S(1)} %get-tuple-element.26.refs_0_), channel_id=1, source_target_pairs={{0,8},{1,9},{2,10},{3,11},{4,12},{5,13},{6,14},{7,15},{8,0},{9,1},... | collective-permute-start | bytes 835592 | tf_op jit(solution)/shard_map/ppermute | solution.py:159
  6.9 22.7 %collective-permute-start.11 = (bf16[4,256,256]{2,1,0:T(8,128)(2,1)S(1)}, bf16[4,256,256]{2,1,0:T(8,128)(2,1)S(1)}, u32[]{:S(2)}, u32[]{:S(2)}) collective-permute-start(bf16[4,256,256]{2,1,0:T(8,128)(2,1)S(1)} %bitcast.16), channel_id=1, source_target_pairs={{0,2},{1,3},{2,0},{3,1},{4,6},{5,7},{6,4},{7,5},{8,10},{9,11},{10,... | collective-permute-start | bytes 1572872 | tf_op jit(solution)/shard_map/ppermute | solution.py:159
  8.4 9.3 %collective-permute-start.3 = (bf16[256,256]{1,0:T(8,128)(2,1)S(1)}, bf16[256,256]{1,0:T(8,128)(2,1)S(1)}, u32[]{:S(2)}, u32[]{:S(2)}) collective-permute-start(bf16[256,256]{1,0:T(8,128)(2,1)S(1)} %half.1.refs_5_), channel_id=1, source_target_pairs={{0,16},{1,17},{2,18},{3,19},{4,20},{5,21},{6,22},{7,23},{8,24},{9,... | collective-permute-start | bytes 393224 | tf_op jit(solution)/shard_map/ppermute | solution.py:159
  11.0 11.2 %collective-permute-start.5 = (bf16[272,512]{1,0:T(8,128)(2,1)S(1)}, bf16[272,512]{1,0:T(8,128)(2,1)S(1)}, u32[]{:S(2)}, u32[]{:S(2)}) collective-permute-start(bf16[272,512]{1,0:T(8,128)(2,1)S(1)} %get-tuple-element.25.refs_0_), channel_id=1, source_target_pairs={{0,8},{1,9},{2,10},{3,11},{4,12},{5,13},{6,14},{7,15},{8,0},{9,1},... | collective-permute-start | bytes 835592 | tf_op jit(solution)/shard_map/ppermute | solution.py:159
  17.7 7.2 %collective-permute-start.2 = (bf16[272,512]{1,0:T(8,128)(2,1)S(1)}, bf16[272,512]{1,0:T(8,128)(2,1)S(1)}, u32[]{:S(2)}, u32[]{:S(2)}) collective-permute-start(bf16[272,512]{1,0:T(8,128)(2,1)S(1)} %collective-permute-done.1.refs_2_), channel_id=1, source_target_pairs={{0,4},{1,5},{2,6},{3,7},{4,0},{5,1},{6,2},{7,3},{8,12},{9,13},{10,... | collective-permute-start | bytes 835592 | tf_op jit(solution)/shard_map/ppermute | solution.py:159
  18.2 6.2 %collective-permute-start.4 = (bf16[256,256]{1,0:T(8,128)(2,1)S(1)}, bf16[256,256]{1,0:T(8,128)(2,1)S(1)}, u32[]{:S(2)}, u32[]{:S(2)}) collective-permute-start(bf16[256,256]{1,0:T(8,128)(2,1)S(1)} %hold.1), channel_id=1, source_target_pairs={{0,1},{1,0},{2,3},{3,2},{4,5},{5,4},{6,7},{7,6},{8,9},{9,8},{10,11... | collective-permute-start | bytes 393224 | tf_op jit(solution)/shard_map/ppermute | solution.py:159
  22.2 7.4 %collective-permute-start.7 = (bf16[128,512]{1,0:T(8,128)(2,1)S(1)}, bf16[128,512]{1,0:T(8,128)(2,1)S(1)}, u32[]{:S(2)}, u32[]{:S(2)}) collective-permute-start(bf16[128,512]{1,0:T(8,128)(2,1)S(1)} %slice.41), channel_id=1, source_target_pairs={{0,4},{1,5},{2,6},{3,7},{4,0},{5,1},{6,2},{7,3},{8,12},{9,13},{10,... | collective-permute-start | bytes 393224 | tf_op jit(solution)/shard_map/ppermute | solution.py:159
  22.6 7.0 %collective-permute-start.6 = (bf16[144,512]{1,0:T(8,128)(2,1)S(1)}, bf16[144,512]{1,0:T(8,128)(2,1)S(1)}, u32[]{:S(2)}, u32[]{:S(2)}) collective-permute-start(bf16[144,512]{1,0:T(8,128)(2,1)S(1)} %slice.40), channel_id=1, source_target_pairs={{0,8},{1,9},{2,10},{3,11},{4,12},{5,13},{6,14},{7,15},{8,0},{9,1},... | collective-permute-start | bytes 442376 | tf_op jit(solution)/shard_map/ppermute | solution.py:159
  25.6 9.5 %collective-permute-start.9 = (bf16[128,256]{1,0:T(8,128)(2,1)S(1)}, bf16[128,256]{1,0:T(8,128)(2,1)S(1)}, u32[]{:S(2)}, u32[]{:S(2)}) collective-permute-start(bf16[128,256]{1,0:T(8,128)(2,1)S(1)} %get-tuple-element.16.refs_6_), channel_id=1, source_target_pairs={{0,16},{1,17},{2,18},{3,19},{4,20},{5,21},{6,22},{7,23},{8,24},{9,... | collective-permute-start | bytes 196616 | tf_op jit(solution)/shard_map/ppermute | solution.py:159
  27.9 9.8 %collective-permute-start.10 = (bf16[128,256]{1,0:T(8,128)(2,1)S(1)}, bf16[128,256]{1,0:T(8,128)(2,1)S(1)}, u32[]{:S(2)}, u32[]{:S(2)}) collective-permute-start(bf16[128,256]{1,0:T(8,128)(2,1)S(1)} %get-tuple-element.20), channel_id=1, source_target_pairs={{0,18},{1,19},{2,16},{3,17},{4,22},{5,23},{6,20},{7,21},{8,26},{9,... | collective-permute-start | bytes 196616 | tf_op jit(solution)/shard_map/ppermute | solution.py:159
  30.4 8.1 %collective-permute-start.12 = (bf16[128,256]{1,0:T(8,128)(2,1)S(1)}, bf16[128,256]{1,0:T(8,128)(2,1)S(1)}, u32[]{:S(2)}, u32[]{:S(2)}) collective-permute-start(bf16[128,256]{1,0:T(8,128)(2,1)S(1)} %get-tuple-element.21), channel_id=1, source_target_pairs={{0,16},{1,17},{2,18},{3,19},{4,20},{5,21},{6,22},{7,23},{8,24},{9,... | collective-permute-start | bytes 196616 | tf_op jit(solution)/shard_map/ppermute | solution.py:159
  32.6 6.7 %collective-permute-start.13 = (bf16[128,256]{1,0:T(8,128)(2,1)S(1)}, bf16[128,256]{1,0:T(8,128)(2,1)S(1)}, u32[]{:S(2)}, u32[]{:S(2)}) collective-permute-start(bf16[128,256]{1,0:T(8,128)(2,1)S(1)} %get-tuple-element.22), channel_id=1, source_target_pairs={{0,18},{1,19},{2,16},{3,17},{4,22},{5,23},{6,20},{7,21},{8,26},{9,... | collective-permute-start | bytes 196616 | tf_op jit(solution)/shard_map/ppermute | solution.py:159
  33.8 5.7 %collective-permute-start.8 = (f32[64,256]{1,0:T(8,128)S(1)}, f32[64,256]{1,0:T(8,128)S(1)}, u32[]{:S(2)}, u32[]{:S(2)}) collective-permute-start(f32[64,256]{1,0:T(8,128)S(1)} %get-tuple-element.19), channel_id=1, source_target_pairs={{0,2},{1,3},{2,0},{3,1},{4,6},{5,7},{6,4},{7,5},{8,10},{9,11},{10,... | collective-permute-start | bytes 196616 | tf_op jit(solution)/shard_map/ppermute | solution.py:159
  39.5 1.3 %collective-permute-start.14 = (f32[32,256]{1,0:T(8,128)S(1)}, f32[32,256]{1,0:T(8,128)S(1)}, u32[]{:S(2)}, u32[]{:S(2)}) collective-permute-start(f32[32,256]{1,0:T(8,128)S(1)} %get-tuple-element.24), channel_id=1, source_target_pairs={{0,1},{1,0},{2,3},{3,2},{4,5},{5,4},{6,7},{7,6},{8,9},{9,8},{10,11... | collective-permute-start | bytes 98312 | tf_op jit(solution)/shard_map/ppermute | solution.py:159
